TPU v7x, 32 devices: a whole 2x2x4 slice. The times are simulated.
32 devices in a mesh: grp: 2 (over y), col: 4 (over z), row: 2 (over x), limb: 2 (over core).
Axes of the slice: x: 2, y: 2, z: 4, core: 2. Of those that a mesh axis runs over, the one named last changes fastest.
Arguments:
- database: bfloat16 [8192, 8192], P(('grp', 'row'), 'col'), parts along dimension 0, may hold values from -128 to 127, as said below
- lwe_matrix: bfloat16 [8192, 2, 512], P('col', 'limb'), may hold values from -0.0008544922 to 0.0008544922
- secret_ct: float32 [2, 2, 2, 512, 4096], P(None, None, 'limb', 'col', 'row'), may hold values from -6 to 6
Outputs:
- encrypted_product: float32 [4, 2, 4096], P('grp', None, 'row'), parts along dimension 0
There are 2 independent parts, one for each index of `grp`. A program takes and returns all parts, laid end to end along the dimension named above; an argument that names none is the same for every part. Nothing has to cross between parts.
Inputs may be any that keep to these rules, and one draw needn't show every extreme that they name: `database`: whole numbers.
All inputs are finite; a program needn't handle non-finite values.
Results may differ from a plain program's by a relative error of at most 0.0003.
Values sent between devices are 32-bit elements; how exact they have to be, the bound alone decides.
No kernel may reach another device: no remote copies, remote signals or barrier semaphores. Data moves between devices by JAX's collectives and lax.ppermute only.
A program may use at most 64 MiB of HBM per device.

v0:
```python
import math

import jax
import jax.numpy as jnp
from jax import lax
from jax.sharding import PartitionSpec as P


def exact_dot(left, right):
    return jnp.dot(left, right, precision=lax.Precision.HIGHEST, preferred_element_type=jnp.float32)


def body(database, lwe_matrix, secret_ct):
    row_count = lax.axis_size("row")
    row_rank = lax.axis_index("row")
    row_dev = database.shape[0]
    degree_all = row_dev * row_count
    sub_rows = row_dev // row_count
    a_panel = lwe_matrix[:, 0, :]
    contract_rows = (((0,), (1,)), ((), ()))
    hint_block = lax.psum_scatter(
        lax.dot_general(a_panel, database, contract_rows, preferred_element_type=jnp.float32),
        "col",
        scatter_dimension=0,
        tiled=True,
    )
    freq_low = jnp.arange(row_count, dtype=jnp.int32)
    odd_index = 2 * freq_low + 1
    by_columns = lax.all_to_all(
        hint_block[:, None, :], "row", split_axis=2, concat_axis=1, tiled=True
    )
    phase_index = freq_low[:, None] * odd_index[None, :] % (2 * row_count)
    angle_small = jnp.pi * phase_index.astype(jnp.float32) / row_count
    mixed_real = jnp.einsum(
        "jas,ak->jks", by_columns, jnp.cos(angle_small), precision=lax.Precision.HIGHEST
    )
    mixed_imag = -jnp.einsum(
        "jas,ak->jks", by_columns, jnp.sin(angle_small), precision=lax.Precision.HIGHEST
    )
    local_rows = row_rank * sub_rows + jnp.arange(sub_rows, dtype=jnp.int32)
    twist_index = odd_index[:, None] * local_rows[None, :] % (2 * degree_all)
    twist_angle = jnp.pi * twist_index.astype(jnp.float32) / degree_all
    twist_cos = jnp.cos(twist_angle)
    twist_sin = jnp.sin(twist_angle)
    turned_real = mixed_real * twist_cos + mixed_imag * twist_sin
    turned_imag = mixed_imag * twist_cos - mixed_real * twist_sin
    back_rows = lax.all_to_all(
        jnp.stack([turned_real, turned_imag]), "row", split_axis=2, concat_axis=3, tiled=True
    )
    point_real = back_rows[0, :, 0, :]
    point_imag = back_rows[1, :, 0, :]
    freq_rows = jnp.arange(row_dev, dtype=jnp.int32)
    table_index = freq_rows[:, None] * freq_rows[None, :] % row_dev
    table_angle = 2.0 * jnp.pi * table_index.astype(jnp.float32) / row_dev
    table_cos = jnp.cos(table_angle)
    table_sin = jnp.sin(table_angle)
    scale_factor = 1.0 / math.sqrt(degree_all)
    spec_real = (exact_dot(point_real, table_cos) + exact_dot(point_imag, table_sin)) * scale_factor
    spec_imag = (exact_dot(point_imag, table_cos) - exact_dot(point_real, table_sin)) * scale_factor
    cipher = secret_ct[:, :, 0]
    prod_real = jnp.sum(spec_real * cipher[:, 0] - spec_imag * cipher[:, 1], axis=1)
    prod_imag = jnp.sum(spec_real * cipher[:, 1] + spec_imag * cipher[:, 0], axis=1)
    slot_total = lax.psum(jnp.stack([prod_real, prod_imag], axis=1), ("col", "limb"))
    return slot_total / math.sqrt(2 * lwe_matrix.shape[2])


def solution(mesh):
    placed = (P(("grp", "row"), "col"), P("col", "limb", None), P(None, None, "limb", "col", "row"))
    return jax.shard_map(
        body, mesh=mesh, in_specs=placed, out_specs=P("grp", None, "row"), check_vma=False
    )
```

profile of v0, /device:TPU:0, one launch (start us, length us, event | category | flops | bytes accessed | tf_op | source)
XLA Modules:
  0.0 507.3 jit_solution(10724719638266237290)
XLA Ops:
  6.5 0.0 copy-start
  6.5 0.0 reduce-scatter.2.cloned.1.call-start
  6.5 1.6 copy-done
  8.1 9.6 %fusion.28 = f32[512,2048]{1,0:T(8,128)} fusion(bf16[2048,2048]{1,0:T(8,128)(2,1)} %param.3, bf16[2048,1,512]{2,0,1:T(8,128)(2,1)S(1)} %copy-done), kind=kOutput, calls=%fused_computation.22 | convolution fusion | flops 4294967296 | bytes 14680064 | tf_op jit(solution)/shard_map/dot_general | solution.py:22
  17.7 0.0 reduce-scatter.2.cloned.1.call-update
  17.8 79.6 %reduce-scatter.2.cloned.1.call-done = f32[128,2048]{1,0:T(8,128)} async-done(((f32[512,2048]{1,0:T(8,128)}), f32[128,2048]{1,0:T(8,128)}) %reduce-scatter.2.cloned.1.call-update) | async-done | bytes 1048592 | tf_op jit(solution)/shard_map/reduce_scatter | solution.py:21
  97.4 3.6 copy.12
  100.9 3.6 all-to-all-start
  104.6 0.2 fusion.34
  104.8 13.7 %all-to-all-done = f32[128,1,2048]{0,1,2:T(1,128)S(1)} async-done(((f32[128,1,2048]{0,1,2:T(1,128)}), f32[128,1,2048]{0,1,2:T(1,128)S(1)}, u32[]{:S(2)}, u32[]{:S(2)}) %all-to-all-start) | async-done | bytes 1048608 | tf_op jit(solution)/shard_map/all_to_all | solution.py:29
  118.4 0.0 copy-start.2
  118.4 1.0 copy-done.2
  119.4 1.6 copy.19
  121.0 3.9 convolution_negate_fusion
  124.9 4.7 add_bitcast_fusion
  129.7 0.9 pad_maximum_fusion
  130.6 0.7 copy.14
  131.3 27.3 %all_to_all.21 = f32[2,128,2,1024]{3,1,0,2:T(8,128)S(1)} all-to-all(f32[2,128,2,1024]{3,1,0,2:T(8,128)S(1)} %copy.14), channel_id=1, replica_groups=mesh['grp'=2,'col'=4,'row'=2,'limb'=2] {'row'}, dimensions={2} | all-to-all | bytes 4194304 | tf_op jit(solution)/shard_map/all_to_all | solution.py:47
  158.6 1.2 fusion.69
  159.8 2.5 copy.21
  162.3 77.7 %fusion.8 = f32[128,2048]{1,0:T(8,128)} fusion(f32[128,2048]{0,1:T(8,128)} %bitcast.52), kind=kOutput, calls=%fused_computation.11 | convolution fusion | flops 6501171200 | bytes 2097152 | tf_op jit(solution)/shard_map/dot_general | solution.py:10
  240.0 1.3 copy.20
  241.4 0.0 copy-start.4
  241.4 0.0 copy-start.5
  241.4 77.3 %fusion.10 = f32[128,2048]{1,0:T(8,128)S(1)} fusion(f32[128,2048]{0,1:T(8,128)} %bitcast.55), kind=kOutput, calls=%fused_computation.12 | convolution fusion | flops 6501171200 | bytes 2097152 | tf_op jit(solution)/shard_map/dot_general | solution.py:10
  318.7 0.0 copy-done.4
  318.7 0.0 copy-done.5
  318.7 0.0 copy-start.3
  318.7 76.5 %fusion.22 = f32[128,2048]{1,0:T(8,128)S(1)} fusion(f32[128,2048]{1,0:T(8,128)S(1)} %copy-done.5, f32[128,2048]{0,1:T(8,128)S(1)} %bitcast.56), kind=kOutput, calls=%fused_computation.17 | convolution fusion | flops 6501695488 | bytes 3145728 | tf_op jit(solution)/shard_map/dot_general | solution.py:10
  395.3 0.0 copy-done.3
  395.3 0.0 copy-start.1
  395.3 76.6 %fusion.25 = f32[128,2048]{1,0:T(8,128)S(1)} fusion(f32[128,2048]{1,0:T(8,128)S(1)} %fusion.10, f32[128,2048]{0,1:T(8,128)S(1)} %bitcast.53), kind=kOutput, calls=%fused_computation.18 | convolution fusion | flops 6501695488 | bytes 3145728 | tf_op jit(solution)/shard_map/dot_general | solution.py:10
  471.9 0.0 copy-done.1
  471.9 0.8 subtract_reduce_fusion
  472.7 26.6 %psum.7 = f32[2,2,2048]{2,0,1:T(2,128)S(1)} all-reduce(f32[2,2,2048]{2,0,1:T(2,128)S(1)} %pad_maximum_fusion.1), channel_id=1, replica_groups=mesh['grp'=2,'col'=4,'row'=2,'limb'=2] {'col','limb'}, use_global_device_ids=true, to_apply=%region_3.4 | all-reduce | flops 8192 | bytes 65536 | tf_op jit(solution)/shard_map/psum | solution.py:63
  499.4 0.6 copy.18
  (4 shorter events, 0.0 us)
Async XLA Ops:
  6.5 1.6 copy-start
  6.5 90.8 %reduce-scatter.2.cloned.1.call-start = ((), (), s32[]{:S(2)}) async-start(), calls=%async_computation.3 | async-start | bytes 5242880 | tf_op jit(solution)/shard_map/reduce_scatter | solution.py:21
  100.9 17.5 %all-to-all-start = ((f32[128,1,2048]{0,1,2:T(1,128)}), f32[128,1,2048]{0,1,2:T(1,128)S(1)}, u32[]{:S(2)}, u32[]{:S(2)}) async-start(f32[128,1,2048]{0,1,2:T(1,128)} %copy.12), calls=%async_computation.1 | async-start | bytes 2097152 | tf_op jit(solution)/shard_map/all_to_all | solution.py:29
  118.4 1.0 copy-start.2
  241.4 77.3 %copy-start.4 = (f32[1,128,2,1024]{1,3,2,0:T(8,128)S(1)}, f32[1,128,2,1024]{1,3,2,0:T(8,128)}, u32[]{:S(2)}) copy-start(f32[1,128,2,1024]{1,3,2,0:T(8,128)} %copy.20) | copy-start | bytes 3145732
  241.4 77.3 %copy-start.5 = (f32[128,2048]{1,0:T(8,128)S(1)}, f32[128,2048]{1,0:T(8,128)}, u32[]{:S(2)}) copy-start(f32[128,2048]{1,0:T(8,128)} %fusion.8) | copy-start | bytes 3145732
  318.7 76.6 %copy-start.3 = (f32[1,128,2,1024]{1,3,2,0:T(8,128)S(1)}, f32[1,128,2,1024]{1,3,2,0:T(8,128)}, u32[]{:S(2)}) copy-start(f32[1,128,2,1024]{1,3,2,0:T(8,128)} %copy.21) | copy-start | bytes 3145732
  395.3 76.6 %copy-start.1 = (f32[2,2,1,128,2048]{4,3,2,1,0:T(8,128)S(1)}, f32[2,2,1,128,2048]{4,3,2,1,0:T(8,128)}, u32[]{:S(2)}) copy-start(f32[2,2,1,128,2048]{4,3,2,1,0:T(8,128)} %param.5) | copy-start | bytes 12582916
Sparse Core Ops, SparseCore 0:
  17.9 79.4 reduce-scatter.1
where the time goes:
time: 514 us; the launch traced here: 507 us
  matrix products  326 us (63%)
  waiting for transfers between devices  93.3 us (18%)
  blocking collectives  53.9 us (10%)
  local copies, waits for them, and re-layouts  14.1 us (3%)
  between operations  14 us (3%)
    dot_general x4, matrix products, exact_dot(): jnp.dot(left, right, precision=lax.Precision.HIGHEST, preferred_element_t...  308 us
    reduce_scatter x1, waiting for transfers between devices, body(): lax.psum_scatter(lax.dot_general(a_panel, database, contract_rows, prefer...  79.6 us
    all_to_all x1, blocking collectives, body(): lax.all_to_all(jnp.stack([turned_real, turned_imag]), 'row', split_axis=2...  27.3 us
    psum x1, blocking collectives, body(): lax.psum(jnp.stack([prod_real, prod_imag], axis=1), ('col', 'limb'))  26.6 us
    all_to_all x1, waiting for transfers between devices, body(): lax.all_to_all(hint_block[:, None, :], 'row', split_axis=2, concat_axis=1...  13.7 us
  transfers between devices with their start and end apart: 2, of which 2 were waited for; matrix products, arithmetic and copies ran while one was open for 0% of the time, Pallas kernels for 0%

commit v1 on v0

v1 whole, which is shorter than its diff:
```python
import functools
import math

import jax
import jax.numpy as jnp
import numpy as np
from jax import lax
from jax.experimental import pallas as pl
from jax.experimental.pallas import tpu as pltpu
from jax.sharding import PartitionSpec as P

LANES = 128
MIB = 1 << 20


def split_bf16(x):
    high = x.astype(jnp.bfloat16)
    low = (x - high.astype(jnp.float32)).astype(jnp.bfloat16)
    return high, low


def hint_kernel(groups, parts, block, lwe_ref, data_ref, *rest):
    outs, turned = rest[:-1], rest[-1]

    @pl.when(pl.program_id(0) == 0)
    def _():
        turned[...] = lwe_ref[...].T

    for g in range(groups):
        rows = slice(g * parts * block, (g + 1) * parts * block)
        res = lax.dot_general(
            turned[rows, :], data_ref[...], (((1,), (1,)), ((), ())), preferred_element_type=jnp.float32
        )
        for k in range(parts):
            outs[k][g * block : (g + 1) * block, :] = res[k * block : (k + 1) * block, :]


def partial_hint(lwe, database, groups, parts):
    depth, columns = lwe.shape
    rows = database.shape[0]
    block = columns // (groups * parts)
    tile = min(256, rows)
    return pl.pallas_call(
        functools.partial(hint_kernel, groups, parts, block),
        grid=(rows // tile,),
        in_specs=[
            pl.BlockSpec((depth, columns), lambda i: (0, 0)),
            pl.BlockSpec((tile, depth), lambda i: (i, 0)),
        ],
        out_specs=[pl.BlockSpec((groups * block, tile), lambda i: (0, i))] * parts,
        out_shape=[jax.ShapeDtypeStruct((groups * block, rows), jnp.float32)] * parts,
        scratch_shapes=[pltpu.VMEM((columns, depth), jnp.bfloat16)],
        compiler_params=pltpu.CompilerParams(vmem_limit_bytes=48 * MIB),
        cost_estimate=pl.CostEstimate(
            flops=2 * rows * depth * columns, bytes_accessed=2 * rows * depth, transcendentals=0
        ),
    )(lwe, database)


def fft_list(re, im):
    n = len(re)
    if n == 1:
        return re, im
    er, ei = fft_list(re[0::2], im[0::2])
    odd_r, odd_i = fft_list(re[1::2], im[1::2])
    half = n // 2
    out_r, out_i = [None] * n, [None] * n
    for k in range(half):
        xr, xi = odd_r[k], odd_i[k]
        if k == 0:
            tr, ti = xr, xi
        elif 4 * k == n:
            tr, ti = xi, -xr
        elif 8 * k == n:
            c = math.sqrt(0.5)
            tr, ti = (xr + xi) * c, (xi - xr) * c
        elif 8 * k == 3 * n:
            c = math.sqrt(0.5)
            tr, ti = (xi - xr) * c, -(xr + xi) * c
        else:
            c, s = math.cos(2 * math.pi * k / n), math.sin(2 * math.pi * k / n)
            tr, ti = xr * c + xi * s, xi * c - xr * s
        out_r[k], out_i[k] = er[k] + tr, ei[k] + ti
        out_r[k + half], out_i[k + half] = er[k] - tr, ei[k] - ti
    return out_r, out_i


def transform_kernel(blocks, radix, rows, *refs):
    hints = refs[:blocks]
    first_ref, twist_ref, table_hi, table_lo, cipher_ref, out_ref, stage = refs[blocks:]
    for top in range(0, rows, 8):
        re, im = [], []
        for u in range(radix):
            lanes = slice(u * LANES, (u + 1) * LANES)
            real = imag = None
            for b in range(blocks):
                h = hints[b][top : top + 8, lanes]
                x, y = h * first_ref[2 * b : 2 * b + 1, lanes], h * first_ref[2 * b + 1 : 2 * b + 2, lanes]
                real = x if real is None else real + x
                imag = y if imag is None else imag + y
            re.append(real)
            im.append(imag)
        re, im = fft_list(re, im)
        for r in range(radix):
            c = twist_ref[2 * r : 2 * r + 1, :]
            s = twist_ref[2 * r + 1 : 2 * r + 2, :]
            at = slice(r * rows + top, r * rows + top + 8)
            stage[at, :LANES] = re[r] * c + im[r] * s
            stage[at, LANES:] = im[r] * c - re[r] * s
    for r in range(radix):
        high, low = split_bf16(stage[r * rows : (r + 1) * rows, :])
        dot = functools.partial(jnp.dot, preferred_element_type=jnp.float32)
        spec = dot(high, table_hi[...]) + (dot(low, table_hi[...]) + dot(high, table_lo[...]))
        sr, si = spec[:, :LANES], spec[:, LANES:]
        lanes = slice(r * LANES, (r + 1) * LANES)
        for c in range(2):
            a, b = cipher_ref[2 * c, :, lanes], cipher_ref[2 * c + 1, :, lanes]
            out_ref[2 * c : 2 * c + 1, lanes] = jnp.sum(sr * a - si * b, axis=0, keepdims=True)
            out_ref[2 * c + 1 : 2 * c + 2, lanes] = jnp.sum(sr * b + si * a, axis=0, keepdims=True)


def transform_products(hints, first, twist, tables, cipher, part):
    rows, points = hints[0].shape
    radix = points // LANES
    whole = lambda a: pl.BlockSpec(a.shape, lambda i: (0,) * a.ndim)
    return pl.pallas_call(
        functools.partial(transform_kernel, len(hints), radix, rows),
        grid=(1,),
        in_specs=[whole(h) for h in hints]
        + [whole(first), whole(twist), whole(tables[0]), whole(tables[1])]
        + [pl.BlockSpec((4, rows, points), lambda i: (0, part, 0))],
        out_specs=pl.BlockSpec((4, points), lambda i: (0, 0)),
        out_shape=jax.ShapeDtypeStruct((4, points), jnp.float32),
        scratch_shapes=[pltpu.VMEM((radix * rows, 2 * LANES), jnp.float32)],
        compiler_params=pltpu.CompilerParams(vmem_limit_bytes=32 * MIB),
        cost_estimate=pl.CostEstimate(
            flops=6 * radix * rows * 256 * 256, bytes_accessed=24 * rows * points, transcendentals=0
        ),
    )(*hints, first, twist, *tables, cipher)


def xor_pairs(size, step):
    return [(i, i ^ step) for i in range(size)]


def sum_over(x, axes):
    for axis in axes:
        size = lax.axis_size(axis)
        if size & (size - 1):
            x = lax.psum(x, axis)
            continue
        step = 1
        while step < size:
            x = x + lax.ppermute(x, axis, xor_pairs(size, step))
            step *= 2
    return x


def body(parts, database, lwe_matrix, secret_ct):
    row_count, row_rank = lax.axis_size("row"), lax.axis_index("row")
    col_count = lax.axis_size("col")
    points = database.shape[0]
    degree = points * row_count
    radix = points // LANES
    own = secret_ct.shape[3]

    cipher = secret_ct.reshape(4, own, LANES, radix).swapaxes(2, 3).reshape(4, own, points)

    source = (row_rank + jnp.arange(row_count, dtype=jnp.int32)) % row_count if row_count == 2 else jnp.arange(row_count, dtype=jnp.int32)
    index = (source[:, None] * points + jnp.arange(points, dtype=jnp.int32)[None, :]) * (2 * row_rank + 1) % (2 * degree)
    angle = index.astype(jnp.float32) * (np.pi / degree)
    first = jnp.stack([jnp.cos(angle), -jnp.sin(angle)], axis=1).reshape(2 * row_count, points)
    lane = np.arange(LANES)
    turn = 2 * np.pi * (np.arange(radix)[:, None] * lane[None, :] % points) / points
    twist = jnp.asarray(np.stack([np.cos(turn), np.sin(turn)], axis=1).reshape(2 * radix, LANES), jnp.float32)
    small = 2 * np.pi * (lane[:, None] * lane[None, :] % LANES) / LANES
    table = np.block([[np.cos(small), -np.sin(small)], [np.sin(small), np.cos(small)]]).astype(np.float32)
    high = table.astype(jnp.bfloat16)
    low = (table - high.astype(np.float32)).astype(jnp.bfloat16)
    tables = (jnp.asarray(high), jnp.asarray(low))

    partial = partial_hint(lwe_matrix[:, 0, :], database, col_count, parts)
    total = None
    for k in range(parts):
        mine = lax.psum_scatter(partial[k], "col", scatter_dimension=0, tiled=True)
        if row_count == 2:
            hints = [mine, lax.ppermute(mine, "row", [(0, 1), (1, 0)])]
        else:
            gathered = lax.all_gather(mine, "row")
            hints = [gathered[b] for b in range(row_count)]
        part = transform_products(hints, first, twist, tables, cipher, k)
        total = part if total is None else total + part
    total = sum_over(total, ("limb", "col"))
    scale = 1.0 / (math.sqrt(degree) * math.sqrt(2 * lwe_matrix.shape[2]))
    total = total.reshape(4, radix, LANES).swapaxes(1, 2).reshape(2, 2, points)
    return total * scale


def solution(mesh):
    placed = (P(("grp", "row"), "col"), P("col", "limb", None), P(None, None, "limb", "col", "row"))

    def whole(database, lwe_matrix, secret_ct):
        own = lwe_matrix.shape[2] // mesh.shape["col"]
        parts = 2 if own % 16 == 0 else 1
        return jax.shard_map(
            functools.partial(body, parts), mesh=mesh, in_specs=placed, out_specs=P("grp", None, "row"), check_vma=False
        )(database, lwe_matrix, secret_ct)

    return whole
```

time: 514 us -> 157 us (0.31); the launches traced: 507 us -> 156 us
  matrix products: 326 us -> 0 us
  blocking collectives: 53.9 us -> 0 us
  Pallas kernels: 0 us -> 18.3 us
  local copies, waits for them, and re-layouts: 14.1 us -> 20.1 us
  waiting for transfers between devices: 93.3 us -> 99 us
    dot_general x7 -> x0, matrix products: 326 us -> none  [the longest x4 308 us: exact_dot(): jnp.dot(left, right, precision=lax.Precision.HIGHEST, preferred_element_t...]
    all_to_all x1 -> x0, blocking collectives: 27.3 us -> none  [body(): lax.all_to_all(jnp.stack([turned_real, turned_imag]), 'row', split_axis=2...]
    psum x1 -> x0, blocking collectives: 26.6 us -> none  [body(): lax.psum(jnp.stack([prod_real, prod_imag], axis=1), ('col', 'limb'))]
    pallas_call x0 -> x3, Pallas kernels: none -> 18.3 us  [the longest x1 15.3 us: partial_hint(): pl.pallas_call(functools.partial(hint_kernel, groups, parts, block), grid...]
    all_to_all x1 -> x0, waiting for transfers between devices: 13.7 us -> none  [body(): lax.all_to_all(hint_block[:, None, :], 'row', split_axis=2, concat_axis=1...]
    reduce_scatter x1 -> x2, waiting for transfers between devices: 79.6 us -> 90.1 us  [body(): mine = lax.psum_scatter(partial[k], 'col', scatter_dimension=0, tiled=True)]
    ppermute x0 -> x5, waiting for transfers between devices: none -> 8.19 us  [the longest x3 8.19 us: sum_over(): x = x + lax.ppermute(x, axis, xor_pairs(size, step))]
    transpose x0 -> x1, local copies, waits for them, and re-layouts: none -> 5.77 us  [body(): secret_ct.reshape(4, own, LANES, radix).swapaxes(2, 3)]
  transfers between devices with their start and end apart: 2 -> 7, of which waited for: 2 -> 5; matrix products, arithmetic and copies ran while one was open for 0% -> 11% of each run, Pallas kernels for 0% -> 1%
where the time goes in v1:
time: 157 us; the launch traced here: 156 us
  waiting for transfers between devices  99 us (63%)
  local copies, waits for them, and re-layouts  20.1 us (13%)
  Pallas kernels  18.3 us (12%)
  between operations  13.5 us (9%)
  starting transfers between devices  4.91 us (3%)
    reduce_scatter x2, waiting for transfers between devices, body(): mine = lax.psum_scatter(partial[k], 'col', scatter_dimension=0, tiled=True)  90.1 us
    pallas_call x1, Pallas kernels, partial_hint(): pl.pallas_call(functools.partial(hint_kernel, groups, parts, block), grid...  15.3 us
    unnamed x16, local copies, waits for them, and re-layouts  8.41 us
    ppermute x3, waiting for transfers between devices, sum_over(): x = x + lax.ppermute(x, axis, xor_pairs(size, step))  8.19 us
    transpose x1, local copies, waits for them, and re-layouts, body(): secret_ct.reshape(4, own, LANES, radix).swapaxes(2, 3)  5.77 us
    reshape x1, local copies, waits for them, and re-layouts, body(): secret_ct.reshape(4, own, LANES, radix).swapaxes(2, 3)  4.99 us
  transfers between devices with their start and end apart: 7, of which 5 were waited for; matrix products, arithmetic and copies ran while one was open for 11% of the time, Pallas kernels for 1%

profile of v1, /device:TPU:0, one launch (start us, length us, event | category | flops | bytes accessed | tf_op | source)
XLA Modules:
  0.0 156.5 jit_solution(16303756680195275632)
XLA Ops:
  6.5 0.0 reduce-scatter.5.cloned.1.call-start
  6.5 15.3 %shard_map.64 = (f32[256,2048]{1,0:T(8,128)}, f32[256,2048]{1,0:T(8,128)}) custom-call(bf16[2048,512]{1,0:T(8,128)(2,1)} %bitcast.15, bf16[2048,2048]{1,0:T(8,128)(2,1)} %data_ref.1), custom_call_target="tpu_custom_call" | custom-call | flops 4294967296 | bytes 8388608 | tf_op jit(solution)/shard_map/pallas_call | solution.py:43
  21.9 0.0 reduce-scatter.5.cloned.1.call-update
  21.9 0.0 reduce-scatter.3.cloned.1.call-start
  22.0 0.7 reduce-scatter.3.cloned.1.call-update
  22.7 46.0 %reduce-scatter.5.cloned.1.call-done.refs_0_ = f32[64,2048]{1,0:T(8,128)} async-done(((f32[256,2048]{1,0:T(8,128)}), f32[64,2048]{1,0:T(8,128)}) %reduce-scatter.5.cloned.1.call-update) | async-done | bytes 524304 | tf_op jit(solution)/shard_map/reduce_scatter | solution.py:185
  68.6 1.5 collective-permute-start.1
  70.1 44.1 %reduce-scatter.3.cloned.1.call-done.refs_0_ = f32[64,2048]{1,0:T(8,128)} async-done(((f32[256,2048]{1,0:T(8,128)}), f32[64,2048]{1,0:T(8,128)}) %reduce-scatter.3.cloned.1.call-update) | async-done | bytes 524304 | tf_op jit(solution)/shard_map/reduce_scatter | solution.py:185
  114.2 1.5 collective-permute-start
  115.7 0.6 fusion.3
  116.4 5.4 %copy.9 = f32[2,2,1,128,2048]{3,4,1,0,2:T(8,128)} copy(f32[2,2,1,128,2048]{4,3,2,1,0:T(8,128)} %param.8) | data formatting | bytes 8388608 | tf_op args[2]
  121.8 5.8 %copy.10 = f32[4,128,16,128]{3,2,1,0:T(8,128)} copy(f32[4,128,16,128]{1,2,3,0:T(8,128)} %bitcast.12) | data formatting | bytes 8388608 | tf_op jit(solution)/shard_map/transpose | solution.py:167
  127.5 0.0 copy-start.2
  127.6 0.0 copy-start.3
  127.6 0.0 copy-start.4
  127.6 0.0 copy-start.6
  127.6 5.0 %reshape.133.refs_6_ = f32[4,128,2048]{2,1,0:T(8,128)} reshape(f32[4,128,16,128]{3,2,1,0:T(8,128)} %copy.10) | data formatting | bytes 8388608 | tf_op jit(solution)/shard_map/reshape | solution.py:167
  132.5 0.0 collective-permute-done.1.refs_1_
  132.6 0.0 copy-done.2
  132.6 0.0 copy-done.3
  132.6 0.0 copy-done.4
  132.6 0.0 copy-done.6
  132.6 0.0 copy-start
  132.6 2.2 %copy-done = f32[4,128,2048]{2,1,0:T(8,128)S(1)} copy-done((f32[4,128,2048]{2,1,0:T(8,128)S(1)}, f32[4,128,2048]{2,1,0:T(8,128)}, u32[]{:S(2)}) %copy-start) | copy-done | bytes 4194328
  134.8 0.0 copy-start.1
  134.8 0.0 copy-start.5
  134.8 1.5 shard_map.66
  136.2 0.0 collective-permute-done.refs_1_
  136.2 0.7 copy-done.1
  137.0 0.1 copy-done.5
  137.1 1.5 shard_map.65
  138.6 0.1 collective-permute-start.2
  138.6 1.2 collective-permute-done.2
  139.8 0.1 collective-permute-start.3
  139.9 3.9 %collective-permute-done.3 = f32[4,2048]{1,0:T(4,128)S(1)} collective-permute-done((f32[4,2048]{1,0:T(4,128)S(1)}, f32[4,2048]{1,0:T(4,128)S(1)}, u32[]{:S(2)}, u32[]{:S(2)}) %collective-permute-start.3) | collective-permute-done | bytes 32800 | tf_op jit(solution)/shard_map/ppermute | solution.py:154
  143.8 1.8 %collective-permute-start.4 = (f32[4,2048]{1,0:T(4,128)S(1)}, f32[4,2048]{1,0:T(4,128)S(1)}, u32[]{:S(2)}, u32[]{:S(2)}) collective-permute-start(f32[4,2048]{1,0:T(4,128)S(1)} %add.90), channel_id=1, source_target_pairs={{0,8},{4,12},{8,0},{12,4},{1,9},{5,13},{9,1},{13,5},{2,10},{6,14},... | collective-permute-start | bytes 98312 | tf_op jit(solution)/shard_map/ppermute | solution.py:154
  145.6 3.1 %collective-permute-done.4 = f32[4,2048]{1,0:T(4,128)S(1)} collective-permute-done((f32[4,2048]{1,0:T(4,128)S(1)}, f32[4,2048]{1,0:T(4,128)S(1)}, u32[]{:S(2)}, u32[]{:S(2)}) %collective-permute-start.4) | collective-permute-done | bytes 32800 | tf_op jit(solution)/shard_map/ppermute | solution.py:154
  148.7 0.1 copy.11
  148.9 0.8 mul.70
  (8 shorter events, 0.1 us)
Async XLA Ops:
  6.5 62.1 %reduce-scatter.5.cloned.1.call-start = ((), (), s32[]{:S(2)}) async-start(), calls=%async_computation.3 | async-start | bytes 2621440 | tf_op jit(solution)/shard_map/reduce_scatter | solution.py:185
  21.9 92.3 %reduce-scatter.3.cloned.1.call-start = ((), (), s32[]{:S(2)}) async-start(), calls=%async_computation.2 | async-start | bytes 2621440 | tf_op jit(solution)/shard_map/reduce_scatter | solution.py:185
  68.6 63.9 %collective-permute-start.1 = (f32[64,2048]{1,0:T(8,128)}, f32[64,2048]{1,0:T(8,128)S(1)}, u32[]{:S(2)}, u32[]{:S(2)}) collective-permute-start(f32[64,2048]{1,0:T(8,128)} %reduce-scatter.5.cloned.1.call-done.refs_0_), channel_id=1, source_target_pairs={{0,2},{2,0},{1,3},{3,1},{4,6},{6,4},{5,7},{7,5},{8,10},{10,8},{9,1... | collective-permute-start | bytes 1572872 | tf_op jit(solution)/shard_map/ppermute | solution.py:187
  114.2 22.0 %collective-permute-start = (f32[64,2048]{1,0:T(8,128)}, f32[64,2048]{1,0:T(8,128)S(1)}, u32[]{:S(2)}, u32[]{:S(2)}) collective-permute-start(f32[64,2048]{1,0:T(8,128)} %reduce-scatter.3.cloned.1.call-done.refs_0_), channel_id=1, source_target_pairs={{0,2},{2,0},{1,3},{3,1},{4,6},{6,4},{5,7},{7,5},{8,10},{10,8},{9,1... | collective-permute-start | bytes 1572872 | tf_op jit(solution)/shard_map/ppermute | solution.py:187
  127.5 5.0 %copy-start.2 = (bf16[256,256]{1,0:T(8,128)(2,1)S(1)}, bf16[256,256]{1,0:T(8,128)(2,1)}, u32[]{:S(2)}) copy-start(bf16[256,256]{1,0:T(8,128)(2,1)} %constant.48.clone.refs_5_) | copy-start | bytes 393220
  127.6 5.0 %copy-start.3 = (bf16[256,256]{1,0:T(8,128)(2,1)S(1)}, bf16[256,256]{1,0:T(8,128)(2,1)}, u32[]{:S(2)}) copy-start(bf16[256,256]{1,0:T(8,128)(2,1)} %constant.47.clone.refs_4_) | copy-start | bytes 393220
  127.6 5.0 %copy-start.4 = (f32[64,2048]{1,0:T(8,128)S(1)}, f32[64,2048]{1,0:T(8,128)}, u32[]{:S(2)}) copy-start(f32[64,2048]{1,0:T(8,128)} %reduce-scatter.5.cloned.1.call-done.refs_0_) | copy-start | bytes 1572868
  127.6 5.0 %copy-start.6 = (f32[32,128]{1,0:T(8,128)S(1)}, f32[32,128]{1,0:T(8,128)}, u32[]{:S(2)}) copy-start(f32[32,128]{1,0:T(8,128)} %constant.46.clone.refs_3_) | copy-start | bytes 49156
  132.6 2.2 %copy-start = (f32[4,128,2048]{2,1,0:T(8,128)S(1)}, f32[4,128,2048]{2,1,0:T(8,128)}, u32[]{:S(2)}) copy-start(f32[4,128,2048]{2,1,0:T(8,128)} %reshape.133.refs_6_) | copy-start | bytes 12582916
  134.8 2.2 %copy-start.1 = (f32[4,128,2048]{2,1,0:T(8,128)S(1)}, f32[4,128,2048]{2,1,0:T(8,128)}, u32[]{:S(2)}) copy-start(f32[4,128,2048]{2,1,0:T(8,128)} %reshape.133.refs_6_) | copy-start | bytes 12582916
  134.8 2.3 %copy-start.5 = (f32[64,2048]{1,0:T(8,128)S(1)}, f32[64,2048]{1,0:T(8,128)}, u32[]{:S(2)}) copy-start(f32[64,2048]{1,0:T(8,128)} %reduce-scatter.3.cloned.1.call-done.refs_0_) | copy-start | bytes 1572868
  138.6 1.3 collective-permute-start.2
  139.8 4.0 %collective-permute-start.3 = (f32[4,2048]{1,0:T(4,128)S(1)}, f32[4,2048]{1,0:T(4,128)S(1)}, u32[]{:S(2)}, u32[]{:S(2)}) collective-permute-start(f32[4,2048]{1,0:T(4,128)S(1)} %add.89), channel_id=1, source_target_pairs={{0,4},{4,0},{8,12},{12,8},{1,5},{5,1},{9,13},{13,9},{2,6},{6,2},{1... | collective-permute-start | bytes 98312 | tf_op jit(solution)/shard_map/ppermute | solution.py:154
  143.8 4.9 %collective-permute-start.4 = (f32[4,2048]{1,0:T(4,128)S(1)}, f32[4,2048]{1,0:T(4,128)S(1)}, u32[]{:S(2)}, u32[]{:S(2)}) collective-permute-start(f32[4,2048]{1,0:T(4,128)S(1)} %add.90), channel_id=1, source_target_pairs={{0,8},{4,12},{8,0},{12,4},{1,9},{5,13},{9,1},{13,5},{2,10},{6,14},... | collective-permute-start | bytes 98312 | tf_op jit(solution)/shard_map/ppermute | solution.py:154
Sparse Core Ops, SparseCore 0:
  22.0 46.5 reduce-scatter.4
  71.0 43.1 reduce-scatter.2

commit v2 on v1

--- a/solution.py
+++ b/solution.py
@@ -11,6 +11,11 @@
 
 LANES = 128
 MIB = 1 << 20
+SWAP = [(0, 1), (1, 0)]
+NEIGHBOURS = [(0, 1), (1, 0), (2, 3), (3, 2)]
+END_TO_FAR_MIDDLE = [(0, 2), (3, 1)]
+CROSS = [(1, 2), (2, 1)]
+ROUND = [(0, 1), (1, 3), (3, 2), (2, 0)]
 
 
 def split_bf16(x):
@@ -55,6 +60,139 @@
             flops=2 * rows * depth * columns, bytes_accessed=2 * rows * depth, transcendentals=0
         ),
     )(lwe, database)
+
+
+def at_end():
+    z = lax.axis_index("col")
+    return jnp.logical_or(z == 0, z == 3)
+
+
+def role_block(role):
+    place = jnp.where(at_end(), role[0], role[1])
+    return jnp.where(lax.axis_index("col") >= 2, place, 3 - place)
+
+
+def line_hint_kernel(roles, cuts, tile, lwe_ref, data_ref, *rest):
+    outs = rest[: sum(len(c) for c in cuts)]
+    lwe_v, data_v, turned, lwe_sem, data_sem = rest[len(outs) :]
+    rows = data_ref.shape[0]
+    own = lwe_v.shape[2]
+    copies = []
+    for b, role in enumerate(roles):
+        at = pl.multiple_of(role_block(role) * own, own)
+        copies.append(pltpu.make_async_copy(lwe_ref.at[:, pl.ds(at, own)], lwe_v.at[b], lwe_sem.at[b]))
+    tiles = []
+    for i in range(rows // tile):
+        at = slice(i * tile, (i + 1) * tile)
+        tiles.append(pltpu.make_async_copy(data_ref.at[at, :], data_v.at[at, :], data_sem.at[i]))
+    for c in copies + tiles:
+        c.start()
+    for b, c in enumerate(copies):
+        c.wait()
+        turned[b * own : (b + 1) * own, :] = lwe_v[b].T
+    for i, c in enumerate(tiles):
+        c.wait()
+        at = slice(i * tile, (i + 1) * tile)
+        res = lax.dot_general(
+            turned[...], data_v[at, :], (((1,), (1,)), ((), ())), preferred_element_type=jnp.float32
+        )
+        n = 0
+        for b in range(len(roles)):
+            top = b * own
+            for rows_k in cuts[b]:
+                outs[n][:, at] = res[top : top + rows_k, :]
+                top += rows_k
+                n += 1
+
+
+def line_hint(lwe, database, roles, cuts):
+    depth, columns = lwe.shape
+    rows = database.shape[0]
+    own = columns // 4
+    tile = min(512, rows)
+    flat = pl.pallas_call(
+        functools.partial(line_hint_kernel, roles, cuts, tile),
+        in_specs=[pl.BlockSpec(memory_space=pl.ANY)] * 2,
+        out_shape=[jax.ShapeDtypeStruct((k, rows), jnp.float32) for c in cuts for k in c],
+        scratch_shapes=[
+            pltpu.VMEM((len(roles), depth, own), jnp.bfloat16),
+            pltpu.VMEM((rows, depth), jnp.bfloat16),
+            pltpu.VMEM((len(roles) * own, depth), jnp.bfloat16),
+            pltpu.SemaphoreType.DMA((len(roles),)),
+            pltpu.SemaphoreType.DMA((rows // tile,)),
+        ],
+        compiler_params=pltpu.CompilerParams(vmem_limit_bytes=56 * MIB),
+        cost_estimate=pl.CostEstimate(
+            flops=2 * rows * depth * own * len(roles), bytes_accessed=2 * rows * depth, transcendentals=0
+        ),
+    )(lwe, database)
+    out, n = [], 0
+    for c in cuts:
+        out.append(list(flat[n : n + len(c)]))
+        n += len(c)
+    return out
+
+
+def pass_kernel(cuts, own_ref, got_ref, *outs):
+    top = 0
+    keep = jnp.where(at_end(), 0.0, 1.0)
+    for k, rows in enumerate(cuts):
+        at = slice(top, top + rows)
+        outs[k][...] = own_ref[at, :] + got_ref[at, :] * keep
+        top += rows
+
+
+def pass_on(own, got, cuts):
+    return pl.pallas_call(
+        functools.partial(pass_kernel, cuts),
+        out_shape=[jax.ShapeDtypeStruct((k, own.shape[1]), jnp.float32) for k in cuts],
+        compiler_params=pltpu.CompilerParams(vmem_limit_bytes=16 * MIB),
+        cost_estimate=pl.CostEstimate(flops=own.size, bytes_accessed=0, transcendentals=0),
+    )(own, got)
+
+
+def final_kernel(own_ref, near_ref, direct_ref, cross_ref, last_ref, sum_ref):
+    keep = jnp.where(at_end(), 1.0, 0.0)
+    sum_ref[...] = (own_ref[...] + near_ref[...] * keep) + (direct_ref[...] + cross_ref[...]) + last_ref[...]
+
+
+def final_hint(top, own, near, direct, cross, last):
+    cut = pl.BlockSpec(last.shape, lambda i: (top // last.shape[0], 0))
+    whole = pl.BlockSpec(last.shape, lambda i: (0, 0))
+    return pl.pallas_call(
+        final_kernel,
+        grid=(1,),
+        in_specs=[cut, cut, cut, cut, whole],
+        out_specs=whole,
+        out_shape=jax.ShapeDtypeStruct(last.shape, jnp.float32),
+        compiler_params=pltpu.CompilerParams(vmem_limit_bytes=16 * MIB),
+        cost_estimate=pl.CostEstimate(flops=last.size, bytes_accessed=0, transcendentals=0),
+    )(own, near, direct, cross, last)
+
+
+def swap_kernel(radix, in_ref, out_ref, stage):
+    groups, rows = in_ref.shape[:2]
+    for k in range(radix):
+        lanes = slice(k * LANES, (k + 1) * LANES)
+        stage[lanes, :] = in_ref[:, :, lanes].reshape(groups * rows, LANES).T
+    for r in range(radix):
+        picked = stage[pl.ds(r, LANES, stride=radix), :].T
+        out_ref[:, :, r * LANES : (r + 1) * LANES] = picked.reshape(groups, rows, LANES)
+
+
+def swap_digits(cipher, offset, rows):
+    points = cipher.shape[2]
+    radix = points // LANES
+    return pl.pallas_call(
+        functools.partial(swap_kernel, radix),
+        grid=(1,),
+        in_specs=[pl.BlockSpec((4, rows, points), lambda i: (0, offset // rows, 0))],
+        out_specs=pl.BlockSpec((4, rows, points), lambda i: (0, 0, 0)),
+        out_shape=jax.ShapeDtypeStruct((4, rows, points), jnp.float32),
+        scratch_shapes=[pltpu.VMEM((points, 4 * rows), jnp.float32)],
+        compiler_params=pltpu.CompilerParams(vmem_limit_bytes=16 * MIB),
+        cost_estimate=pl.CostEstimate(flops=0, bytes_accessed=32 * rows * points, transcendentals=0),
+    )(cipher)
 
 
 def fft_list(re, im):
@@ -87,7 +225,7 @@
 
 def transform_kernel(blocks, radix, rows, *refs):
     hints = refs[:blocks]
-    first_ref, twist_ref, table_hi, table_lo, cipher_ref, out_ref, stage = refs[blocks:]
+    first_ref, twist_ref, table_hi, table_lo, cipher_ref, total_ref, out_ref, stage = refs[blocks:]
     for top in range(0, rows, 8):
         re, im = [], []
         for u in range(radix):
@@ -115,11 +253,13 @@
         lanes = slice(r * LANES, (r + 1) * LANES)
         for c in range(2):
             a, b = cipher_ref[2 * c, :, lanes], cipher_ref[2 * c + 1, :, lanes]
-            out_ref[2 * c : 2 * c + 1, lanes] = jnp.sum(sr * a - si * b, axis=0, keepdims=True)
-            out_ref[2 * c + 1 : 2 * c + 2, lanes] = jnp.sum(sr * b + si * a, axis=0, keepdims=True)
-
-
-def transform_products(hints, first, twist, tables, cipher, part):
+            real = jnp.sum(sr * a - si * b, axis=0, keepdims=True)
+            imag = jnp.sum(sr * b + si * a, axis=0, keepdims=True)
+            out_ref[2 * c : 2 * c + 1, lanes] = total_ref[2 * c : 2 * c + 1, lanes] + real
+            out_ref[2 * c + 1 : 2 * c + 2, lanes] = total_ref[2 * c + 1 : 2 * c + 2, lanes] + imag
+
+
+def transform_products(hints, first, twist, tables, cipher, part, total):
     rows, points = hints[0].shape
     radix = points // LANES
     whole = lambda a: pl.BlockSpec(a.shape, lambda i: (0,) * a.ndim)
@@ -128,7 +268,7 @@
         grid=(1,),
         in_specs=[whole(h) for h in hints]
         + [whole(first), whole(twist), whole(tables[0]), whole(tables[1])]
-        + [pl.BlockSpec((4, rows, points), lambda i: (0, part, 0))],
+        + [pl.BlockSpec((4, rows, points), lambda i: (0, part, 0)), whole(total)],
         out_specs=pl.BlockSpec((4, points), lambda i: (0, 0)),
         out_shape=jax.ShapeDtypeStruct((4, points), jnp.float32),
         scratch_shapes=[pltpu.VMEM((radix * rows, 2 * LANES), jnp.float32)],
@@ -136,7 +276,7 @@
         cost_estimate=pl.CostEstimate(
             flops=6 * radix * rows * 256 * 256, bytes_accessed=24 * rows * points, transcendentals=0
         ),
-    )(*hints, first, twist, *tables, cipher)
+    )(*hints, first, twist, *tables, cipher, total)
 
 
 def xor_pairs(size, step):
@@ -156,6 +296,24 @@
     return x
 
 
+def line_parts(lwe, database, cipher, cuts):
+    own = cipher.shape[1]
+    (first,), (far_mid,), (kept,), (later,) = line_hint(
+        lwe, database, [(0, 3), (1, 1), (3, 2), (2, 0)], [[own]] * 4
+    )
+    near = lax.ppermute(first, "col", NEIGHBOURS)
+    direct = lax.ppermute(far_mid, "col", END_TO_FAR_MIDDLE)
+    cross = lax.ppermute(far_mid, "col", CROSS)
+    cipher = lax.optimization_barrier((cipher, first))[0]
+    tops = [sum(cuts[:k]) for k in range(len(cuts))]
+    swapped = [swap_digits(cipher, top, rows) for top, rows in zip(tops, cuts)]
+    near, swapped = lax.optimization_barrier((near, swapped))
+    last = [lax.ppermute(x, "col", ROUND) for x in pass_on(later, near, cuts)]
+    for k, top in enumerate(tops):
+        mine = final_hint(top, kept, near, direct, cross, last[k])
+        yield [mine, lax.ppermute(mine, "row", SWAP)], swapped[k]
+
+
 def body(parts, database, lwe_matrix, secret_ct):
     row_count, row_rank = lax.axis_size("row"), lax.axis_index("row")
     col_count = lax.axis_size("col")
@@ -163,8 +321,6 @@
     degree = points * row_count
     radix = points // LANES
     own = secret_ct.shape[3]
-
-    cipher = secret_ct.reshape(4, own, LANES, radix).swapaxes(2, 3).reshape(4, own, points)
 
     source = (row_rank + jnp.arange(row_count, dtype=jnp.int32)) % row_count if row_count == 2 else jnp.arange(row_count, dtype=jnp.int32)
     index = (source[:, None] * points + jnp.arange(points, dtype=jnp.int32)[None, :]) * (2 * row_rank + 1) % (2 * degree)
@@ -179,17 +335,24 @@
     low = (table - high.astype(np.float32)).astype(jnp.bfloat16)
     tables = (jnp.asarray(high), jnp.asarray(low))
 
-    partial = partial_hint(lwe_matrix[:, 0, :], database, col_count, parts)
-    total = None
-    for k in range(parts):
-        mine = lax.psum_scatter(partial[k], "col", scatter_dimension=0, tiled=True)
-        if row_count == 2:
-            hints = [mine, lax.ppermute(mine, "row", [(0, 1), (1, 0)])]
-        else:
-            gathered = lax.all_gather(mine, "row")
-            hints = [gathered[b] for b in range(row_count)]
-        part = transform_products(hints, first, twist, tables, cipher, k)
-        total = part if total is None else total + part
+    lwe = lwe_matrix[:, 0, :]
+    cipher = secret_ct.reshape(4, own, points)
+    total = jnp.zeros((4, points), jnp.float32)
+    if col_count == 4 and row_count == 2 and own == LANES and points % 512 == 0:
+        cuts = [32, 32, 32, 32]
+        for hints, swapped in line_parts(lwe, database, cipher, cuts):
+            total = transform_products(hints, first, twist, tables, swapped, 0, total)
+    else:
+        swapped = cipher.reshape(4, own, LANES, radix).swapaxes(2, 3).reshape(4, own, points)
+        partial = partial_hint(lwe, database, col_count, parts)
+        for k in range(parts):
+            mine = lax.psum_scatter(partial[k], "col", scatter_dimension=0, tiled=True)
+            if row_count == 2:
+                hints = [mine, lax.ppermute(mine, "row", SWAP)]
+            else:
+                gathered = lax.all_gather(mine, "row")
+                hints = [gathered[b] for b in range(row_count)]
+            total = transform_products(hints, first, twist, tables, swapped, k, total)
     total = sum_over(total, ("limb", "col"))
     scale = 1.0 / (math.sqrt(degree) * math.sqrt(2 * lwe_matrix.shape[2]))
     total = total.reshape(4, radix, LANES).swapaxes(1, 2).reshape(2, 2, points)

time: 157 us -> 117 us (0.75)
  waiting for transfers between devices: 99 us -> 48.1 us
  starting transfers between devices: 4.91 us -> 25.5 us
  between operations: 13.5 us -> 0.26 us
  Pallas kernels: 18.3 us -> 30.4 us
  local copies, waits for them, and re-layouts: 20.1 us -> 11.2 us
    reduce_scatter x2 -> x0, waiting for transfers between devices: 90.1 us -> none  [body(): mine = lax.psum_scatter(partial[k], 'col', scatter_dimension=0, tiled=True)]
    ppermute x2 -> x11, waiting for transfers between devices: 0.01 us -> 39.3 us  [the longest x1 14.7 us: line_parts(): direct = lax.ppermute(far_mid, 'col', END_TO_FAR_MIDDLE)]
    ppermute x2 -> x11, starting transfers between devices: 2.93 us -> 24.1 us  [the longest x4 8.84 us: line_parts(): last = [lax.ppermute(x, 'col', ROUND) for x in pass_on(later, near, cuts)]]
    pallas_call x1 -> x10, Pallas kernels: 15.3 us -> 21.5 us  [the longest x1 10.9 us: line_hint(): pl.pallas_call(functools.partial(line_hint_kernel, roles, cuts, tile), in...]
    pallas_call x2 -> x4, Pallas kernels: 2.91 us -> 8.88 us  [transform_products(): pl.pallas_call(functools.partial(transform_kernel, len(hints), radix, row...]
    transpose x1 -> x0, local copies, waits for them, and re-layouts: 5.77 us -> none  [body(): secret_ct.reshape(4, own, LANES, radix).swapaxes(2, 3)]
    reshape x1 -> x0, local copies, waits for them, and re-layouts: 4.99 us -> none  [body(): secret_ct.reshape(4, own, LANES, radix).swapaxes(2, 3)]
    unnamed x16 -> x33, local copies, waits for them, and re-layouts: 8.41 us -> 10.3 us
  transfers between devices with their start and end apart: 7 -> 14, of which waited for: 5 -> 9; matrix products, arithmetic and copies ran while one was open for 11% -> 1% of each run, Pallas kernels for 1% -> 15%
where the time goes in v2:
time: 117 us; the launch traced here: 116 us
  waiting for transfers between devices  48.1 us (41%)
  Pallas kernels  30.4 us (26%)
  starting transfers between devices  25.5 us (22%)
  local copies, waits for them, and re-layouts  11.2 us (10%)
    ppermute x1, waiting for transfers between devices, line_parts(): direct = lax.ppermute(far_mid, 'col', END_TO_FAR_MIDDLE)  14.7 us
    ppermute x4, waiting for transfers between devices, line_parts(): last = [lax.ppermute(x, 'col', ROUND) for x in pass_on(later, near, cuts)]  13.6 us
    ppermute x1, waiting for transfers between devices, line_parts(): near = lax.ppermute(first, 'col', NEIGHBOURS)  11 us
    pallas_call x1, Pallas kernels, line_hint(): pl.pallas_call(functools.partial(line_hint_kernel, roles, cuts, tile), in...  10.9 us
    unnamed x33, local copies, waits for them, and re-layouts  10.3 us
    pallas_call x4, Pallas kernels, transform_products(): pl.pallas_call(functools.partial(transform_kernel, len(hints), radix, row...  8.88 us
    ppermute x4, starting transfers between devices, line_parts(): last = [lax.ppermute(x, 'col', ROUND) for x in pass_on(later, near, cuts)]  8.84 us
    ppermute x3, waiting for transfers between devices, sum_over(): x = x + lax.ppermute(x, axis, xor_pairs(size, step))  8.8 us
  transfers between devices with their start and end apart: 14, of which 9 were waited for; matrix products, arithmetic and copies ran while one was open for 1% of the time, Pallas kernels for 15%

profile of v2, /device:TPU:0, one launch (start us, length us, event | category | flops | bytes accessed | tf_op | source)
XLA Modules:
  0.0 116.1 jit_solution(16997796952023980629)
XLA Ops:
  0.0 10.9 %shard_map.64 = (f32[128,2048]{1,0:T(8,128)}, f32[128,2048]{1,0:T(8,128)}, f32[128,2048]{1,0:T(8,128)}, f32[128,2048]{1,0:T(8,128)}) custom-call(bf16[2048,512]{1,0:T(8,128)(2,1)} %bitcast.14, bf16[2048,2048]{1,0:T(8,128)(2,1)} %data_ref.1), custom_call_target="tpu_custom_call" | custom-call | flops 4294967296 | bytes 8388608 | tf_op jit(solution)/shard_map/pallas_call | solution.py:113
  10.9 3.1 %collective-permute-start = (f32[128,2048]{1,0:T(8,128)}, f32[128,2048]{1,0:T(8,128)S(1)}, u32[]{:S(2)}, u32[]{:S(2)}) collective-permute-start(f32[128,2048]{1,0:T(8,128)} %get-tuple-element.20), channel_id=1, source_target_pairs={{0,4},{4,0},{8,12},{12,8},{1,5},{5,1},{9,13},{13,9},{2,6},{6,2},{1... | collective-permute-start | bytes 3145736 | tf_op jit(solution)/shard_map/ppermute | solution.py:304
  14.0 4.5 %collective-permute-start.1 = (f32[128,2048]{1,0:T(8,128)}, f32[128,2048]{1,0:T(8,128)S(1)}, u32[]{:S(2)}, u32[]{:S(2)}) collective-permute-start(f32[128,2048]{1,0:T(8,128)} %get-tuple-element.23), channel_id=1, source_target_pairs={{0,8},{12,4},{1,9},{13,5},{2,10},{14,6},{3,11},{15,7},{16,24},{28,... | collective-permute-start | bytes 3145736 | tf_op jit(solution)/shard_map/ppermute | solution.py:305
  18.5 1.6 %collective-permute-start.2 = (f32[128,2048]{1,0:T(8,128)}, f32[128,2048]{1,0:T(8,128)}, u32[]{:S(2)}, u32[]{:S(2)}) collective-permute-start(f32[128,2048]{1,0:T(8,128)} %get-tuple-element.23), channel_id=1, source_target_pairs={{4,8},{8,4},{5,9},{9,5},{6,10},{10,6},{7,11},{11,7},{20,24},{24,20... | collective-permute-start | bytes 3145736 | tf_op jit(solution)/shard_map/ppermute | solution.py:306
  20.2 0.7 shard_map.65.refs_6_
  20.8 1.0 copy-done.8
  21.9 0.7 shard_map.66.refs_6_
  22.5 1.0 copy-done.6
  23.5 0.7 shard_map.67.refs_6_
  24.2 1.0 copy-done.4
  25.2 0.7 shard_map.68.refs_6_
  25.8 1.0 copy-done.2
  26.8 11.0 %collective-permute-done.got_ref.near_ref = f32[128,2048]{1,0:T(8,128)S(1)} collective-permute-done((f32[128,2048]{1,0:T(8,128)}, f32[128,2048]{1,0:T(8,128)S(1)}, u32[]{:S(2)}, u32[]{:S(2)}) %collective-permute-start) | collective-permute-done | bytes 1048608 | tf_op jit(solution)/shard_map/ppermute | solution.py:304
  37.9 0.9 shard_map.69
  38.8 0.7 copy-done.14
  39.5 0.7 copy-done.15
  40.2 2.4 %collective-permute-start.9 = (f32[32,2048]{1,0:T(8,128)}, f32[32,2048]{1,0:T(8,128)}, u32[]{:S(2)}, u32[]{:S(2)}) collective-permute-start(f32[32,2048]{1,0:T(8,128)} %get-tuple-element.31), channel_id=1, source_target_pairs={{0,4},{4,12},{12,8},{8,0},{1,5},{5,13},{13,9},{9,1},{2,6},{6,14},{... | collective-permute-start | bytes 786440 | tf_op jit(solution)/shard_map/ppermute | solution.py:311
  42.6 1.4 %collective-permute-start.7 = (f32[32,2048]{1,0:T(8,128)}, f32[32,2048]{1,0:T(8,128)S(1)}, u32[]{:S(2)}, u32[]{:S(2)}) collective-permute-start(f32[32,2048]{1,0:T(8,128)} %get-tuple-element.29), channel_id=1, source_target_pairs={{0,4},{4,12},{12,8},{8,0},{1,5},{5,13},{13,9},{9,1},{2,6},{6,14},{... | collective-permute-start | bytes 786440 | tf_op jit(solution)/shard_map/ppermute | solution.py:311
  44.1 1.6 %collective-permute-start.5 = (f32[32,2048]{1,0:T(8,128)}, f32[32,2048]{1,0:T(8,128)S(1)}, u32[]{:S(2)}, u32[]{:S(2)}) collective-permute-start(f32[32,2048]{1,0:T(8,128)} %copy-done.15), channel_id=1, source_target_pairs={{0,4},{4,12},{12,8},{8,0},{1,5},{5,13},{13,9},{9,1},{2,6},{6,14},{... | collective-permute-start | bytes 786440 | tf_op jit(solution)/shard_map/ppermute | solution.py:311
  45.7 14.7 %collective-permute-done.1.direct_ref = f32[128,2048]{1,0:T(8,128)S(1)} collective-permute-done((f32[128,2048]{1,0:T(8,128)}, f32[128,2048]{1,0:T(8,128)S(1)}, u32[]{:S(2)}, u32[]{:S(2)}) %collective-permute-start.1) | collective-permute-done | bytes 1048608 | tf_op jit(solution)/shard_map/ppermute | solution.py:305
  60.4 3.4 %collective-permute-start.3 = (f32[32,2048]{1,0:T(8,128)}, f32[32,2048]{1,0:T(8,128)S(1)}, u32[]{:S(2)}, u32[]{:S(2)}) collective-permute-start(f32[32,2048]{1,0:T(8,128)} %copy-done.14), channel_id=1, source_target_pairs={{0,4},{4,12},{12,8},{8,0},{1,5},{5,13},{13,9},{9,1},{2,6},{6,14},{... | collective-permute-start | bytes 786440 | tf_op jit(solution)/shard_map/ppermute | solution.py:311
  63.8 8.4 %collective-permute-done.9.last_ref = f32[32,2048]{1,0:T(8,128)} collective-permute-done((f32[32,2048]{1,0:T(8,128)}, f32[32,2048]{1,0:T(8,128)}, u32[]{:S(2)}, u32[]{:S(2)}) %collective-permute-start.9) | collective-permute-done | bytes 262176 | tf_op jit(solution)/shard_map/ppermute | solution.py:311
  72.2 1.8 %shard_map.73.refs_0_ = f32[32,2048]{1,0:T(8,128)} custom-call(f32[128,2048]{1,0:T(8,128)S(1)} %copy-done.1, f32[128,2048]{1,0:T(8,128)S(1)} %collective-permute-done.got_ref.near_ref, f32[128,2048]{1,0:T(8,128)S(1)} %collective-permute-done.1.direct_ref, f32[128,2048]{1,0:T(8,128)} %collective-permute-done.2.cross_ref, ...), custom_call_target="tpu_custom_call" | custom-call | flops 65536 | tf_op jit(solution)/shard_map/pallas_call | solution.py:162
  74.0 1.5 %collective-permute-start.10 = (f32[32,2048]{1,0:T(8,128)}, f32[32,2048]{1,0:T(8,128)}, u32[]{:S(2)}, u32[]{:S(2)}) collective-permute-start(f32[32,2048]{1,0:T(8,128)} %shard_map.73.refs_0_), channel_id=1, source_target_pairs={{0,2},{2,0},{1,3},{3,1},{4,6},{6,4},{5,7},{7,5},{8,10},{10,8},{9,1... | collective-permute-start | bytes 786440 | tf_op jit(solution)/shard_map/ppermute | solution.py:314
  75.5 2.2 %collective-permute-done.7.last_ref = f32[32,2048]{1,0:T(8,128)S(1)} collective-permute-done((f32[32,2048]{1,0:T(8,128)}, f32[32,2048]{1,0:T(8,128)S(1)}, u32[]{:S(2)}, u32[]{:S(2)}) %collective-permute-start.7) | collective-permute-done | bytes 262176 | tf_op jit(solution)/shard_map/ppermute | solution.py:311
  77.7 1.7 %shard_map.72.refs_0_ = f32[32,2048]{1,0:T(8,128)} custom-call(f32[128,2048]{1,0:T(8,128)S(1)} %copy-done.1, f32[128,2048]{1,0:T(8,128)S(1)} %collective-permute-done.got_ref.near_ref, f32[128,2048]{1,0:T(8,128)S(1)} %collective-permute-done.1.direct_ref, f32[128,2048]{1,0:T(8,128)} %collective-permute-done.2.cross_ref, ...), custom_call_target="tpu_custom_call" | custom-call | flops 65536 | tf_op jit(solution)/shard_map/pallas_call | solution.py:162
  79.4 1.5 %collective-permute-start.8 = (f32[32,2048]{1,0:T(8,128)}, f32[32,2048]{1,0:T(8,128)}, u32[]{:S(2)}, u32[]{:S(2)}) collective-permute-start(f32[32,2048]{1,0:T(8,128)} %shard_map.72.refs_0_), channel_id=1, source_target_pairs={{0,2},{2,0},{1,3},{3,1},{4,6},{6,4},{5,7},{7,5},{8,10},{10,8},{9,1... | collective-permute-start | bytes 786440 | tf_op jit(solution)/shard_map/ppermute | solution.py:314
  80.9 0.6 fusion.3
  81.6 1.7 %collective-permute-done.5.last_ref = f32[32,2048]{1,0:T(8,128)S(1)} collective-permute-done((f32[32,2048]{1,0:T(8,128)}, f32[32,2048]{1,0:T(8,128)S(1)}, u32[]{:S(2)}, u32[]{:S(2)}) %collective-permute-start.5) | collective-permute-done | bytes 262176 | tf_op jit(solution)/shard_map/ppermute | solution.py:311
  83.3 1.7 %shard_map.71.refs_0_ = f32[32,2048]{1,0:T(8,128)} custom-call(f32[128,2048]{1,0:T(8,128)S(1)} %copy-done.1, f32[128,2048]{1,0:T(8,128)S(1)} %collective-permute-done.got_ref.near_ref, f32[128,2048]{1,0:T(8,128)S(1)} %collective-permute-done.1.direct_ref, f32[128,2048]{1,0:T(8,128)} %collective-permute-done.2.cross_ref, ...), custom_call_target="tpu_custom_call" | custom-call | flops 65536 | tf_op jit(solution)/shard_map/pallas_call | solution.py:162
  85.0 1.5 %collective-permute-start.6 = (f32[32,2048]{1,0:T(8,128)}, f32[32,2048]{1,0:T(8,128)}, u32[]{:S(2)}, u32[]{:S(2)}) collective-permute-start(f32[32,2048]{1,0:T(8,128)} %shard_map.71.refs_0_), channel_id=1, source_target_pairs={{0,2},{2,0},{1,3},{3,1},{4,6},{6,4},{5,7},{7,5},{8,10},{10,8},{9,1... | collective-permute-start | bytes 786440 | tf_op jit(solution)/shard_map/ppermute | solution.py:314
  86.5 1.2 %collective-permute-done.3.last_ref = f32[32,2048]{1,0:T(8,128)S(1)} collective-permute-done((f32[32,2048]{1,0:T(8,128)}, f32[32,2048]{1,0:T(8,128)S(1)}, u32[]{:S(2)}, u32[]{:S(2)}) %collective-permute-start.3) | collective-permute-done | bytes 262176 | tf_op jit(solution)/shard_map/ppermute | solution.py:311
  87.8 1.7 %shard_map.70.refs_0_ = f32[32,2048]{1,0:T(8,128)} custom-call(f32[128,2048]{1,0:T(8,128)S(1)} %copy-done.1, f32[128,2048]{1,0:T(8,128)S(1)} %collective-permute-done.got_ref.near_ref, f32[128,2048]{1,0:T(8,128)S(1)} %collective-permute-done.1.direct_ref, f32[128,2048]{1,0:T(8,128)} %collective-permute-done.2.cross_ref, ...), custom_call_target="tpu_custom_call" | custom-call | flops 65536 | tf_op jit(solution)/shard_map/pallas_call | solution.py:162
  89.5 1.5 %collective-permute-start.4 = (f32[32,2048]{1,0:T(8,128)}, f32[32,2048]{1,0:T(8,128)S(1)}, u32[]{:S(2)}, u32[]{:S(2)}) collective-permute-start(f32[32,2048]{1,0:T(8,128)} %shard_map.70.refs_0_), channel_id=1, source_target_pairs={{0,2},{2,0},{1,3},{3,1},{4,6},{6,4},{5,7},{7,5},{8,10},{10,8},{9,1... | collective-permute-start | bytes 786440 | tf_op jit(solution)/shard_map/ppermute | solution.py:314
  91.1 1.2 %copy-done.9 = f32[4,32,2048]{2,1,0:T(8,128)S(1)} copy-done((f32[4,32,2048]{2,1,0:T(8,128)S(1)}, f32[4,32,2048]{2,1,0:T(8,128)}, u32[]{:S(2)}) %copy-start.9) | copy-done | bytes 1048600
  92.4 2.2 %shard_map.74.refs_7_ = f32[4,2048]{1,0:T(4,128)S(1)} custom-call(f32[32,2048]{1,0:T(8,128)} %shard_map.73.refs_0_, f32[32,2048]{1,0:T(8,128)} %collective-permute-done.10.refs_1_, f32[4,2048]{1,0:T(4,128)S(1)} %reshape.129.refs_2_, f32[32,128]{1,0:T(8,128)S(1)} %copy-done.13, bf16[256,256]{1,0:T(8,128)(2,1)S(1)} %copy-done.10, ...), custom_call_target="tpu_custom_call" | custom-call | flops 201326592 | bytes 1572864 | tf_op jit(solution)/shard_map/pallas_call | solution.py:266
  94.6 1.2 %copy-done.7 = f32[4,32,2048]{2,1,0:T(8,128)S(1)} copy-done((f32[4,32,2048]{2,1,0:T(8,128)S(1)}, f32[4,32,2048]{2,1,0:T(8,128)}, u32[]{:S(2)}) %copy-start.7) | copy-done | bytes 1048600
  95.8 2.2 %shard_map.75.refs_7_ = f32[4,2048]{1,0:T(4,128)S(1)} custom-call(f32[32,2048]{1,0:T(8,128)} %shard_map.72.refs_0_, f32[32,2048]{1,0:T(8,128)} %collective-permute-done.8.refs_1_, f32[4,2048]{1,0:T(4,128)S(1)} %reshape.129.refs_2_, f32[32,128]{1,0:T(8,128)S(1)} %copy-done.13, bf16[256,256]{1,0:T(8,128)(2,1)S(1)} %copy-done.10, ...), custom_call_target="tpu_custom_call" | custom-call | flops 201326592 | bytes 1572864 | tf_op jit(solution)/shard_map/pallas_call | solution.py:266
  98.1 1.2 %copy-done.5 = f32[4,32,2048]{2,1,0:T(8,128)S(1)} copy-done((f32[4,32,2048]{2,1,0:T(8,128)S(1)}, f32[4,32,2048]{2,1,0:T(8,128)}, u32[]{:S(2)}) %copy-start.5) | copy-done | bytes 1048600
  99.3 2.2 %shard_map.76.refs_7_ = f32[4,2048]{1,0:T(4,128)S(1)} custom-call(f32[32,2048]{1,0:T(8,128)} %shard_map.71.refs_0_, f32[32,2048]{1,0:T(8,128)} %collective-permute-done.6.refs_1_, f32[4,2048]{1,0:T(4,128)S(1)} %reshape.129.refs_2_, f32[32,128]{1,0:T(8,128)S(1)} %copy-done.13, bf16[256,256]{1,0:T(8,128)(2,1)S(1)} %copy-done.10, ...), custom_call_target="tpu_custom_call" | custom-call | flops 201326592 | bytes 1572864 | tf_op jit(solution)/shard_map/pallas_call | solution.py:266
  101.6 1.2 %copy-done.3 = f32[4,32,2048]{2,1,0:T(8,128)S(1)} copy-done((f32[4,32,2048]{2,1,0:T(8,128)S(1)}, f32[4,32,2048]{2,1,0:T(8,128)}, u32[]{:S(2)}) %copy-start.3) | copy-done | bytes 1048600
  102.8 2.2 %shard_map.77 = f32[4,2048]{1,0:T(4,128)S(1)} custom-call(f32[32,2048]{1,0:T(8,128)} %shard_map.70.refs_0_, f32[32,2048]{1,0:T(8,128)S(1)} %collective-permute-done.4.refs_1_, f32[4,2048]{1,0:T(4,128)S(1)} %reshape.129.refs_2_, f32[32,128]{1,0:T(8,128)S(1)} %copy-done.13, bf16[256,256]{1,0:T(8,128)(2,1)S(1)} %copy-done.10, bf16[256,256]{1,0:T(8,128)(2,1)S(1)} %copy-done.11, ...), custom_call_target="tpu_custom_call" | custom-call | flops 201326592 | bytes 1572864 | tf_op jit(solution)/shard_map/pallas_call | solution.py:266
  105.1 1.2 %collective-permute-done.11 = f32[4,2048]{1,0:T(4,128)S(1)} collective-permute-done((f32[4,2048]{1,0:T(4,128)S(1)}, f32[4,2048]{1,0:T(4,128)S(1)}, u32[]{:S(2)}, u32[]{:S(2)}) %collective-permute-start.11) | collective-permute-done | bytes 32800 | tf_op jit(solution)/shard_map/ppermute | solution.py:294
  106.3 3.9 %collective-permute-done.12 = f32[4,2048]{1,0:T(4,128)S(1)} collective-permute-done((f32[4,2048]{1,0:T(4,128)S(1)}, f32[4,2048]{1,0:T(4,128)S(1)}, u32[]{:S(2)}, u32[]{:S(2)}) %collective-permute-start.12) | collective-permute-done | bytes 32800 | tf_op jit(solution)/shard_map/ppermute | solution.py:294
  110.3 1.2 %collective-permute-start.13 = (f32[4,2048]{1,0:T(4,128)S(1)}, f32[4,2048]{1,0:T(4,128)S(1)}, u32[]{:S(2)}, u32[]{:S(2)}) collective-permute-start(f32[4,2048]{1,0:T(4,128)S(1)} %add.82), channel_id=1, source_target_pairs={{0,8},{4,12},{8,0},{12,4},{1,9},{5,13},{9,1},{13,5},{2,10},{6,14},... | collective-permute-start | bytes 98312 | tf_op jit(solution)/shard_map/ppermute | solution.py:294
  111.5 3.7 %collective-permute-done.13 = f32[4,2048]{1,0:T(4,128)S(1)} collective-permute-done((f32[4,2048]{1,0:T(4,128)S(1)}, f32[4,2048]{1,0:T(4,128)S(1)}, u32[]{:S(2)}, u32[]{:S(2)}) %collective-permute-start.13) | collective-permute-done | bytes 32800 | tf_op jit(solution)/shard_map/ppermute | solution.py:294
  115.2 0.1 copy.8
  115.4 0.8 mul.70
  (37 shorter events, 0.3 us)
Async XLA Ops:
  0.0 20.2 %copy-start = (f32[2,2,1,128,2048]{4,3,2,1,0:T(8,128)S(1)}, f32[2,2,1,128,2048]{4,3,2,1,0:T(8,128)}, u32[]{:S(2)}) copy-start(f32[2,2,1,128,2048]{4,3,2,1,0:T(8,128)} %param.8) | copy-start | bytes 12582916
  10.9 27.0 %collective-permute-start = (f32[128,2048]{1,0:T(8,128)}, f32[128,2048]{1,0:T(8,128)S(1)}, u32[]{:S(2)}, u32[]{:S(2)}) collective-permute-start(f32[128,2048]{1,0:T(8,128)} %get-tuple-element.20), channel_id=1, source_target_pairs={{0,4},{4,0},{8,12},{12,8},{1,5},{5,1},{9,13},{13,9},{2,6},{6,2},{1... | collective-permute-start | bytes 3145736 | tf_op jit(solution)/shard_map/ppermute | solution.py:304
  14.0 46.4 %collective-permute-start.1 = (f32[128,2048]{1,0:T(8,128)}, f32[128,2048]{1,0:T(8,128)S(1)}, u32[]{:S(2)}, u32[]{:S(2)}) collective-permute-start(f32[128,2048]{1,0:T(8,128)} %get-tuple-element.23), channel_id=1, source_target_pairs={{0,8},{12,4},{1,9},{13,5},{2,10},{14,6},{3,11},{15,7},{16,24},{28,... | collective-permute-start | bytes 3145736 | tf_op jit(solution)/shard_map/ppermute | solution.py:305
  18.5 45.2 %collective-permute-start.2 = (f32[128,2048]{1,0:T(8,128)}, f32[128,2048]{1,0:T(8,128)}, u32[]{:S(2)}, u32[]{:S(2)}) collective-permute-start(f32[128,2048]{1,0:T(8,128)} %get-tuple-element.23), channel_id=1, source_target_pairs={{4,8},{8,4},{5,9},{9,5},{6,10},{10,6},{7,11},{11,7},{20,24},{24,20... | collective-permute-start | bytes 3145736 | tf_op jit(solution)/shard_map/ppermute | solution.py:306
  20.8 1.0 copy-start.8
  22.5 1.0 copy-start.6
  23.5 14.3 %copy-start.12 = (f32[128,2048]{1,0:T(8,128)S(1)}, f32[128,2048]{1,0:T(8,128)}, u32[]{:S(2)}) copy-start(f32[128,2048]{1,0:T(8,128)} %get-tuple-element.24.own_ref) | copy-start | bytes 3145732
  24.2 1.0 copy-start.4
  25.2 47.0 %copy-start.1 = (f32[128,2048]{1,0:T(8,128)S(1)}, f32[128,2048]{1,0:T(8,128)}, u32[]{:S(2)}) copy-start(f32[128,2048]{1,0:T(8,128)} %get-tuple-element.19.own_ref) | copy-start | bytes 3145732
  25.8 1.0 copy-start.2
  38.8 0.7 copy-start.14
  39.5 0.7 copy-start.15
  40.2 31.9 %collective-permute-start.9 = (f32[32,2048]{1,0:T(8,128)}, f32[32,2048]{1,0:T(8,128)}, u32[]{:S(2)}, u32[]{:S(2)}) collective-permute-start(f32[32,2048]{1,0:T(8,128)} %get-tuple-element.31), channel_id=1, source_target_pairs={{0,4},{4,12},{12,8},{8,0},{1,5},{5,13},{13,9},{9,1},{2,6},{6,14},{... | collective-permute-start | bytes 786440 | tf_op jit(solution)/shard_map/ppermute | solution.py:311
  42.6 35.1 %collective-permute-start.7 = (f32[32,2048]{1,0:T(8,128)}, f32[32,2048]{1,0:T(8,128)S(1)}, u32[]{:S(2)}, u32[]{:S(2)}) collective-permute-start(f32[32,2048]{1,0:T(8,128)} %get-tuple-element.29), channel_id=1, source_target_pairs={{0,4},{4,12},{12,8},{8,0},{1,5},{5,13},{13,9},{9,1},{2,6},{6,14},{... | collective-permute-start | bytes 786440 | tf_op jit(solution)/shard_map/ppermute | solution.py:311
  44.1 39.2 %collective-permute-start.5 = (f32[32,2048]{1,0:T(8,128)}, f32[32,2048]{1,0:T(8,128)S(1)}, u32[]{:S(2)}, u32[]{:S(2)}) collective-permute-start(f32[32,2048]{1,0:T(8,128)} %copy-done.15), channel_id=1, source_target_pairs={{0,4},{4,12},{12,8},{8,0},{1,5},{5,13},{13,9},{9,1},{2,6},{6,14},{... | collective-permute-start | bytes 786440 | tf_op jit(solution)/shard_map/ppermute | solution.py:311
  60.4 27.4 %collective-permute-start.3 = (f32[32,2048]{1,0:T(8,128)}, f32[32,2048]{1,0:T(8,128)S(1)}, u32[]{:S(2)}, u32[]{:S(2)}) collective-permute-start(f32[32,2048]{1,0:T(8,128)} %copy-done.14), channel_id=1, source_target_pairs={{0,4},{4,12},{12,8},{8,0},{1,5},{5,13},{13,9},{9,1},{2,6},{6,14},{... | collective-permute-start | bytes 786440 | tf_op jit(solution)/shard_map/ppermute | solution.py:311
  74.0 17.1 %collective-permute-start.10 = (f32[32,2048]{1,0:T(8,128)}, f32[32,2048]{1,0:T(8,128)}, u32[]{:S(2)}, u32[]{:S(2)}) collective-permute-start(f32[32,2048]{1,0:T(8,128)} %shard_map.73.refs_0_), channel_id=1, source_target_pairs={{0,2},{2,0},{1,3},{3,1},{4,6},{6,4},{5,7},{7,5},{8,10},{10,8},{9,1... | collective-permute-start | bytes 786440 | tf_op jit(solution)/shard_map/ppermute | solution.py:314
  79.4 15.2 %collective-permute-start.8 = (f32[32,2048]{1,0:T(8,128)}, f32[32,2048]{1,0:T(8,128)}, u32[]{:S(2)}, u32[]{:S(2)}) collective-permute-start(f32[32,2048]{1,0:T(8,128)} %shard_map.72.refs_0_), channel_id=1, source_target_pairs={{0,2},{2,0},{1,3},{3,1},{4,6},{6,4},{5,7},{7,5},{8,10},{10,8},{9,1... | collective-permute-start | bytes 786440 | tf_op jit(solution)/shard_map/ppermute | solution.py:314
  81.5 9.6 %copy-start.10 = (bf16[256,256]{1,0:T(8,128)(2,1)S(1)}, bf16[256,256]{1,0:T(8,128)(2,1)}, u32[]{:S(2)}) copy-start(bf16[256,256]{1,0:T(8,128)(2,1)} %constant.49.clone.refs_4_) | copy-start | bytes 393220
  81.5 9.6 %copy-start.11 = (bf16[256,256]{1,0:T(8,128)(2,1)S(1)}, bf16[256,256]{1,0:T(8,128)(2,1)}, u32[]{:S(2)}) copy-start(bf16[256,256]{1,0:T(8,128)(2,1)} %constant.50.clone.refs_5_) | copy-start | bytes 393220
  81.6 9.6 %copy-start.13 = (f32[32,128]{1,0:T(8,128)S(1)}, f32[32,128]{1,0:T(8,128)}, u32[]{:S(2)}) copy-start(f32[32,128]{1,0:T(8,128)} %constant.48.clone.refs_3_) | copy-start | bytes 49156
  85.0 13.1 %collective-permute-start.6 = (f32[32,2048]{1,0:T(8,128)}, f32[32,2048]{1,0:T(8,128)}, u32[]{:S(2)}, u32[]{:S(2)}) collective-permute-start(f32[32,2048]{1,0:T(8,128)} %shard_map.71.refs_0_), channel_id=1, source_target_pairs={{0,2},{2,0},{1,3},{3,1},{4,6},{6,4},{5,7},{7,5},{8,10},{10,8},{9,1... | collective-permute-start | bytes 786440 | tf_op jit(solution)/shard_map/ppermute | solution.py:314
  89.5 12.1 %collective-permute-start.4 = (f32[32,2048]{1,0:T(8,128)}, f32[32,2048]{1,0:T(8,128)S(1)}, u32[]{:S(2)}, u32[]{:S(2)}) collective-permute-start(f32[32,2048]{1,0:T(8,128)} %shard_map.70.refs_0_), channel_id=1, source_target_pairs={{0,2},{2,0},{1,3},{3,1},{4,6},{6,4},{5,7},{7,5},{8,10},{10,8},{9,1... | collective-permute-start | bytes 786440 | tf_op jit(solution)/shard_map/ppermute | solution.py:314
  91.1 1.2 %copy-start.9 = (f32[4,32,2048]{2,1,0:T(8,128)S(1)}, f32[4,32,2048]{2,1,0:T(8,128)}, u32[]{:S(2)}) copy-start(f32[4,32,2048]{2,1,0:T(8,128)} %copy-done.8) | copy-start | bytes 3145732
  94.6 1.2 %copy-start.7 = (f32[4,32,2048]{2,1,0:T(8,128)S(1)}, f32[4,32,2048]{2,1,0:T(8,128)}, u32[]{:S(2)}) copy-start(f32[4,32,2048]{2,1,0:T(8,128)} %copy-done.6) | copy-start | bytes 3145732
  98.1 1.2 %copy-start.5 = (f32[4,32,2048]{2,1,0:T(8,128)S(1)}, f32[4,32,2048]{2,1,0:T(8,128)}, u32[]{:S(2)}) copy-start(f32[4,32,2048]{2,1,0:T(8,128)} %copy-done.4) | copy-start | bytes 3145732
  101.6 1.2 %copy-start.3 = (f32[4,32,2048]{2,1,0:T(8,128)S(1)}, f32[4,32,2048]{2,1,0:T(8,128)}, u32[]{:S(2)}) copy-start(f32[4,32,2048]{2,1,0:T(8,128)} %copy-done.2) | copy-start | bytes 3145732
  105.0 1.3 %collective-permute-start.11 = (f32[4,2048]{1,0:T(4,128)S(1)}, f32[4,2048]{1,0:T(4,128)S(1)}, u32[]{:S(2)}, u32[]{:S(2)}) collective-permute-start(f32[4,2048]{1,0:T(4,128)S(1)} %shard_map.77), channel_id=1, source_target_pairs={{0,1},{1,0},{2,3},{3,2},{4,5},{5,4},{6,7},{7,6},{8,9},{9,8},{10,11... | collective-permute-start | bytes 98312 | tf_op jit(solution)/shard_map/ppermute | solution.py:294
  106.3 4.0 %collective-permute-start.12 = (f32[4,2048]{1,0:T(4,128)S(1)}, f32[4,2048]{1,0:T(4,128)S(1)}, u32[]{:S(2)}, u32[]{:S(2)}) collective-permute-start(f32[4,2048]{1,0:T(4,128)S(1)} %add.81), channel_id=1, source_target_pairs={{0,4},{4,0},{8,12},{12,8},{1,5},{5,1},{9,13},{13,9},{2,6},{6,2},{1... | collective-permute-start | bytes 98312 | tf_op jit(solution)/shard_map/ppermute | solution.py:294
  110.3 4.9 %collective-permute-start.13 = (f32[4,2048]{1,0:T(4,128)S(1)}, f32[4,2048]{1,0:T(4,128)S(1)}, u32[]{:S(2)}, u32[]{:S(2)}) collective-permute-start(f32[4,2048]{1,0:T(4,128)S(1)} %add.82), channel_id=1, source_target_pairs={{0,8},{4,12},{8,0},{12,4},{1,9},{5,13},{9,1},{13,5},{2,10},{6,14},... | collective-permute-start | bytes 98312 | tf_op jit(solution)/shard_map/ppermute | solution.py:294

commit v3 on v2

--- a/solution.py
+++ b/solution.py
@@ -133,51 +133,17 @@
     return out
 
 
-def pass_kernel(cuts, own_ref, got_ref, *outs):
-    top = 0
-    keep = jnp.where(at_end(), 0.0, 1.0)
-    for k, rows in enumerate(cuts):
-        at = slice(top, top + rows)
-        outs[k][...] = own_ref[at, :] + got_ref[at, :] * keep
-        top += rows
-
-
-def pass_on(own, got, cuts):
-    return pl.pallas_call(
-        functools.partial(pass_kernel, cuts),
-        out_shape=[jax.ShapeDtypeStruct((k, own.shape[1]), jnp.float32) for k in cuts],
-        compiler_params=pltpu.CompilerParams(vmem_limit_bytes=16 * MIB),
-        cost_estimate=pl.CostEstimate(flops=own.size, bytes_accessed=0, transcendentals=0),
-    )(own, got)
-
-
-def final_kernel(own_ref, near_ref, direct_ref, cross_ref, last_ref, sum_ref):
-    keep = jnp.where(at_end(), 1.0, 0.0)
-    sum_ref[...] = (own_ref[...] + near_ref[...] * keep) + (direct_ref[...] + cross_ref[...]) + last_ref[...]
-
-
-def final_hint(top, own, near, direct, cross, last):
-    cut = pl.BlockSpec(last.shape, lambda i: (top // last.shape[0], 0))
-    whole = pl.BlockSpec(last.shape, lambda i: (0, 0))
-    return pl.pallas_call(
-        final_kernel,
-        grid=(1,),
-        in_specs=[cut, cut, cut, cut, whole],
-        out_specs=whole,
-        out_shape=jax.ShapeDtypeStruct(last.shape, jnp.float32),
-        compiler_params=pltpu.CompilerParams(vmem_limit_bytes=16 * MIB),
-        cost_estimate=pl.CostEstimate(flops=last.size, bytes_accessed=0, transcendentals=0),
-    )(own, near, direct, cross, last)
-
-
 def swap_kernel(radix, in_ref, out_ref, stage):
     groups, rows = in_ref.shape[:2]
-    for k in range(radix):
-        lanes = slice(k * LANES, (k + 1) * LANES)
-        stage[lanes, :] = in_ref[:, :, lanes].reshape(groups * rows, LANES).T
-    for r in range(radix):
-        picked = stage[pl.ds(r, LANES, stride=radix), :].T
-        out_ref[:, :, r * LANES : (r + 1) * LANES] = picked.reshape(groups, rows, LANES)
+    some = stage.shape[2] // rows
+    for n in range(groups // some):
+        at = slice(n * some, (n + 1) * some)
+        for k in range(radix):
+            lanes = slice(k * LANES, (k + 1) * LANES)
+            stage[n, lanes, :] = in_ref[at, :, lanes].reshape(some * rows, LANES).T
+        for r in range(radix):
+            picked = stage[n, pl.ds(r, LANES, stride=radix), :].T
+            out_ref[at, :, r * LANES : (r + 1) * LANES] = picked.reshape(some, rows, LANES)
 
 
 def swap_digits(cipher, offset, rows):
@@ -189,7 +155,7 @@
         in_specs=[pl.BlockSpec((4, rows, points), lambda i: (0, offset // rows, 0))],
         out_specs=pl.BlockSpec((4, rows, points), lambda i: (0, 0, 0)),
         out_shape=jax.ShapeDtypeStruct((4, rows, points), jnp.float32),
-        scratch_shapes=[pltpu.VMEM((points, 4 * rows), jnp.float32)],
+        scratch_shapes=[pltpu.VMEM((max(1, 4 * rows // LANES), points, min(4 * rows, LANES)), jnp.float32)],
         compiler_params=pltpu.CompilerParams(vmem_limit_bytes=16 * MIB),
         cost_estimate=pl.CostEstimate(flops=0, bytes_accessed=32 * rows * points, transcendentals=0),
     )(cipher)
@@ -259,59 +225,64 @@
             out_ref[2 * c + 1 : 2 * c + 2, lanes] = total_ref[2 * c + 1 : 2 * c + 2, lanes] + imag
 
 
-def transform_products(hints, first, twist, tables, cipher, part, total):
+def transform_products(hints, tables, cipher, total):
     rows, points = hints[0].shape
     radix = points // LANES
-    whole = lambda a: pl.BlockSpec(a.shape, lambda i: (0,) * a.ndim)
     return pl.pallas_call(
         functools.partial(transform_kernel, len(hints), radix, rows),
-        grid=(1,),
-        in_specs=[whole(h) for h in hints]
-        + [whole(first), whole(twist), whole(tables[0]), whole(tables[1])]
-        + [pl.BlockSpec((4, rows, points), lambda i: (0, part, 0)), whole(total)],
-        out_specs=pl.BlockSpec((4, points), lambda i: (0, 0)),
         out_shape=jax.ShapeDtypeStruct((4, points), jnp.float32),
         scratch_shapes=[pltpu.VMEM((radix * rows, 2 * LANES), jnp.float32)],
-        compiler_params=pltpu.CompilerParams(vmem_limit_bytes=32 * MIB),
+        compiler_params=pltpu.CompilerParams(vmem_limit_bytes=16 * MIB),
         cost_estimate=pl.CostEstimate(
-            flops=6 * radix * rows * 256 * 256, bytes_accessed=24 * rows * points, transcendentals=0
+            flops=6 * radix * rows * 256 * 256, bytes_accessed=0, transcendentals=0
         ),
-    )(*hints, first, twist, *tables, cipher, total)
+    )(*hints, *tables, cipher, total)
 
 
 def xor_pairs(size, step):
     return [(i, i ^ step) for i in range(size)]
 
 
-def sum_over(x, axes):
-    for axis in axes:
-        size = lax.axis_size(axis)
-        if size & (size - 1):
-            x = lax.psum(x, axis)
-            continue
-        step = 1
-        while step < size:
-            x = x + lax.ppermute(x, axis, xor_pairs(size, step))
-            step *= 2
+def sum_over(x, axis):
+    size = lax.axis_size(axis)
+    if size == 4:
+        near, far, across = [lax.ppermute(x, axis, xor_pairs(size, step)) for step in (1, 2, 3)]
+        return (x + near) + (far + across)
+    if size & (size - 1):
+        return lax.psum(x, axis)
+    step = 1
+    while step < size:
+        x = x + lax.ppermute(x, axis, xor_pairs(size, step))
+        step *= 2
     return x
 
 
-def line_parts(lwe, database, cipher, cuts):
+def line_total(lwe, database, cipher, tables, total, cuts):
     own = cipher.shape[1]
-    (first,), (far_mid,), (kept,), (later,) = line_hint(
-        lwe, database, [(0, 3), (1, 1), (3, 2), (2, 0)], [[own]] * 4
-    )
+    tops = [sum(cuts[:k]) for k in range(len(cuts))]
+    ats = [slice(top, top + rows) for top, rows in zip(tops, cuts)]
+    (first,), far_mid = line_hint(lwe, database, [(0, 3), (1, 1)], [[own], cuts])
     near = lax.ppermute(first, "col", NEIGHBOURS)
-    direct = lax.ppermute(far_mid, "col", END_TO_FAR_MIDDLE)
-    cross = lax.ppermute(far_mid, "col", CROSS)
-    cipher = lax.optimization_barrier((cipher, first))[0]
-    tops = [sum(cuts[:k]) for k in range(len(cuts))]
+    cross = [lax.ppermute(jnp.concatenate(far_mid, axis=0), "col", CROSS)]
+    direct = [lax.ppermute(far_mid[0], "col", END_TO_FAR_MIDDLE)]
+    lwe, database, cipher = lax.optimization_barrier((lwe, database, cipher, first))[:3]
+    (kept,), (later,) = line_hint(lwe, database, [(3, 2), (2, 0)], [[own]] * 2)
     swapped = [swap_digits(cipher, top, rows) for top, rows in zip(tops, cuts)]
-    near, swapped = lax.optimization_barrier((near, swapped))
-    last = [lax.ppermute(x, "col", ROUND) for x in pass_on(later, near, cuts)]
-    for k, top in enumerate(tops):
-        mine = final_hint(top, kept, near, direct, cross, last[k])
-        yield [mine, lax.ppermute(mine, "row", SWAP)], swapped[k]
+    near, kept, swapped, far_mid = lax.optimization_barrier((near, kept, swapped, far_mid))
+    end = at_end()
+    passed = later + jnp.where(end, 0.0, near)
+    last = [lax.ppermute(passed[at], "col", ROUND) for at in ats]
+    direct += [lax.ppermute(x, "col", END_TO_FAR_MIDDLE) for x in far_mid[1:]]
+    sums, mine = [total], None
+    for k, at in enumerate(ats):
+        got = last[k]
+        if k >= 2:
+            got, sums[k - 1] = lax.optimization_barrier((got, sums[k - 1]))
+        if k >= 1:
+            got, mine = lax.optimization_barrier((got, mine))
+        mine = (kept[at] + jnp.where(end, near[at], 0.0)) + (cross[0][at] + direct[k]) + got
+        sums.append(transform_products([mine, lax.ppermute(mine, "row", SWAP)], tables, swapped[k], sums[k]))
+    return sums[-1]
 
 
 def body(parts, database, lwe_matrix, secret_ct):
@@ -333,18 +304,18 @@
     table = np.block([[np.cos(small), -np.sin(small)], [np.sin(small), np.cos(small)]]).astype(np.float32)
     high = table.astype(jnp.bfloat16)
     low = (table - high.astype(np.float32)).astype(jnp.bfloat16)
-    tables = (jnp.asarray(high), jnp.asarray(low))
+    tables = (first, twist, jnp.asarray(high), jnp.asarray(low))
 
     lwe = lwe_matrix[:, 0, :]
     cipher = secret_ct.reshape(4, own, points)
     total = jnp.zeros((4, points), jnp.float32)
     if col_count == 4 and row_count == 2 and own == LANES and points % 512 == 0:
-        cuts = [32, 32, 32, 32]
-        for hints, swapped in line_parts(lwe, database, cipher, cuts):
-            total = transform_products(hints, first, twist, tables, swapped, 0, total)
+        cuts = [64, 32, 32]
+        total = line_total(lwe, database, cipher, tables, total, cuts)
     else:
         swapped = cipher.reshape(4, own, LANES, radix).swapaxes(2, 3).reshape(4, own, points)
         partial = partial_hint(lwe, database, col_count, parts)
+        block = own // parts
         for k in range(parts):
             mine = lax.psum_scatter(partial[k], "col", scatter_dimension=0, tiled=True)
             if row_count == 2:
@@ -352,8 +323,8 @@
             else:
                 gathered = lax.all_gather(mine, "row")
                 hints = [gathered[b] for b in range(row_count)]
-            total = transform_products(hints, first, twist, tables, swapped, k, total)
-    total = sum_over(total, ("limb", "col"))
+            total = transform_products(hints, tables, swapped[:, k * block : (k + 1) * block], total)
+    total = sum_over(sum_over(total, "limb"), "col")
     scale = 1.0 / (math.sqrt(degree) * math.sqrt(2 * lwe_matrix.shape[2]))
     total = total.reshape(4, radix, LANES).swapaxes(1, 2).reshape(2, 2, points)
     return total * scale

time: 117 us -> 107 us (0.915)
  local copies, waits for them, and re-layouts: 11.2 us -> 2.14 us
  waiting for transfers between devices: 48.1 us -> 39.6 us
  other arithmetic: 0.68 us -> 9.13 us
  Pallas kernels: 30.4 us -> 24.2 us
  starting transfers between devices: 25.5 us -> 31.3 us
    unnamed x33 -> x15, local copies, waits for them, and re-layouts: 10.3 us -> 0.33 us
    pallas_call x5 -> x0, Pallas kernels: 7.97 us -> none  [the longest x4 7.03 us: final_hint(): pl.pallas_call(final_kernel, grid=(1,), in_specs=[cut, cut, cut, cut, who...]
    ppermute x3 -> x1, waiting for transfers between devices: 8.8 us -> 1.19 us  [sum_over(): x = x + lax.ppermute(x, axis, xor_pairs(size, step))]
    ppermute x11 -> x14, starting transfers between devices: 24.1 us -> 31.2 us  [the longest x2 9.27 us: line_total(): direct += [lax.ppermute(x, 'col', END_TO_FAR_MIDDLE) for x in far_mid[1:]]]
    add x0 -> x4, other arithmetic: none -> 6.15 us  [the longest x3 4.81 us: line_total(): kept[at] + jnp.where(end, near[at], 0.0) + (cross[0][at] + direct[k]) + got]
    pallas_call x1 -> x2, Pallas kernels: 10.9 us -> 16.5 us  [line_hint(): pl.pallas_call(functools.partial(line_hint_kernel, roles, cuts, tile), in...]
    pallas_call x4 -> x3, Pallas kernels: 8.88 us -> 5.07 us  [transform_products(): pl.pallas_call(functools.partial(transform_kernel, len(hints), radix, row...]
    concatenate x0 -> x1, other arithmetic: none -> 2.31 us  [line_total(): cross = [lax.ppermute(jnp.concatenate(far_mid, axis=0), 'col', CROSS)]]
  transfers between devices with their start and end apart: 14 -> 15, of which waited for: 9 -> 8; matrix products, arithmetic and copies ran while one was open for 1% -> 9% of each run, Pallas kernels for 15% -> 14%
where the time goes in v3:
time: 107 us
  waiting for transfers between devices  39.6 us (37%)
  starting transfers between devices  31.3 us (29%)
  Pallas kernels  24.2 us (23%)
  other arithmetic  9.13 us (9%)
  local copies, waits for them, and re-layouts  2.14 us (2%)
    ppermute x3, waiting for transfers between devices, line_total(): last = [lax.ppermute(passed[at], 'col', ROUND) for at in ats]  25.2 us
    pallas_call x2, Pallas kernels, line_hint(): pl.pallas_call(functools.partial(line_hint_kernel, roles, cuts, tile), in...  16.5 us
    ppermute x2, starting transfers between devices, line_total(): direct += [lax.ppermute(x, 'col', END_TO_FAR_MIDDLE) for x in far_mid[1:]]  9.27 us
    ppermute x3, waiting for transfers between devices, line_total(): lax.ppermute(mine, 'row', SWAP)  6.84 us
    ppermute x1, starting transfers between devices, line_total(): direct = [lax.ppermute(far_mid[0], 'col', END_TO_FAR_MIDDLE)]  5.34 us
    pallas_call x3, Pallas kernels, transform_products(): pl.pallas_call(functools.partial(transform_kernel, len(hints), radix, row...  5.07 us
    add x3, other arithmetic, line_total(): kept[at] + jnp.where(end, near[at], 0.0) + (cross[0][at] + direct[k]) + got  4.81 us
    ppermute x3, starting transfers between devices, line_total(): lax.ppermute(mine, 'row', SWAP)  4.17 us
  transfers between devices with their start and end apart: 15, of which 8 were waited for; matrix products, arithmetic and copies ran while one was open for 9% of the time, Pallas kernels for 14%

profile of v3, /device:TPU:0, one launch (start us, length us, event | category | flops | bytes accessed | tf_op | source)
XLA Modules:
  0.0 106.5 jit_solution(9312019985864950346)
XLA Ops:
  0.0 8.3 %shard_map.64 = (f32[128,2048]{1,0:T(8,128)}, f32[64,2048]{1,0:T(8,128)}, f32[32,2048]{1,0:T(8,128)}, f32[32,2048]{1,0:T(8,128)}) custom-call(bf16[2048,512]{1,0:T(8,128)(2,1)} %bitcast.11, bf16[2048,2048]{1,0:T(8,128)(2,1)} %data_ref.2), custom_call_target="tpu_custom_call" | custom-call | flops 2147483648 | bytes 8388608 | tf_op jit(solution)/shard_map/pallas_call | solution.py:113
  8.4 3.1 %collective-permute-start = (f32[128,2048]{1,0:T(8,128)}, f32[128,2048]{1,0:T(8,128)}, u32[]{:S(2)}, u32[]{:S(2)}) collective-permute-start(f32[128,2048]{1,0:T(8,128)} %get-tuple-element.24), channel_id=1, source_target_pairs={{0,4},{4,0},{8,12},{12,8},{1,5},{5,1},{9,13},{13,9},{2,6},{6,2},{1... | collective-permute-start | bytes 3145736 | tf_op jit(solution)/shard_map/ppermute | solution.py:265
  11.4 5.3 %collective-permute-start.4 = (f32[64,2048]{1,0:T(8,128)}, f32[64,2048]{1,0:T(8,128)}, u32[]{:S(2)}, u32[]{:S(2)}) collective-permute-start(f32[64,2048]{1,0:T(8,128)} %get-tuple-element.29), channel_id=1, source_target_pairs={{0,8},{12,4},{1,9},{13,5},{2,10},{14,6},{3,11},{15,7},{16,24},{28,... | collective-permute-start | bytes 1572872 | tf_op jit(solution)/shard_map/ppermute | solution.py:267
  16.8 2.3 %pad_maximum_fusion = f32[128,2048]{1,0:T(8,128)} fusion(f32[32,2048]{1,0:T(8,128)} %get-tuple-element.34, f32[32,2048]{1,0:T(8,128)} %get-tuple-element.38, f32[64,2048]{1,0:T(8,128)} %get-tuple-element.29), kind=kLoop, calls=%fused_computation | loop fusion | flops 524288 | bytes 2097152 | tf_op jit(solution)/shard_map/concatenate | solution.py:266
  19.1 1.6 %collective-permute-start.1 = (f32[128,2048]{1,0:T(8,128)}, f32[128,2048]{1,0:T(8,128)}, u32[]{:S(2)}, u32[]{:S(2)}) collective-permute-start(f32[128,2048]{1,0:T(8,128)} %pad_maximum_fusion), channel_id=1, source_target_pairs={{4,8},{8,4},{5,9},{9,5},{6,10},{10,6},{7,11},{11,7},{20,24},{24,20... | collective-permute-start | bytes 3145736 | tf_op jit(solution)/shard_map/ppermute | solution.py:266
  20.7 1.3 %shard_map.66.refs_6_ = f32[4,64,2048]{2,1,0:T(8,128)S(1)} custom-call(f32[4,128,2048]{2,1,0:T(8,128)S(1)} %bitcast.8), custom_call_target="tpu_custom_call" | custom-call | bytes 4194304 | tf_op jit(solution)/shard_map/pallas_call | solution.py:152
  22.0 0.7 shard_map.67.refs_6_
  22.7 0.7 shard_map.68.refs_6_
  23.4 0.3 copy-done.1
  23.7 8.2 %shard_map.65 = (f32[128,2048]{1,0:T(8,128)}, f32[128,2048]{1,0:T(8,128)}) custom-call(bf16[2048,512]{1,0:T(8,128)(2,1)} %bitcast.12, bf16[2048,2048]{1,0:T(8,128)(2,1)} %data_ref.2), custom_call_target="tpu_custom_call" | custom-call | flops 2147483648 | bytes 8388608 | tf_op jit(solution)/shard_map/pallas_call | solution.py:113
  31.9 3.5 %collective-permute-done = f32[128,2048]{1,0:T(8,128)} collective-permute-done((f32[128,2048]{1,0:T(8,128)}, f32[128,2048]{1,0:T(8,128)}, u32[]{:S(2)}, u32[]{:S(2)}) %collective-permute-start) | collective-permute-done | bytes 1048608 | tf_op jit(solution)/shard_map/ppermute | solution.py:265
  35.3 1.3 %select_add_fusion = f32[128,2048]{1,0:T(8,128)S(1)} fusion(f32[128,2048]{1,0:T(8,128)} %get-tuple-element.35, f32[128,2048]{1,0:T(8,128)} %collective-permute-done, pred[]{:T(512)S(6)} %or.3), kind=kLoop, calls=%fused_computation.1 | loop fusion | flops 524288 | bytes 3145729 | tf_op jit(solution)/shard_map/add | solution.py:273
  36.7 0.0 copy-start.3
  36.7 0.0 copy-start.4
  36.7 0.0 copy-start.5
  36.7 2.8 %collective-permute-start.5 = (f32[64,2048]{1,0:T(8,128)S(1)}, f32[64,2048]{1,0:T(8,128)S(1)}, u32[]{:S(2)}, u32[]{:S(2)}) collective-permute-start(f32[64,2048]{1,0:T(8,128)S(1)} %slice.51), channel_id=1, source_target_pairs={{0,4},{4,12},{12,8},{8,0},{1,5},{5,13},{13,9},{9,1},{2,6},{6,14},{... | collective-permute-start | bytes 1572872 | tf_op jit(solution)/shard_map/ppermute | solution.py:274
  39.6 0.6 fusion.9
  40.2 0.8 fusion.12
  41.0 1.1 %collective-permute-start.8 = (f32[32,2048]{1,0:T(8,128)}, f32[32,2048]{1,0:T(8,128)}, u32[]{:S(2)}, u32[]{:S(2)}) collective-permute-start(f32[32,2048]{1,0:T(8,128)} %get-tuple-element.43), channel_id=1, source_target_pairs={{0,4},{4,12},{12,8},{8,0},{1,5},{5,13},{13,9},{9,1},{2,6},{6,14},{... | collective-permute-start | bytes 786440 | tf_op jit(solution)/shard_map/ppermute | solution.py:274
  42.2 4.4 %collective-permute-start.7 = (f32[32,2048]{1,0:T(8,128)}, f32[32,2048]{1,0:T(8,128)}, u32[]{:S(2)}, u32[]{:S(2)}) collective-permute-start(f32[32,2048]{1,0:T(8,128)} %get-tuple-element.38), channel_id=1, source_target_pairs={{0,8},{12,4},{1,9},{13,5},{2,10},{14,6},{3,11},{15,7},{16,24},{28,... | collective-permute-start | bytes 786440 | tf_op jit(solution)/shard_map/ppermute | solution.py:275
  46.6 0.0 collective-permute-done.4
  46.6 0.0 collective-permute-done.1
  46.6 25.2 %collective-permute-done.5 = f32[64,2048]{1,0:T(8,128)S(1)} collective-permute-done((f32[64,2048]{1,0:T(8,128)S(1)}, f32[64,2048]{1,0:T(8,128)S(1)}, u32[]{:S(2)}, u32[]{:S(2)}) %collective-permute-start.5) | collective-permute-done | bytes 524320 | tf_op jit(solution)/shard_map/ppermute | solution.py:274
  71.8 2.3 %fusion.1.refs_0_ = f32[64,2048]{1,0:T(8,128)} fusion(f32[64,2048]{1,0:T(8,128)S(1)} %collective-permute-done.5, f32[64,2048]{1,0:T(8,128)} %collective-permute-done.4, f32[128,2048]{1,0:T(8,128)} %collective-permute-done.1, f32[128,2048]{1,0:T(8,128)} %collective-permute-done, f32[128,2048]{1,0:T(8,128)S(1)} %copy-done.6, pred[]{:T(512)S(6)} %or.3), kind=kLoop, calls=%fused_computation.4 | loop fusion | flops 655360 | bytes 3145729 | tf_op jit(solution)/shard_map/add | solution.py:283
  74.1 1.5 %collective-permute-start.6 = (f32[64,2048]{1,0:T(8,128)}, f32[64,2048]{1,0:T(8,128)}, u32[]{:S(2)}, u32[]{:S(2)}) collective-permute-start(f32[64,2048]{1,0:T(8,128)} %fusion.1.refs_0_), channel_id=1, source_target_pairs={{0,2},{2,0},{1,3},{3,1},{4,6},{6,4},{5,7},{7,5},{8,10},{10,8},{9,1... | collective-permute-start | bytes 1572872 | tf_op jit(solution)/shard_map/ppermute | solution.py:284
  75.7 0.2 collective-permute-start.3
  75.9 4.9 %collective-permute-start.2 = (f32[32,2048]{1,0:T(8,128)}, f32[32,2048]{1,0:T(8,128)S(1)}, u32[]{:S(2)}, u32[]{:S(2)}) collective-permute-start(f32[32,2048]{1,0:T(8,128)} %get-tuple-element.34), channel_id=1, source_target_pairs={{0,8},{12,4},{1,9},{13,5},{2,10},{14,6},{3,11},{15,7},{16,24},{28,... | collective-permute-start | bytes 786440 | tf_op jit(solution)/shard_map/ppermute | solution.py:275
  80.8 0.0 collective-permute-done.8
  80.8 1.3 %fusion.3.refs_0_ = f32[32,2048]{1,0:T(8,128)S(1)} fusion(f32[32,2048]{1,0:T(8,128)} %collective-permute-done.8, f32[32,2048]{1,0:T(8,128)} %collective-permute-done.7, f32[128,2048]{1,0:T(8,128)} %collective-permute-done.1, f32[128,2048]{1,0:T(8,128)} %collective-permute-done, f32[128,2048]{1,0:T(8,128)} %get-tuple-element.32, pred[]{:T(512)S(6)} %or.3), kind=kLoop, calls=%fused_computation.7 | loop fusion | flops 327680 | bytes 1572865 | tf_op jit(solution)/shard_map/add | solution.py:283
  82.1 1.1 %collective-permute-start.10 = (f32[32,2048]{1,0:T(8,128)S(1)}, f32[32,2048]{1,0:T(8,128)S(1)}, u32[]{:S(2)}, u32[]{:S(2)}) collective-permute-start(f32[32,2048]{1,0:T(8,128)S(1)} %fusion.3.refs_0_), channel_id=1, source_target_pairs={{0,2},{2,0},{1,3},{3,1},{4,6},{6,4},{5,7},{7,5},{8,10},{10,8},{9,1... | collective-permute-start | bytes 786440 | tf_op jit(solution)/shard_map/ppermute | solution.py:284
  83.3 3.2 %collective-permute-done.6.refs_1_ = f32[64,2048]{1,0:T(8,128)} collective-permute-done((f32[64,2048]{1,0:T(8,128)}, f32[64,2048]{1,0:T(8,128)}, u32[]{:S(2)}, u32[]{:S(2)}) %collective-permute-start.6) | collective-permute-done | bytes 524320 | tf_op jit(solution)/shard_map/ppermute | solution.py:284
  86.5 2.7 %shard_map.69.refs_7_ = f32[4,2048]{1,0:T(4,128)S(1)} custom-call(f32[64,2048]{1,0:T(8,128)} %fusion.1.refs_0_, f32[64,2048]{1,0:T(8,128)} %collective-permute-done.6.refs_1_, f32[4,2048]{1,0:T(4,128)S(1)} %reshape.129.refs_2_, f32[32,128]{1,0:T(8,128)S(1)} %copy-done.5, bf16[256,256]{1,0:T(8,128)(2,1)S(1)} %copy-done.3, bf16[256,256]{1,0:T(8,128)(2,1)S(1)} %copy-done.4, ...), custom_call_target="tpu_custom_call" | custom-call | flops 402653184 | tf_op jit(solution)/shard_map/pallas_call | solution.py:231
  89.1 0.0 collective-permute-done.2
  89.2 1.2 %fusion.5.refs_0_ = f32[32,2048]{1,0:T(8,128)S(1)} fusion(f32[32,2048]{1,0:T(8,128)S(1)} %collective-permute-done.3, f32[32,2048]{1,0:T(8,128)S(1)} %collective-permute-done.2, f32[128,2048]{1,0:T(8,128)} %collective-permute-done.1, f32[128,2048]{1,0:T(8,128)} %collective-permute-done, f32[128,2048]{1,0:T(8,128)} %get-tuple-element.32, pred[]{:T(512)S(6)} %or.3), kind=kLoop, calls=%fused_computation.10 | loop fusion | flops 327680 | bytes 1572865 | tf_op jit(solution)/shard_map/add | solution.py:283
  90.3 1.6 %collective-permute-start.9 = (f32[32,2048]{1,0:T(8,128)S(1)}, f32[32,2048]{1,0:T(8,128)S(1)}, u32[]{:S(2)}, u32[]{:S(2)}) collective-permute-start(f32[32,2048]{1,0:T(8,128)S(1)} %fusion.5.refs_0_), channel_id=1, source_target_pairs={{0,2},{2,0},{1,3},{3,1},{4,6},{6,4},{5,7},{7,5},{8,10},{10,8},{9,1... | collective-permute-start | bytes 786440 | tf_op jit(solution)/shard_map/ppermute | solution.py:284
  91.9 1.2 %shard_map.70.refs_7_ = f32[4,2048]{1,0:T(4,128)S(1)} custom-call(f32[32,2048]{1,0:T(8,128)S(1)} %fusion.3.refs_0_, f32[32,2048]{1,0:T(8,128)S(1)} %collective-permute-done.10.refs_1_, f32[4,2048]{1,0:T(4,128)S(1)} %reshape.129.refs_2_, f32[32,128]{1,0:T(8,128)S(1)} %copy-done.5, bf16[256,256]{1,0:T(8,128)(2,1)S(1)} %copy-done.3, ...), custom_call_target="tpu_custom_call" | custom-call | flops 201326592 | tf_op jit(solution)/shard_map/pallas_call | solution.py:231
  93.1 3.7 %collective-permute-done.9.refs_1_ = f32[32,2048]{1,0:T(8,128)S(1)} collective-permute-done((f32[32,2048]{1,0:T(8,128)S(1)}, f32[32,2048]{1,0:T(8,128)S(1)}, u32[]{:S(2)}, u32[]{:S(2)}) %collective-permute-start.9) | collective-permute-done | bytes 262176 | tf_op jit(solution)/shard_map/ppermute | solution.py:284
  96.8 1.2 %shard_map.71 = f32[4,2048]{1,0:T(4,128)S(1)} custom-call(f32[32,2048]{1,0:T(8,128)S(1)} %fusion.5.refs_0_, f32[32,2048]{1,0:T(8,128)S(1)} %collective-permute-done.9.refs_1_, f32[4,2048]{1,0:T(4,128)S(1)} %reshape.129.refs_2_, f32[32,128]{1,0:T(8,128)S(1)} %copy-done.5, bf16[256,256]{1,0:T(8,128)(2,1)S(1)} %copy-done.3, bf16[256,256]{1,0:T(8,128)(2,1)S(1)} %copy-done.4, ...), custom_call_target="tpu_custom_call" | custom-call | flops 201326592 | tf_op jit(solution)/shard_map/pallas_call | solution.py:231
  98.0 0.1 collective-permute-start.11
  98.1 1.2 %collective-permute-done.11 = f32[4,2048]{1,0:T(4,128)S(1)} collective-permute-done((f32[4,2048]{1,0:T(4,128)S(1)}, f32[4,2048]{1,0:T(4,128)S(1)}, u32[]{:S(2)}, u32[]{:S(2)}) %collective-permute-start.11) | collective-permute-done | bytes 32800 | tf_op jit(solution)/shard_map/ppermute | solution.py:255
  99.3 0.1 collective-permute-start.13
  99.4 2.1 %collective-permute-start.14 = (f32[4,2048]{1,0:T(4,128)S(1)}, f32[4,2048]{1,0:T(4,128)S(1)}, u32[]{:S(2)}, u32[]{:S(2)}) collective-permute-start(f32[4,2048]{1,0:T(4,128)S(1)} %add.136), channel_id=1, source_target_pairs={{0,12},{4,8},{8,4},{12,0},{1,13},{5,9},{9,5},{13,1},{2,14},{6,10},... | collective-permute-start | bytes 98312 | tf_op jit(solution)/shard_map/ppermute | solution.py:249
  101.5 1.4 %collective-permute-start.12 = (f32[4,2048]{1,0:T(4,128)S(1)}, f32[4,2048]{1,0:T(4,128)S(1)}, u32[]{:S(2)}, u32[]{:S(2)}) collective-permute-start(f32[4,2048]{1,0:T(4,128)S(1)} %add.136), channel_id=1, source_target_pairs={{0,4},{4,0},{8,12},{12,8},{1,5},{5,1},{9,13},{13,9},{2,6},{6,2},{1... | collective-permute-start | bytes 98312 | tf_op jit(solution)/shard_map/ppermute | solution.py:249
  102.8 2.0 %collective-permute-done.13 = f32[4,2048]{1,0:T(4,128)S(1)} collective-permute-done((f32[4,2048]{1,0:T(4,128)S(1)}, f32[4,2048]{1,0:T(4,128)S(1)}, u32[]{:S(2)}, u32[]{:S(2)}) %collective-permute-start.13) | collective-permute-done | bytes 32800 | tf_op jit(solution)/shard_map/ppermute | solution.py:249
  104.8 0.4 collective-permute-done.14
  105.2 0.4 collective-permute-done.12
  105.6 0.1 copy.8
  105.8 0.8 mul.70
  (21 shorter events, 0.2 us)
Async XLA Ops:
  0.0 20.7 %copy-start = (f32[2,2,1,128,2048]{4,3,2,1,0:T(8,128)S(1)}, f32[2,2,1,128,2048]{4,3,2,1,0:T(8,128)}, u32[]{:S(2)}) copy-start(f32[2,2,1,128,2048]{4,3,2,1,0:T(8,128)} %param.8) | copy-start | bytes 12582916
  8.4 27.0 %collective-permute-start = (f32[128,2048]{1,0:T(8,128)}, f32[128,2048]{1,0:T(8,128)}, u32[]{:S(2)}, u32[]{:S(2)}) collective-permute-start(f32[128,2048]{1,0:T(8,128)} %get-tuple-element.24), channel_id=1, source_target_pairs={{0,4},{4,0},{8,12},{12,8},{1,5},{5,1},{9,13},{13,9},{2,6},{6,2},{1... | collective-permute-start | bytes 3145736 | tf_op jit(solution)/shard_map/ppermute | solution.py:265
  11.4 35.2 %collective-permute-start.4 = (f32[64,2048]{1,0:T(8,128)}, f32[64,2048]{1,0:T(8,128)}, u32[]{:S(2)}, u32[]{:S(2)}) collective-permute-start(f32[64,2048]{1,0:T(8,128)} %get-tuple-element.29), channel_id=1, source_target_pairs={{0,8},{12,4},{1,9},{13,5},{2,10},{14,6},{3,11},{15,7},{16,24},{28,... | collective-permute-start | bytes 1572872 | tf_op jit(solution)/shard_map/ppermute | solution.py:267
  19.1 27.5 %collective-permute-start.1 = (f32[128,2048]{1,0:T(8,128)}, f32[128,2048]{1,0:T(8,128)}, u32[]{:S(2)}, u32[]{:S(2)}) collective-permute-start(f32[128,2048]{1,0:T(8,128)} %pad_maximum_fusion), channel_id=1, source_target_pairs={{4,8},{8,4},{5,9},{9,5},{6,10},{10,6},{7,11},{11,7},{20,24},{24,20... | collective-permute-start | bytes 3145736 | tf_op jit(solution)/shard_map/ppermute | solution.py:266
  22.7 1.0 copy-start.1
  31.8 40.0 %copy-start.6 = (f32[128,2048]{1,0:T(8,128)S(1)}, f32[128,2048]{1,0:T(8,128)}, u32[]{:S(2)}) copy-start(f32[128,2048]{1,0:T(8,128)} %get-tuple-element.32) | copy-start | bytes 3145732
  36.7 49.8 %copy-start.3 = (bf16[256,256]{1,0:T(8,128)(2,1)S(1)}, bf16[256,256]{1,0:T(8,128)(2,1)}, u32[]{:S(2)}) copy-start(bf16[256,256]{1,0:T(8,128)(2,1)} %constant.58.clone.refs_4_) | copy-start | bytes 393220
  36.7 49.8 %copy-start.4 = (bf16[256,256]{1,0:T(8,128)(2,1)S(1)}, bf16[256,256]{1,0:T(8,128)(2,1)}, u32[]{:S(2)}) copy-start(bf16[256,256]{1,0:T(8,128)(2,1)} %constant.59.clone.refs_5_) | copy-start | bytes 393220
  36.7 49.8 %copy-start.5 = (f32[32,128]{1,0:T(8,128)S(1)}, f32[32,128]{1,0:T(8,128)}, u32[]{:S(2)}) copy-start(f32[32,128]{1,0:T(8,128)} %constant.57.clone.refs_3_) | copy-start | bytes 49156
  36.7 35.1 %collective-permute-start.5 = (f32[64,2048]{1,0:T(8,128)S(1)}, f32[64,2048]{1,0:T(8,128)S(1)}, u32[]{:S(2)}, u32[]{:S(2)}) collective-permute-start(f32[64,2048]{1,0:T(8,128)S(1)} %slice.51), channel_id=1, source_target_pairs={{0,4},{4,12},{12,8},{8,0},{1,5},{5,13},{13,9},{9,1},{2,6},{6,14},{... | collective-permute-start | bytes 1572872 | tf_op jit(solution)/shard_map/ppermute | solution.py:274
  41.0 39.8 %collective-permute-start.8 = (f32[32,2048]{1,0:T(8,128)}, f32[32,2048]{1,0:T(8,128)}, u32[]{:S(2)}, u32[]{:S(2)}) collective-permute-start(f32[32,2048]{1,0:T(8,128)} %get-tuple-element.43), channel_id=1, source_target_pairs={{0,4},{4,12},{12,8},{8,0},{1,5},{5,13},{13,9},{9,1},{2,6},{6,14},{... | collective-permute-start | bytes 786440 | tf_op jit(solution)/shard_map/ppermute | solution.py:274
  42.2 38.6 %collective-permute-start.7 = (f32[32,2048]{1,0:T(8,128)}, f32[32,2048]{1,0:T(8,128)}, u32[]{:S(2)}, u32[]{:S(2)}) collective-permute-start(f32[32,2048]{1,0:T(8,128)} %get-tuple-element.38), channel_id=1, source_target_pairs={{0,8},{12,4},{1,9},{13,5},{2,10},{14,6},{3,11},{15,7},{16,24},{28,... | collective-permute-start | bytes 786440 | tf_op jit(solution)/shard_map/ppermute | solution.py:275
  74.1 12.3 %collective-permute-start.6 = (f32[64,2048]{1,0:T(8,128)}, f32[64,2048]{1,0:T(8,128)}, u32[]{:S(2)}, u32[]{:S(2)}) collective-permute-start(f32[64,2048]{1,0:T(8,128)} %fusion.1.refs_0_), channel_id=1, source_target_pairs={{0,2},{2,0},{1,3},{3,1},{4,6},{6,4},{5,7},{7,5},{8,10},{10,8},{9,1... | collective-permute-start | bytes 1572872 | tf_op jit(solution)/shard_map/ppermute | solution.py:284
  75.7 16.2 %copy-start.2 = (f32[4,32,2048]{2,1,0:T(8,128)S(1)}, f32[4,32,2048]{2,1,0:T(8,128)}, u32[]{:S(2)}) copy-start(f32[4,32,2048]{2,1,0:T(8,128)} %copy-done.1) | copy-start | bytes 3145732
  75.7 13.4 %collective-permute-start.3 = (f32[32,2048]{1,0:T(8,128)}, f32[32,2048]{1,0:T(8,128)S(1)}, u32[]{:S(2)}, u32[]{:S(2)}) collective-permute-start(f32[32,2048]{1,0:T(8,128)} %get-tuple-element.44), channel_id=1, source_target_pairs={{0,4},{4,12},{12,8},{8,0},{1,5},{5,13},{13,9},{9,1},{2,6},{6,14},{... | collective-permute-start | bytes 786440 | tf_op jit(solution)/shard_map/ppermute | solution.py:274
  75.9 13.2 %collective-permute-start.2 = (f32[32,2048]{1,0:T(8,128)}, f32[32,2048]{1,0:T(8,128)S(1)}, u32[]{:S(2)}, u32[]{:S(2)}) collective-permute-start(f32[32,2048]{1,0:T(8,128)} %get-tuple-element.34), channel_id=1, source_target_pairs={{0,8},{12,4},{1,9},{13,5},{2,10},{14,6},{3,11},{15,7},{16,24},{28,... | collective-permute-start | bytes 786440 | tf_op jit(solution)/shard_map/ppermute | solution.py:275
  82.1 9.7 %collective-permute-start.10 = (f32[32,2048]{1,0:T(8,128)S(1)}, f32[32,2048]{1,0:T(8,128)S(1)}, u32[]{:S(2)}, u32[]{:S(2)}) collective-permute-start(f32[32,2048]{1,0:T(8,128)S(1)} %fusion.3.refs_0_), channel_id=1, source_target_pairs={{0,2},{2,0},{1,3},{3,1},{4,6},{6,4},{5,7},{7,5},{8,10},{10,8},{9,1... | collective-permute-start | bytes 786440 | tf_op jit(solution)/shard_map/ppermute | solution.py:284
  90.3 6.4 %collective-permute-start.9 = (f32[32,2048]{1,0:T(8,128)S(1)}, f32[32,2048]{1,0:T(8,128)S(1)}, u32[]{:S(2)}, u32[]{:S(2)}) collective-permute-start(f32[32,2048]{1,0:T(8,128)S(1)} %fusion.5.refs_0_), channel_id=1, source_target_pairs={{0,2},{2,0},{1,3},{3,1},{4,6},{6,4},{5,7},{7,5},{8,10},{10,8},{9,1... | collective-permute-start | bytes 786440 | tf_op jit(solution)/shard_map/ppermute | solution.py:284
  98.0 1.3 %collective-permute-start.11 = (f32[4,2048]{1,0:T(4,128)S(1)}, f32[4,2048]{1,0:T(4,128)S(1)}, u32[]{:S(2)}, u32[]{:S(2)}) collective-permute-start(f32[4,2048]{1,0:T(4,128)S(1)} %shard_map.71), channel_id=1, source_target_pairs={{0,1},{1,0},{2,3},{3,2},{4,5},{5,4},{6,7},{7,6},{8,9},{9,8},{10,11... | collective-permute-start | bytes 98312 | tf_op jit(solution)/shard_map/ppermute | solution.py:255
  99.3 5.5 %collective-permute-start.13 = (f32[4,2048]{1,0:T(4,128)S(1)}, f32[4,2048]{1,0:T(4,128)S(1)}, u32[]{:S(2)}, u32[]{:S(2)}) collective-permute-start(f32[4,2048]{1,0:T(4,128)S(1)} %add.136), channel_id=1, source_target_pairs={{0,8},{4,12},{8,0},{12,4},{1,9},{5,13},{9,1},{13,5},{2,10},{6,14},... | collective-permute-start | bytes 98312 | tf_op jit(solution)/shard_map/ppermute | solution.py:249
  99.4 5.9 %collective-permute-start.14 = (f32[4,2048]{1,0:T(4,128)S(1)}, f32[4,2048]{1,0:T(4,128)S(1)}, u32[]{:S(2)}, u32[]{:S(2)}) collective-permute-start(f32[4,2048]{1,0:T(4,128)S(1)} %add.136), channel_id=1, source_target_pairs={{0,12},{4,8},{8,4},{12,0},{1,13},{5,9},{9,5},{13,1},{2,14},{6,10},... | collective-permute-start | bytes 98312 | tf_op jit(solution)/shard_map/ppermute | solution.py:249
  101.5 4.1 %collective-permute-start.12 = (f32[4,2048]{1,0:T(4,128)S(1)}, f32[4,2048]{1,0:T(4,128)S(1)}, u32[]{:S(2)}, u32[]{:S(2)}) collective-permute-start(f32[4,2048]{1,0:T(4,128)S(1)} %add.136), channel_id=1, source_target_pairs={{0,4},{4,0},{8,12},{12,8},{1,5},{5,1},{9,13},{13,9},{2,6},{6,2},{1... | collective-permute-start | bytes 98312 | tf_op jit(solution)/shard_map/ppermute | solution.py:249

commit v4 on v3

--- a/solution.py
+++ b/solution.py
@@ -12,6 +12,7 @@
 LANES = 128
 MIB = 1 << 20
 SWAP = [(0, 1), (1, 0)]
+INWARD = [(0, 1), (3, 2)]
 NEIGHBOURS = [(0, 1), (1, 0), (2, 3), (3, 2)]
 END_TO_FAR_MIDDLE = [(0, 2), (3, 1)]
 CROSS = [(1, 2), (2, 1)]
@@ -73,39 +74,38 @@
 
 
 def line_hint_kernel(roles, cuts, tile, lwe_ref, data_ref, *rest):
-    outs = rest[: sum(len(c) for c in cuts)]
-    lwe_v, data_v, turned, lwe_sem, data_sem = rest[len(outs) :]
+    pieces = [(b, top, size) for b, c in enumerate(cuts) for top, size in c]
+    outs = rest[: len(pieces)]
+    lwe_v, data_v, turned, made, lwe_sem, data_sem, out_sem = rest[len(pieces) :]
     rows = data_ref.shape[0]
-    own = lwe_v.shape[2]
-    copies = []
-    for b, role in enumerate(roles):
-        at = pl.multiple_of(role_block(role) * own, own)
-        copies.append(pltpu.make_async_copy(lwe_ref.at[:, pl.ds(at, own)], lwe_v.at[b], lwe_sem.at[b]))
+    own = made.shape[0] // len(roles)
+    lwe_copy = pltpu.make_async_copy(lwe_ref, lwe_v, lwe_sem)
+    lwe_copy.start()
     tiles = []
     for i in range(rows // tile):
         at = slice(i * tile, (i + 1) * tile)
         tiles.append(pltpu.make_async_copy(data_ref.at[at, :], data_v.at[at, :], data_sem.at[i]))
-    for c in copies + tiles:
-        c.start()
-    for b, c in enumerate(copies):
-        c.wait()
-        turned[b * own : (b + 1) * own, :] = lwe_v[b].T
+        tiles[-1].start()
+    lwe_copy.wait()
+    for b, role in enumerate(roles):
+        at = pl.multiple_of(role_block(role) * own, own)
+        turned[b * own : (b + 1) * own, :] = lwe_v[:, pl.ds(at, own)].T
+    written = []
     for i, c in enumerate(tiles):
         c.wait()
         at = slice(i * tile, (i + 1) * tile)
-        res = lax.dot_general(
+        made[:, at] = lax.dot_general(
             turned[...], data_v[at, :], (((1,), (1,)), ((), ())), preferred_element_type=jnp.float32
         )
-        n = 0
-        for b in range(len(roles)):
-            top = b * own
-            for rows_k in cuts[b]:
-                outs[n][:, at] = res[top : top + rows_k, :]
-                top += rows_k
-                n += 1
-
-
-def line_hint(lwe, database, roles, cuts):
+        for n, (b, top, size) in enumerate(pieces):
+            source = made.at[b * own + top : b * own + top + size, at]
+            written.append(pltpu.make_async_copy(source, outs[n].at[:, at], out_sem.at[i * len(pieces) + n]))
+            written[-1].start()
+    for c in written:
+        c.wait()
+
+
+def line_hint(lwe, database, roles, cuts, limit):
     depth, columns = lwe.shape
     rows = database.shape[0]
     own = columns // 4
@@ -113,15 +113,18 @@
     flat = pl.pallas_call(
         functools.partial(line_hint_kernel, roles, cuts, tile),
         in_specs=[pl.BlockSpec(memory_space=pl.ANY)] * 2,
-        out_shape=[jax.ShapeDtypeStruct((k, rows), jnp.float32) for c in cuts for k in c],
+        out_shape=[jax.ShapeDtypeStruct((k, rows), jnp.float32) for c in cuts for _, k in c],
+        out_specs=[pl.BlockSpec(memory_space=pl.ANY)] * sum(len(c) for c in cuts),
         scratch_shapes=[
-            pltpu.VMEM((len(roles), depth, own), jnp.bfloat16),
+            pltpu.VMEM((depth, columns), jnp.bfloat16),
             pltpu.VMEM((rows, depth), jnp.bfloat16),
             pltpu.VMEM((len(roles) * own, depth), jnp.bfloat16),
-            pltpu.SemaphoreType.DMA((len(roles),)),
+            pltpu.VMEM((len(roles) * own, rows), jnp.float32),
+            pltpu.SemaphoreType.DMA,
             pltpu.SemaphoreType.DMA((rows // tile,)),
+            pltpu.SemaphoreType.DMA((rows // tile * sum(len(c) for c in cuts),)),
         ],
-        compiler_params=pltpu.CompilerParams(vmem_limit_bytes=56 * MIB),
+        compiler_params=pltpu.CompilerParams(vmem_limit_bytes=limit * MIB),
         cost_estimate=pl.CostEstimate(
             flops=2 * rows * depth * own * len(roles), bytes_accessed=2 * rows * depth, transcendentals=0
         ),
@@ -135,15 +138,15 @@
 
 def swap_kernel(radix, in_ref, out_ref, stage):
     groups, rows = in_ref.shape[:2]
-    some = stage.shape[2] // rows
-    for n in range(groups // some):
+    some = stage.shape[2] // groups
+    for n in range(rows // some):
         at = slice(n * some, (n + 1) * some)
         for k in range(radix):
             lanes = slice(k * LANES, (k + 1) * LANES)
-            stage[n, lanes, :] = in_ref[at, :, lanes].reshape(some * rows, LANES).T
+            stage[n, lanes, :] = in_ref[:, at, lanes].reshape(groups * some, LANES).T
         for r in range(radix):
             picked = stage[n, pl.ds(r, LANES, stride=radix), :].T
-            out_ref[at, :, r * LANES : (r + 1) * LANES] = picked.reshape(some, rows, LANES)
+            out_ref[:, at, r * LANES : (r + 1) * LANES] = picked.reshape(groups, some, LANES)
 
 
 def swap_digits(cipher, offset, rows):
@@ -155,7 +158,7 @@
         in_specs=[pl.BlockSpec((4, rows, points), lambda i: (0, offset // rows, 0))],
         out_specs=pl.BlockSpec((4, rows, points), lambda i: (0, 0, 0)),
         out_shape=jax.ShapeDtypeStruct((4, rows, points), jnp.float32),
-        scratch_shapes=[pltpu.VMEM((max(1, 4 * rows // LANES), points, min(4 * rows, LANES)), jnp.float32)],
+        scratch_shapes=[pltpu.VMEM((max(1, rows // 32), points, min(4 * rows, LANES)), jnp.float32)],
         compiler_params=pltpu.CompilerParams(vmem_limit_bytes=16 * MIB),
         cost_estimate=pl.CostEstimate(flops=0, bytes_accessed=32 * rows * points, transcendentals=0),
     )(cipher)
@@ -191,7 +194,9 @@
 
 def transform_kernel(blocks, radix, rows, *refs):
     hints = refs[:blocks]
-    first_ref, twist_ref, table_hi, table_lo, cipher_ref, total_ref, out_ref, stage = refs[blocks:]
+    first_ref, twist_ref, table_hi, table_lo, cipher_any, total_ref, out_ref, stage, cipher_ref, sem = refs[blocks:]
+    copy = pltpu.make_async_copy(cipher_any, cipher_ref, sem)
+    copy.start()
     for top in range(0, rows, 8):
         re, im = [], []
         for u in range(radix):
@@ -211,6 +216,7 @@
             at = slice(r * rows + top, r * rows + top + 8)
             stage[at, :LANES] = re[r] * c + im[r] * s
             stage[at, LANES:] = im[r] * c - re[r] * s
+    copy.wait()
     for r in range(radix):
         high, low = split_bf16(stage[r * rows : (r + 1) * rows, :])
         dot = functools.partial(jnp.dot, preferred_element_type=jnp.float32)
@@ -231,7 +237,13 @@
     return pl.pallas_call(
         functools.partial(transform_kernel, len(hints), radix, rows),
         out_shape=jax.ShapeDtypeStruct((4, points), jnp.float32),
-        scratch_shapes=[pltpu.VMEM((radix * rows, 2 * LANES), jnp.float32)],
+        in_specs=[pl.BlockSpec(memory_space=pltpu.VMEM)] * (len(hints) + 4)
+        + [pl.BlockSpec(memory_space=pl.ANY), pl.BlockSpec(memory_space=pltpu.VMEM)],
+        scratch_shapes=[
+            pltpu.VMEM((radix * rows, 2 * LANES), jnp.float32),
+            pltpu.VMEM((4, rows, points), jnp.float32),
+            pltpu.SemaphoreType.DMA,
+        ],
         compiler_params=pltpu.CompilerParams(vmem_limit_bytes=16 * MIB),
         cost_estimate=pl.CostEstimate(
             flops=6 * radix * rows * 256 * 256, bytes_accessed=0, transcendentals=0
@@ -257,32 +269,37 @@
     return x
 
 
-def line_total(lwe, database, cipher, tables, total, cuts):
+def line_total(lwe, database, cipher, tables, total):
     own = cipher.shape[1]
-    tops = [sum(cuts[:k]) for k in range(len(cuts))]
-    ats = [slice(top, top + rows) for top, rows in zip(tops, cuts)]
-    (first,), far_mid = line_hint(lwe, database, [(0, 3), (1, 1)], [[own], cuts])
+    q = own // 4
+    h = own - q
+    (first,), (far_mid, far_tail) = line_hint(lwe, database, [(0, 3), (1, 1)], [[(0, own)], [(0, h), (h, q)]], 56)
     near = lax.ppermute(first, "col", NEIGHBOURS)
-    cross = [lax.ppermute(jnp.concatenate(far_mid, axis=0), "col", CROSS)]
-    direct = [lax.ppermute(far_mid[0], "col", END_TO_FAR_MIDDLE)]
+    cross = lax.ppermute(far_mid, "col", CROSS)
+    direct = lax.ppermute(far_mid, "col", END_TO_FAR_MIDDLE)
     lwe, database, cipher = lax.optimization_barrier((lwe, database, cipher, first))[:3]
-    (kept,), (later,) = line_hint(lwe, database, [(3, 2), (2, 0)], [[own]] * 2)
-    swapped = [swap_digits(cipher, top, rows) for top, rows in zip(tops, cuts)]
-    near, kept, swapped, far_mid = lax.optimization_barrier((near, kept, swapped, far_mid))
+    (kept,), (later,) = line_hint(lwe, database, [(3, 2), (2, 0)], [[(0, own)]] * 2, 32)
+    cuts = [(0, 2 * q), (2 * q, q), (h, q)]
+    swapped = [swap_digits(cipher, top, rows) for top, rows in cuts]
+    near, kept, swapped = lax.optimization_barrier((near, kept, swapped))
     end = at_end()
-    passed = later + jnp.where(end, 0.0, near)
-    last = [lax.ppermute(passed[at], "col", ROUND) for at in ats]
-    direct += [lax.ppermute(x, "col", END_TO_FAR_MIDDLE) for x in far_mid[1:]]
-    sums, mine = [total], None
-    for k, at in enumerate(ats):
-        got = last[k]
-        if k >= 2:
-            got, sums[k - 1] = lax.optimization_barrier((got, sums[k - 1]))
-        if k >= 1:
-            got, mine = lax.optimization_barrier((got, mine))
-        mine = (kept[at] + jnp.where(end, near[at], 0.0)) + (cross[0][at] + direct[k]) + got
-        sums.append(transform_products([mine, lax.ppermute(mine, "row", SWAP)], tables, swapped[k], sums[k]))
-    return sums[-1]
+    round_a = lax.ppermute(later[: 2 * q] + jnp.where(end, 0.0, near[: 2 * q]), "col", ROUND)
+    spare = jnp.where(end, far_tail, later[h:] + near[h:])
+    piece = later[2 * q : h] + jnp.where(end, 0.0, near[2 * q : h])
+    round_b = lax.ppermute(jnp.concatenate([piece, spare], axis=0), "col", ROUND)
+    near_tail = lax.ppermute(later[h:], "col", INWARD)
+    far_sum = lax.ppermute(far_tail + round_b[q:], "col", CROSS)
+    base = kept + jnp.where(end, near, 0.0)
+    hint_a = base[: 2 * q] + (cross[: 2 * q] + direct[: 2 * q]) + round_a
+    waited, _ = lax.optimization_barrier((round_b, hint_a))
+    hint_b = base[2 * q : h] + (cross[2 * q :] + direct[2 * q :]) + waited[:q]
+    far_sum, _ = lax.optimization_barrier((far_sum, hint_b))
+    with_a = lambda t: transform_products([hint_a, lax.ppermute(hint_a, "row", SWAP)], tables, swapped[0], t)
+    hint_c = base[h:] + jnp.where(end, round_b[q:], 0.0) + (near_tail + far_sum)
+    total = with_a(total)
+    for hint, part in ((hint_b, swapped[1]), (hint_c, swapped[2])):
+        total = transform_products([hint, lax.ppermute(hint, "row", SWAP)], tables, part, total)
+    return total
 
 
 def body(parts, database, lwe_matrix, secret_ct):
@@ -310,8 +327,7 @@
     cipher = secret_ct.reshape(4, own, points)
     total = jnp.zeros((4, points), jnp.float32)
     if col_count == 4 and row_count == 2 and own == LANES and points % 512 == 0:
-        cuts = [64, 32, 32]
-        total = line_total(lwe, database, cipher, tables, total, cuts)
+        total = line_total(lwe, database, cipher, tables, total)
     else:
         swapped = cipher.reshape(4, own, LANES, radix).swapaxes(2, 3).reshape(4, own, points)
         partial = partial_hint(lwe, database, col_count, parts)

time: 107 us -> 106 us (level)
  starting transfers between devices: 31.3 us -> 25.6 us
  local copies, waits for them, and re-layouts: 2.14 us -> 5.72 us
  waiting for transfers between devices: 39.6 us -> 41.7 us
  Pallas kernels: 24.2 us -> 22.9 us
    ppermute x10 -> x9, starting transfers between devices: 24.6 us -> 18 us  [the longest x1 5.75 us: line_total(): direct = lax.ppermute(far_mid, 'col', END_TO_FAR_MIDDLE)]
    unnamed x15 -> x23, local copies, waits for them, and re-layouts: 0.33 us -> 4.78 us
    pallas_call x2, Pallas kernels: 16.5 us -> 12.2 us  [line_hint(): pl.pallas_call(functools.partial(line_hint_kernel, roles, cuts, tile), in...]
    pallas_call x3, Pallas kernels: 5.07 us -> 8.14 us  [transform_products(): pl.pallas_call(functools.partial(transform_kernel, len(hints), radix, row...]
    concatenate x1, other arithmetic: 2.31 us -> 0.04 us  [line_total(): jnp.concatenate([piece, spare], axis=0)]
    add x4 -> x7, other arithmetic: 6.15 us -> 8.27 us  [the longest x1 2.11 us: line_total(): hint_a = base[:2 * q] + (cross[:2 * q] + direct[:2 * q]) + round_a]
    ppermute x10 -> x9, waiting for transfers between devices: 32.1 us -> 33 us  [the longest x1 13 us: line_total(): lax.ppermute(later[:2 * q] + jnp.where(end, 0.0, near[:2 * q]), 'col', RO...]
  transfers between devices with their start and end apart: 15 -> 14, of which waited for: 8 -> 9; matrix products, arithmetic and copies ran while one was open for 9% -> 9% of each run, Pallas kernels for 14% -> 12%
where the time goes in v4:
time: 106 us; the launch traced here: 105 us
  waiting for transfers between devices  41.7 us (39%)
  starting transfers between devices  25.6 us (24%)
  Pallas kernels  22.9 us (22%)
  other arithmetic  8.99 us (8%)
  local copies, waits for them, and re-layouts  5.72 us (5%)
    ppermute x1, waiting for transfers between devices, line_total(): lax.ppermute(later[:2 * q] + jnp.where(end, 0.0, near[:2 * q]), 'col', RO...  13 us
    pallas_call x2, Pallas kernels, line_hint(): pl.pallas_call(functools.partial(line_hint_kernel, roles, cuts, tile), in...  12.2 us
    pallas_call x3, Pallas kernels, transform_products(): pl.pallas_call(functools.partial(transform_kernel, len(hints), radix, row...  8.14 us
    ppermute x1, waiting for transfers between devices, line_total(): lax.ppermute(jnp.concatenate([piece, spare], axis=0), 'col', ROUND)  7.54 us
    ppermute x1, waiting for transfers between devices, line_total(): direct = lax.ppermute(far_mid, 'col', END_TO_FAR_MIDDLE)  6.91 us
    ppermute x1, starting transfers between devices, line_total(): direct = lax.ppermute(far_mid, 'col', END_TO_FAR_MIDDLE)  5.75 us
    ppermute x2, waiting for transfers between devices, line_total(): lax.ppermute(hint, 'row', SWAP)  5.55 us
    unnamed x23, local copies, waits for them, and re-layouts  4.78 us
  transfers between devices with their start and end apart: 14, of which 9 were waited for; matrix products, arithmetic and copies ran while one was open for 9% of the time, Pallas kernels for 12%

profile of v4, /device:TPU:0, one launch (start us, length us, event | category | flops | bytes accessed | tf_op | source)
XLA Modules:
  0.0 105.2 jit_solution(14292356961321279224)
XLA Ops:
  0.0 7.9 %shard_map.64 = (f32[128,2048]{1,0:T(8,128)}, f32[96,2048]{1,0:T(8,128)}, f32[32,2048]{1,0:T(8,128)}) custom-call(bf16[2048,512]{1,0:T(8,128)(2,1)} %bitcast.11, bf16[2048,2048]{1,0:T(8,128)(2,1)} %data_ref.2), custom_call_target="tpu_custom_call" | custom-call | flops 2147483648 | bytes 8388608 | tf_op jit(solution)/shard_map/pallas_call | solution.py:113
  7.9 3.1 %collective-permute-start = (f32[128,2048]{1,0:T(8,128)}, f32[128,2048]{1,0:T(8,128)}, u32[]{:S(2)}, u32[]{:S(2)}) collective-permute-start(f32[128,2048]{1,0:T(8,128)} %get-tuple-element.20), channel_id=1, source_target_pairs={{0,4},{4,0},{8,12},{12,8},{1,5},{5,1},{9,13},{13,9},{2,6},{6,2},{1... | collective-permute-start | bytes 3145736 | tf_op jit(solution)/shard_map/ppermute | solution.py:277
  11.0 1.6 %collective-permute-start.4 = (f32[96,2048]{1,0:T(8,128)}, f32[96,2048]{1,0:T(8,128)}, u32[]{:S(2)}, u32[]{:S(2)}) collective-permute-start(f32[96,2048]{1,0:T(8,128)} %get-tuple-element.29), channel_id=1, source_target_pairs={{4,8},{8,4},{5,9},{9,5},{6,10},{10,6},{7,11},{11,7},{20,24},{24,20... | collective-permute-start | bytes 2359304 | tf_op jit(solution)/shard_map/ppermute | solution.py:278
  12.5 5.7 %collective-permute-start.5 = (f32[96,2048]{1,0:T(8,128)}, f32[96,2048]{1,0:T(8,128)}, u32[]{:S(2)}, u32[]{:S(2)}) collective-permute-start(f32[96,2048]{1,0:T(8,128)} %get-tuple-element.29), channel_id=1, source_target_pairs={{0,8},{12,4},{1,9},{13,5},{2,10},{14,6},{3,11},{15,7},{16,24},{28,... | collective-permute-start | bytes 2359304 | tf_op jit(solution)/shard_map/ppermute | solution.py:279
  18.3 1.3 %shard_map.66.refs_6_ = f32[4,64,2048]{2,1,0:T(8,128)S(1)} custom-call(f32[4,128,2048]{2,1,0:T(8,128)S(1)} %bitcast.8), custom_call_target="tpu_custom_call" | custom-call | bytes 4194304 | tf_op jit(solution)/shard_map/pallas_call | solution.py:155
  19.6 0.0 copy-start.2
  19.6 0.7 shard_map.67.refs_6_
  20.3 0.7 shard_map.68.refs_6_
  21.0 0.3 copy-done.5
  21.3 1.0 copy-done.2
  22.3 3.4 %copy-done.1 = bf16[2048,2048]{1,0:T(8,128)(2,1)S(1)} copy-done((bf16[2048,2048]{1,0:T(8,128)(2,1)S(1)}, bf16[2048,2048]{1,0:T(8,128)(2,1)}, u32[]{:S(2)}) %copy-start.1) | copy-done | bytes 8388632
  25.7 4.3 %shard_map.65 = (f32[128,2048]{1,0:T(8,128)S(1)}, f32[128,2048]{1,0:T(8,128)S(1)}) custom-call(bf16[2048,512]{1,0:T(8,128)(2,1)S(1)} %bitcast.12, bf16[2048,2048]{1,0:T(8,128)(2,1)S(1)} %copy-done.1), custom_call_target="tpu_custom_call" | custom-call | flops 2147483648 | bytes 8388608 | tf_op jit(solution)/shard_map/pallas_call | solution.py:113
  30.0 0.6 fusion.8
  30.6 4.3 %collective-permute-done = f32[128,2048]{1,0:T(8,128)} collective-permute-done((f32[128,2048]{1,0:T(8,128)}, f32[128,2048]{1,0:T(8,128)}, u32[]{:S(2)}, u32[]{:S(2)}) %collective-permute-start) | collective-permute-done | bytes 1048608 | tf_op jit(solution)/shard_map/ppermute | solution.py:277
  34.9 1.1 %select_add_fusion.1 = f32[64,2048]{1,0:T(8,128)S(1)} fusion(f32[128,2048]{1,0:T(8,128)} %collective-permute-done, f32[128,2048]{1,0:T(8,128)S(1)} %get-tuple-element.27, pred[]{:T(512)S(6)} %or.3), kind=kLoop, calls=%fused_computation.5 | loop fusion | flops 262144 | bytes 1572865 | tf_op jit(solution)/shard_map/add | solution.py:286
  36.0 2.5 %collective-permute-start.6 = (f32[64,2048]{1,0:T(8,128)S(1)}, f32[64,2048]{1,0:T(8,128)S(1)}, u32[]{:S(2)}, u32[]{:S(2)}) collective-permute-start(f32[64,2048]{1,0:T(8,128)S(1)} %select_add_fusion.1), channel_id=1, source_target_pairs={{0,4},{4,12},{12,8},{8,0},{1,5},{5,13},{13,9},{9,1},{2,6},{6,14},{... | collective-permute-start | bytes 1572872 | tf_op jit(solution)/shard_map/ppermute | solution.py:286
  38.5 1.1 %select_add_fusion.2 = (f32[32,2048]{1,0:T(8,128)S(1)}, f32[32,2048]{1,0:T(8,128)S(1)}, f32[32,2048]{1,0:T(8,128)S(1)}) fusion(f32[128,2048]{1,0:T(8,128)} %collective-permute-done, f32[128,2048]{1,0:T(8,128)S(1)} %get-tuple-element.27, pred[]{:T(512)S(6)} %or.3, f32[32,2048]{1,0:T(8,128)S(1)} %copy-done.10), kind=kLoop, calls=%fused_computation.12 | loop fusion | flops 262144 | bytes 2097153 | tf_op jit(solution)/shard_map/add | solution.py:288
  39.7 0.0 copy-start.7
  39.7 0.0 copy-start.8
  39.7 0.0 copy-start.9
  39.7 1.5 %collective-permute-start.1 = (f32[64,2048]{1,0:T(8,128)S(1)}, f32[64,2048]{1,0:T(8,128)S(1)}, u32[]{:S(2)}, u32[]{:S(2)}) collective-permute-start(f32[64,2048]{1,0:T(8,128)S(1)} %pad_maximum_fusion), channel_id=1, source_target_pairs={{0,4},{4,12},{12,8},{8,0},{1,5},{5,13},{13,9},{9,1},{2,6},{6,14},{... | collective-permute-start | bytes 1572872 | tf_op jit(solution)/shard_map/ppermute | solution.py:289
  41.2 1.3 %select_add_fusion = f32[128,2048]{1,0:T(8,128)S(1)} fusion(f32[128,2048]{1,0:T(8,128)S(1)} %get-tuple-element.25, f32[128,2048]{1,0:T(8,128)} %collective-permute-done, pred[]{:T(512)S(6)} %or.3), kind=kLoop, calls=%fused_computation | loop fusion | flops 524288 | bytes 3145729 | tf_op jit(solution)/shard_map/add | solution.py:292
  42.6 2.3 %collective-permute-start.2 = (f32[32,2048]{1,0:T(8,128)S(1)}, f32[32,2048]{1,0:T(8,128)S(1)}, u32[]{:S(2)}, u32[]{:S(2)}) collective-permute-start(f32[32,2048]{1,0:T(8,128)S(1)} %get-tuple-element.37), channel_id=1, source_target_pairs={{0,4},{12,8},{1,5},{13,9},{2,6},{14,10},{3,7},{15,11},{16,20},{28,... | collective-permute-start | bytes 786440 | tf_op jit(solution)/shard_map/ppermute | solution.py:290
  44.8 0.0 collective-permute-done.4
  44.9 6.9 %collective-permute-done.5 = f32[96,2048]{1,0:T(8,128)} collective-permute-done((f32[96,2048]{1,0:T(8,128)}, f32[96,2048]{1,0:T(8,128)}, u32[]{:S(2)}, u32[]{:S(2)}) %collective-permute-start.5) | collective-permute-done | bytes 786464 | tf_op jit(solution)/shard_map/ppermute | solution.py:279
  51.8 13.0 %collective-permute-done.6 = f32[64,2048]{1,0:T(8,128)S(1)} collective-permute-done((f32[64,2048]{1,0:T(8,128)S(1)}, f32[64,2048]{1,0:T(8,128)S(1)}, u32[]{:S(2)}, u32[]{:S(2)}) %collective-permute-start.6) | collective-permute-done | bytes 524320 | tf_op jit(solution)/shard_map/ppermute | solution.py:286
  64.7 2.1 %fusion.1.refs_0_ = f32[64,2048]{1,0:T(8,128)} fusion(f32[64,2048]{1,0:T(8,128)S(1)} %collective-permute-done.6, f32[96,2048]{1,0:T(8,128)} %collective-permute-done.5, f32[96,2048]{1,0:T(8,128)} %collective-permute-done.4, f32[128,2048]{1,0:T(8,128)S(1)} %select_add_fusion), kind=kLoop, calls=%fused_computation.3 | loop fusion | flops 393216 | bytes 2621440 | tf_op jit(solution)/shard_map/add | solution.py:293
  66.8 1.5 %collective-permute-start.9 = (f32[64,2048]{1,0:T(8,128)}, f32[64,2048]{1,0:T(8,128)}, u32[]{:S(2)}, u32[]{:S(2)}) collective-permute-start(f32[64,2048]{1,0:T(8,128)} %fusion.1.refs_0_), channel_id=1, source_target_pairs={{0,2},{2,0},{1,3},{3,1},{4,6},{6,4},{5,7},{7,5},{8,10},{10,8},{9,1... | collective-permute-start | bytes 1572872 | tf_op jit(solution)/shard_map/ppermute | solution.py:297
  68.3 7.5 %collective-permute-done.1 = f32[64,2048]{1,0:T(8,128)S(1)} collective-permute-done((f32[64,2048]{1,0:T(8,128)S(1)}, f32[64,2048]{1,0:T(8,128)S(1)}, u32[]{:S(2)}, u32[]{:S(2)}) %collective-permute-start.1) | collective-permute-done | bytes 524320 | tf_op jit(solution)/shard_map/ppermute | solution.py:289
  75.9 0.9 collective-permute-start.3
  76.8 1.8 %fusion.3.refs_0_ = f32[32,2048]{1,0:T(8,128)} fusion(f32[96,2048]{1,0:T(8,128)} %collective-permute-done.5, f32[96,2048]{1,0:T(8,128)} %collective-permute-done.4, f32[128,2048]{1,0:T(8,128)S(1)} %select_add_fusion, f32[64,2048]{1,0:T(8,128)S(1)} %collective-permute-done.1), kind=kLoop, calls=%fused_computation.8 | loop fusion | flops 196608 | bytes 1310720 | tf_op jit(solution)/shard_map/add | solution.py:295
  78.6 1.5 %collective-permute-start.8 = (f32[32,2048]{1,0:T(8,128)}, f32[32,2048]{1,0:T(8,128)}, u32[]{:S(2)}, u32[]{:S(2)}) collective-permute-start(f32[32,2048]{1,0:T(8,128)} %fusion.3.refs_0_), channel_id=1, source_target_pairs={{0,2},{2,0},{1,3},{3,1},{4,6},{6,4},{5,7},{7,5},{8,10},{10,8},{9,1... | collective-permute-start | bytes 786440 | tf_op jit(solution)/shard_map/ppermute | solution.py:301
  80.1 0.8 fusion.4.refs_0_
  80.9 0.5 collective-permute-start.7
  81.5 3.1 %shard_map.69.refs_7_ = f32[4,2048]{1,0:T(4,128)S(1)} custom-call(f32[64,2048]{1,0:T(8,128)} %fusion.1.refs_0_, f32[64,2048]{1,0:T(8,128)} %collective-permute-done.9.refs_1_, f32[4,2048]{1,0:T(4,128)S(1)} %reshape.129.refs_2_, f32[32,128]{1,0:T(8,128)S(1)} %copy-done.9, bf16[256,256]{1,0:T(8,128)(2,1)S(1)} %copy-done.7, bf16[256,256]{1,0:T(8,128)(2,1)S(1)} %copy-done.8, ...), custom_call_target="tpu_custom_call" | custom-call | flops 402653184 | tf_op jit(solution)/shard_map/pallas_call | solution.py:237
  84.6 3.4 %collective-permute-done.8.refs_1_ = f32[32,2048]{1,0:T(8,128)} collective-permute-done((f32[32,2048]{1,0:T(8,128)}, f32[32,2048]{1,0:T(8,128)}, u32[]{:S(2)}, u32[]{:S(2)}) %collective-permute-start.8) | collective-permute-done | bytes 262176 | tf_op jit(solution)/shard_map/ppermute | solution.py:301
  88.0 2.5 %shard_map.70.refs_7_ = f32[4,2048]{1,0:T(4,128)S(1)} custom-call(f32[32,2048]{1,0:T(8,128)} %fusion.3.refs_0_, f32[32,2048]{1,0:T(8,128)} %collective-permute-done.8.refs_1_, f32[4,2048]{1,0:T(4,128)S(1)} %reshape.129.refs_2_, f32[32,128]{1,0:T(8,128)S(1)} %copy-done.9, bf16[256,256]{1,0:T(8,128)(2,1)S(1)} %copy-done.7, bf16[256,256]{1,0:T(8,128)(2,1)S(1)} %copy-done.8, ...), custom_call_target="tpu_custom_call" | custom-call | flops 201326592 | tf_op jit(solution)/shard_map/pallas_call | solution.py:237
  90.6 2.1 %collective-permute-done.7.refs_1_ = f32[32,2048]{1,0:T(8,128)} collective-permute-done((f32[32,2048]{1,0:T(8,128)}, f32[32,2048]{1,0:T(8,128)}, u32[]{:S(2)}, u32[]{:S(2)}) %collective-permute-start.7) | collective-permute-done | bytes 262176 | tf_op jit(solution)/shard_map/ppermute | solution.py:301
  92.7 2.5 %shard_map.71 = f32[4,2048]{1,0:T(4,128)S(1)} custom-call(f32[32,2048]{1,0:T(8,128)} %fusion.4.refs_0_, f32[32,2048]{1,0:T(8,128)} %collective-permute-done.7.refs_1_, f32[4,2048]{1,0:T(4,128)S(1)} %reshape.129.refs_2_, f32[32,128]{1,0:T(8,128)S(1)} %copy-done.9, bf16[256,256]{1,0:T(8,128)(2,1)S(1)} %copy-done.7, bf16[256,256]{1,0:T(8,128)(2,1)S(1)} %copy-done.8, ...), custom_call_target="tpu_custom_call" | custom-call | flops 201326592 | tf_op jit(solution)/shard_map/pallas_call | solution.py:237
  95.3 0.1 collective-permute-start.10
  95.3 1.2 %collective-permute-done.10 = f32[4,2048]{1,0:T(4,128)S(1)} collective-permute-done((f32[4,2048]{1,0:T(4,128)S(1)}, f32[4,2048]{1,0:T(4,128)S(1)}, u32[]{:S(2)}, u32[]{:S(2)}) %collective-permute-start.10) | collective-permute-done | bytes 32800 | tf_op jit(solution)/shard_map/ppermute | solution.py:267
  96.5 1.2 %collective-permute-start.11 = (f32[4,2048]{1,0:T(4,128)S(1)}, f32[4,2048]{1,0:T(4,128)S(1)}, u32[]{:S(2)}, u32[]{:S(2)}) collective-permute-start(f32[4,2048]{1,0:T(4,128)S(1)} %add.140), channel_id=1, source_target_pairs={{0,4},{4,0},{8,12},{12,8},{1,5},{5,1},{9,13},{13,9},{2,6},{6,2},{1... | collective-permute-start | bytes 98312 | tf_op jit(solution)/shard_map/ppermute | solution.py:261
  97.8 0.7 collective-permute-start.12
  98.5 2.5 %collective-permute-start.13 = (f32[4,2048]{1,0:T(4,128)S(1)}, f32[4,2048]{1,0:T(4,128)S(1)}, u32[]{:S(2)}, u32[]{:S(2)}) collective-permute-start(f32[4,2048]{1,0:T(4,128)S(1)} %add.140), channel_id=1, source_target_pairs={{0,12},{4,8},{8,4},{12,0},{1,13},{5,9},{9,5},{13,1},{2,14},{6,10},... | collective-permute-start | bytes 98312 | tf_op jit(solution)/shard_map/ppermute | solution.py:261
  101.0 1.6 %collective-permute-done.12 = f32[4,2048]{1,0:T(4,128)S(1)} collective-permute-done((f32[4,2048]{1,0:T(4,128)S(1)}, f32[4,2048]{1,0:T(4,128)S(1)}, u32[]{:S(2)}, u32[]{:S(2)}) %collective-permute-start.12) | collective-permute-done | bytes 32800 | tf_op jit(solution)/shard_map/ppermute | solution.py:261
  102.6 1.6 %collective-permute-done.13 = f32[4,2048]{1,0:T(4,128)S(1)} collective-permute-done((f32[4,2048]{1,0:T(4,128)S(1)}, f32[4,2048]{1,0:T(4,128)S(1)}, u32[]{:S(2)}, u32[]{:S(2)}) %collective-permute-start.13) | collective-permute-done | bytes 32800 | tf_op jit(solution)/shard_map/ppermute | solution.py:261
  104.3 0.1 copy.8
  104.4 0.8 mul.70
  (28 shorter events, 0.2 us)
Async XLA Ops:
  0.0 18.3 %copy-start = (f32[2,2,1,128,2048]{4,3,2,1,0:T(8,128)S(1)}, f32[2,2,1,128,2048]{4,3,2,1,0:T(8,128)}, u32[]{:S(2)}) copy-start(f32[2,2,1,128,2048]{4,3,2,1,0:T(8,128)} %param.8) | copy-start | bytes 12582916
  7.9 27.0 %collective-permute-start = (f32[128,2048]{1,0:T(8,128)}, f32[128,2048]{1,0:T(8,128)}, u32[]{:S(2)}, u32[]{:S(2)}) collective-permute-start(f32[128,2048]{1,0:T(8,128)} %get-tuple-element.20), channel_id=1, source_target_pairs={{0,4},{4,0},{8,12},{12,8},{1,5},{5,1},{9,13},{13,9},{2,6},{6,2},{1... | collective-permute-start | bytes 3145736 | tf_op jit(solution)/shard_map/ppermute | solution.py:277
  11.0 33.9 %collective-permute-start.4 = (f32[96,2048]{1,0:T(8,128)}, f32[96,2048]{1,0:T(8,128)}, u32[]{:S(2)}, u32[]{:S(2)}) collective-permute-start(f32[96,2048]{1,0:T(8,128)} %get-tuple-element.29), channel_id=1, source_target_pairs={{4,8},{8,4},{5,9},{9,5},{6,10},{10,6},{7,11},{11,7},{20,24},{24,20... | collective-permute-start | bytes 2359304 | tf_op jit(solution)/shard_map/ppermute | solution.py:278
  12.5 39.2 %collective-permute-start.5 = (f32[96,2048]{1,0:T(8,128)}, f32[96,2048]{1,0:T(8,128)}, u32[]{:S(2)}, u32[]{:S(2)}) collective-permute-start(f32[96,2048]{1,0:T(8,128)} %get-tuple-element.29), channel_id=1, source_target_pairs={{0,8},{12,4},{1,9},{13,5},{2,10},{14,6},{3,11},{15,7},{16,24},{28,... | collective-permute-start | bytes 2359304 | tf_op jit(solution)/shard_map/ppermute | solution.py:279
  19.6 1.4 %copy-start.3 = (f32[4,64,2048]{2,1,0:T(8,128)}, f32[4,64,2048]{2,1,0:T(8,128)S(1)}, u32[]{:S(2)}) copy-start(f32[4,64,2048]{2,1,0:T(8,128)S(1)} %shard_map.66.refs_6_) | copy-start | bytes 6291460
  19.6 2.7 %copy-start.2 = (bf16[2048,1,512]{2,0,1:T(8,128)(2,1)S(1)}, bf16[2048,1,512]{2,0,1:T(8,128)(2,1)}, u32[]{:S(2)}) copy-start(bf16[2048,1,512]{2,0,1:T(8,128)(2,1)} %param.7) | copy-start | bytes 6291460
  20.3 1.0 copy-start.5
  22.3 3.4 %copy-start.1 = (bf16[2048,2048]{1,0:T(8,128)(2,1)S(1)}, bf16[2048,2048]{1,0:T(8,128)(2,1)}, u32[]{:S(2)}) copy-start(bf16[2048,2048]{1,0:T(8,128)(2,1)} %data_ref.2) | copy-start | bytes 25165828
  25.7 12.8 %copy-start.10 = (f32[32,2048]{1,0:T(8,128)S(1)}, f32[32,2048]{1,0:T(8,128)}, u32[]{:S(2)}) copy-start(f32[32,2048]{1,0:T(8,128)} %get-tuple-element.28) | copy-start | bytes 786436
  36.0 28.8 %collective-permute-start.6 = (f32[64,2048]{1,0:T(8,128)S(1)}, f32[64,2048]{1,0:T(8,128)S(1)}, u32[]{:S(2)}, u32[]{:S(2)}) collective-permute-start(f32[64,2048]{1,0:T(8,128)S(1)} %select_add_fusion.1), channel_id=1, source_target_pairs={{0,4},{4,12},{12,8},{8,0},{1,5},{5,13},{13,9},{9,1},{2,6},{6,14},{... | collective-permute-start | bytes 1572872 | tf_op jit(solution)/shard_map/ppermute | solution.py:286
  39.7 41.8 %copy-start.4 = (f32[4,64,2048]{2,1,0:T(8,128)S(1)}, f32[4,64,2048]{2,1,0:T(8,128)}, u32[]{:S(2)}) copy-start(f32[4,64,2048]{2,1,0:T(8,128)} %copy-done.3) | copy-start | bytes 6291460
  39.7 41.8 %copy-start.7 = (bf16[256,256]{1,0:T(8,128)(2,1)S(1)}, bf16[256,256]{1,0:T(8,128)(2,1)}, u32[]{:S(2)}) copy-start(bf16[256,256]{1,0:T(8,128)(2,1)} %constant.58.clone.refs_4_) | copy-start | bytes 393220
  39.7 41.8 %copy-start.8 = (bf16[256,256]{1,0:T(8,128)(2,1)S(1)}, bf16[256,256]{1,0:T(8,128)(2,1)}, u32[]{:S(2)}) copy-start(bf16[256,256]{1,0:T(8,128)(2,1)} %constant.59.clone.refs_5_) | copy-start | bytes 393220
  39.7 41.8 %copy-start.9 = (f32[32,128]{1,0:T(8,128)S(1)}, f32[32,128]{1,0:T(8,128)}, u32[]{:S(2)}) copy-start(f32[32,128]{1,0:T(8,128)} %constant.57.clone.refs_3_) | copy-start | bytes 49156
  39.7 36.2 %collective-permute-start.1 = (f32[64,2048]{1,0:T(8,128)S(1)}, f32[64,2048]{1,0:T(8,128)S(1)}, u32[]{:S(2)}, u32[]{:S(2)}) collective-permute-start(f32[64,2048]{1,0:T(8,128)S(1)} %pad_maximum_fusion), channel_id=1, source_target_pairs={{0,4},{4,12},{12,8},{8,0},{1,5},{5,13},{13,9},{9,1},{2,6},{6,14},{... | collective-permute-start | bytes 1572872 | tf_op jit(solution)/shard_map/ppermute | solution.py:289
  42.6 37.5 %collective-permute-start.2 = (f32[32,2048]{1,0:T(8,128)S(1)}, f32[32,2048]{1,0:T(8,128)S(1)}, u32[]{:S(2)}, u32[]{:S(2)}) collective-permute-start(f32[32,2048]{1,0:T(8,128)S(1)} %get-tuple-element.37), channel_id=1, source_target_pairs={{0,4},{12,8},{1,5},{13,9},{2,6},{14,10},{3,7},{15,11},{16,20},{28,... | collective-permute-start | bytes 786440 | tf_op jit(solution)/shard_map/ppermute | solution.py:290
  66.8 14.6 %collective-permute-start.9 = (f32[64,2048]{1,0:T(8,128)}, f32[64,2048]{1,0:T(8,128)}, u32[]{:S(2)}, u32[]{:S(2)}) collective-permute-start(f32[64,2048]{1,0:T(8,128)} %fusion.1.refs_0_), channel_id=1, source_target_pairs={{0,2},{2,0},{1,3},{3,1},{4,6},{6,4},{5,7},{7,5},{8,10},{10,8},{9,1... | collective-permute-start | bytes 1572872 | tf_op jit(solution)/shard_map/ppermute | solution.py:297
  75.9 4.2 %collective-permute-start.3 = (f32[32,2048]{1,0:T(8,128)S(1)}, f32[32,2048]{1,0:T(8,128)S(1)}, u32[]{:S(2)}, u32[]{:S(2)}) collective-permute-start(f32[32,2048]{1,0:T(8,128)S(1)} %slice_add_fusion.3), channel_id=1, source_target_pairs={{4,8},{8,4},{5,9},{9,5},{6,10},{10,6},{7,11},{11,7},{20,24},{24,20... | collective-permute-start | bytes 786440 | tf_op jit(solution)/shard_map/ppermute | solution.py:291
  78.6 9.5 %collective-permute-start.8 = (f32[32,2048]{1,0:T(8,128)}, f32[32,2048]{1,0:T(8,128)}, u32[]{:S(2)}, u32[]{:S(2)}) collective-permute-start(f32[32,2048]{1,0:T(8,128)} %fusion.3.refs_0_), channel_id=1, source_target_pairs={{0,2},{2,0},{1,3},{3,1},{4,6},{6,4},{5,7},{7,5},{8,10},{10,8},{9,1... | collective-permute-start | bytes 786440 | tf_op jit(solution)/shard_map/ppermute | solution.py:301
  80.9 11.9 %collective-permute-start.7 = (f32[32,2048]{1,0:T(8,128)}, f32[32,2048]{1,0:T(8,128)}, u32[]{:S(2)}, u32[]{:S(2)}) collective-permute-start(f32[32,2048]{1,0:T(8,128)} %fusion.4.refs_0_), channel_id=1, source_target_pairs={{0,2},{2,0},{1,3},{3,1},{4,6},{6,4},{5,7},{7,5},{8,10},{10,8},{9,1... | collective-permute-start | bytes 786440 | tf_op jit(solution)/shard_map/ppermute | solution.py:301
  81.5 6.6 %copy-start.6 = (f32[4,32,2048]{2,1,0:T(8,128)S(1)}, f32[4,32,2048]{2,1,0:T(8,128)}, u32[]{:S(2)}) copy-start(f32[4,32,2048]{2,1,0:T(8,128)} %copy-done.5) | copy-start | bytes 3145732
  95.3 1.3 %collective-permute-start.10 = (f32[4,2048]{1,0:T(4,128)S(1)}, f32[4,2048]{1,0:T(4,128)S(1)}, u32[]{:S(2)}, u32[]{:S(2)}) collective-permute-start(f32[4,2048]{1,0:T(4,128)S(1)} %shard_map.71), channel_id=1, source_target_pairs={{0,1},{1,0},{2,3},{3,2},{4,5},{5,4},{6,7},{7,6},{8,9},{9,8},{10,11... | collective-permute-start | bytes 98312 | tf_op jit(solution)/shard_map/ppermute | solution.py:267
  96.5 4.5 %collective-permute-start.11 = (f32[4,2048]{1,0:T(4,128)S(1)}, f32[4,2048]{1,0:T(4,128)S(1)}, u32[]{:S(2)}, u32[]{:S(2)}) collective-permute-start(f32[4,2048]{1,0:T(4,128)S(1)} %add.140), channel_id=1, source_target_pairs={{0,4},{4,0},{8,12},{12,8},{1,5},{5,1},{9,13},{13,9},{2,6},{6,2},{1... | collective-permute-start | bytes 98312 | tf_op jit(solution)/shard_map/ppermute | solution.py:261
  97.8 4.8 %collective-permute-start.12 = (f32[4,2048]{1,0:T(4,128)S(1)}, f32[4,2048]{1,0:T(4,128)S(1)}, u32[]{:S(2)}, u32[]{:S(2)}) collective-permute-start(f32[4,2048]{1,0:T(4,128)S(1)} %add.140), channel_id=1, source_target_pairs={{0,8},{4,12},{8,0},{12,4},{1,9},{5,13},{9,1},{13,5},{2,10},{6,14},... | collective-permute-start | bytes 98312 | tf_op jit(solution)/shard_map/ppermute | solution.py:261
  98.5 5.7 %collective-permute-start.13 = (f32[4,2048]{1,0:T(4,128)S(1)}, f32[4,2048]{1,0:T(4,128)S(1)}, u32[]{:S(2)}, u32[]{:S(2)}) collective-permute-start(f32[4,2048]{1,0:T(4,128)S(1)} %add.140), channel_id=1, source_target_pairs={{0,12},{4,8},{8,4},{12,0},{1,13},{5,9},{9,5},{13,1},{2,14},{6,10},... | collective-permute-start | bytes 98312 | tf_op jit(solution)/shard_map/ppermute | solution.py:261

commit v5 on v4

--- a/solution.py
+++ b/solution.py
@@ -85,8 +85,11 @@
     for i in range(rows // tile):
         at = slice(i * tile, (i + 1) * tile)
         tiles.append(pltpu.make_async_copy(data_ref.at[at, :], data_v.at[at, :], data_sem.at[i]))
-        tiles[-1].start()
+    for c in tiles[:1]:
+        c.start()
     lwe_copy.wait()
+    for c in tiles[1:]:
+        c.start()
     for b, role in enumerate(roles):
         at = pl.multiple_of(role_block(role) * own, own)
         turned[b * own : (b + 1) * own, :] = lwe_v[:, pl.ds(at, own)].T
@@ -194,9 +197,7 @@
 
 def transform_kernel(blocks, radix, rows, *refs):
     hints = refs[:blocks]
-    first_ref, twist_ref, table_hi, table_lo, cipher_any, total_ref, out_ref, stage, cipher_ref, sem = refs[blocks:]
-    copy = pltpu.make_async_copy(cipher_any, cipher_ref, sem)
-    copy.start()
+    first_ref, twist_ref, table_hi, table_lo, cipher_ref, total_ref, out_ref, stage = refs[blocks:]
     for top in range(0, rows, 8):
         re, im = [], []
         for u in range(radix):
@@ -216,7 +217,6 @@
             at = slice(r * rows + top, r * rows + top + 8)
             stage[at, :LANES] = re[r] * c + im[r] * s
             stage[at, LANES:] = im[r] * c - re[r] * s
-    copy.wait()
     for r in range(radix):
         high, low = split_bf16(stage[r * rows : (r + 1) * rows, :])
         dot = functools.partial(jnp.dot, preferred_element_type=jnp.float32)
@@ -237,16 +237,14 @@
     return pl.pallas_call(
         functools.partial(transform_kernel, len(hints), radix, rows),
         out_shape=jax.ShapeDtypeStruct((4, points), jnp.float32),
-        in_specs=[pl.BlockSpec(memory_space=pltpu.VMEM)] * (len(hints) + 4)
-        + [pl.BlockSpec(memory_space=pl.ANY), pl.BlockSpec(memory_space=pltpu.VMEM)],
+        in_specs=[pl.BlockSpec(memory_space=pltpu.VMEM)] * (len(hints) + 6),
+        out_specs=pl.BlockSpec(memory_space=pltpu.VMEM),
         scratch_shapes=[
             pltpu.VMEM((radix * rows, 2 * LANES), jnp.float32),
-            pltpu.VMEM((4, rows, points), jnp.float32),
-            pltpu.SemaphoreType.DMA,
         ],
         compiler_params=pltpu.CompilerParams(vmem_limit_bytes=16 * MIB),
         cost_estimate=pl.CostEstimate(
-            flops=6 * radix * rows * 256 * 256, bytes_accessed=0, transcendentals=0
+            flops=6 * radix * rows * 256 * 256, bytes_accessed=24 * rows * points, transcendentals=0
         ),
     )(*hints, *tables, cipher, total)
 

time: 106 us -> 104 us (0.981)
  Pallas kernels: 22.9 us -> 20.8 us
    pallas_call x2, Pallas kernels: 12.2 us -> 11 us  [line_hint(): pl.pallas_call(functools.partial(line_hint_kernel, roles, cuts, tile), in...]
  transfers between devices with their start and end apart: 14 -> 14, of which waited for: 9 -> 9; matrix products, arithmetic and copies ran while one was open for 9% -> 9% of each run, Pallas kernels for 12% -> 11%
where the time goes in v5:
time: 104 us
  waiting for transfers between devices  42.3 us (41%)
  starting transfers between devices  25.6 us (25%)
  Pallas kernels  20.8 us (20%)
  other arithmetic  8.99 us (9%)
  local copies, waits for them, and re-layouts  5.72 us (6%)
    ppermute x1, waiting for transfers between devices, line_total(): lax.ppermute(later[:2 * q] + jnp.where(end, 0.0, near[:2 * q]), 'col', RO...  13 us
    pallas_call x2, Pallas kernels, line_hint(): pl.pallas_call(functools.partial(line_hint_kernel, roles, cuts, tile), in...  11 us
    ppermute x1, waiting for transfers between devices, line_total(): lax.ppermute(jnp.concatenate([piece, spare], axis=0), 'col', ROUND)  7.54 us
    pallas_call x3, Pallas kernels, transform_products(): pl.pallas_call(functools.partial(transform_kernel, len(hints), radix, row...  7.21 us
    ppermute x1, waiting for transfers between devices, line_total(): direct = lax.ppermute(far_mid, 'col', END_TO_FAR_MIDDLE)  6.91 us
    ppermute x2, waiting for transfers between devices, line_total(): lax.ppermute(hint, 'row', SWAP)  6.2 us
    ppermute x1, starting transfers between devices, line_total(): direct = lax.ppermute(far_mid, 'col', END_TO_FAR_MIDDLE)  5.75 us
    unnamed x23, local copies, waits for them, and re-layouts  4.78 us
  transfers between devices with their start and end apart: 14, of which 9 were waited for; matrix products, arithmetic and copies ran while one was open for 9% of the time, Pallas kernels for 11%

profile of v5, /device:TPU:0, one launch (start us, length us, event | category | flops | bytes accessed | tf_op | source)
XLA Modules:
  0.0 103.7 jit_solution(12919516804497861482)
XLA Ops:
  0.0 6.7 %shard_map.64 = (f32[128,2048]{1,0:T(8,128)}, f32[96,2048]{1,0:T(8,128)}, f32[32,2048]{1,0:T(8,128)}) custom-call(bf16[2048,512]{1,0:T(8,128)(2,1)} %bitcast.11, bf16[2048,2048]{1,0:T(8,128)(2,1)} %data_ref.2), custom_call_target="tpu_custom_call" | custom-call | flops 2147483648 | bytes 8388608 | tf_op jit(solution)/shard_map/pallas_call | solution.py:116
  6.7 3.1 %collective-permute-start = (f32[128,2048]{1,0:T(8,128)}, f32[128,2048]{1,0:T(8,128)}, u32[]{:S(2)}, u32[]{:S(2)}) collective-permute-start(f32[128,2048]{1,0:T(8,128)} %get-tuple-element.20), channel_id=1, source_target_pairs={{0,4},{4,0},{8,12},{12,8},{1,5},{5,1},{9,13},{13,9},{2,6},{6,2},{1... | collective-permute-start | bytes 3145736 | tf_op jit(solution)/shard_map/ppermute | solution.py:275
  9.8 1.6 %collective-permute-start.4 = (f32[96,2048]{1,0:T(8,128)}, f32[96,2048]{1,0:T(8,128)}, u32[]{:S(2)}, u32[]{:S(2)}) collective-permute-start(f32[96,2048]{1,0:T(8,128)} %get-tuple-element.29), channel_id=1, source_target_pairs={{4,8},{8,4},{5,9},{9,5},{6,10},{10,6},{7,11},{11,7},{20,24},{24,20... | collective-permute-start | bytes 2359304 | tf_op jit(solution)/shard_map/ppermute | solution.py:276
  11.4 5.7 %collective-permute-start.5 = (f32[96,2048]{1,0:T(8,128)}, f32[96,2048]{1,0:T(8,128)}, u32[]{:S(2)}, u32[]{:S(2)}) collective-permute-start(f32[96,2048]{1,0:T(8,128)} %get-tuple-element.29), channel_id=1, source_target_pairs={{0,8},{12,4},{1,9},{13,5},{2,10},{14,6},{3,11},{15,7},{16,24},{28,... | collective-permute-start | bytes 2359304 | tf_op jit(solution)/shard_map/ppermute | solution.py:277
  17.1 1.3 %shard_map.66.refs_6_ = f32[4,64,2048]{2,1,0:T(8,128)S(1)} custom-call(f32[4,128,2048]{2,1,0:T(8,128)S(1)} %bitcast.8), custom_call_target="tpu_custom_call" | custom-call | bytes 4194304 | tf_op jit(solution)/shard_map/pallas_call | solution.py:158
  18.4 0.0 copy-start.2
  18.4 0.7 shard_map.67.refs_6_
  19.1 0.7 shard_map.68.refs_6_
  19.8 0.3 copy-done.5
  20.1 1.0 %copy-done.2 = bf16[2048,1,512]{2,0,1:T(8,128)(2,1)S(1)} copy-done((bf16[2048,1,512]{2,0,1:T(8,128)(2,1)S(1)}, bf16[2048,1,512]{2,0,1:T(8,128)(2,1)}, u32[]{:S(2)}) %copy-start.2) | copy-done | bytes 2097176
  21.2 3.4 %copy-done.1 = bf16[2048,2048]{1,0:T(8,128)(2,1)S(1)} copy-done((bf16[2048,2048]{1,0:T(8,128)(2,1)S(1)}, bf16[2048,2048]{1,0:T(8,128)(2,1)}, u32[]{:S(2)}) %copy-start.1) | copy-done | bytes 8388632
  24.5 4.3 %shard_map.65 = (f32[128,2048]{1,0:T(8,128)S(1)}, f32[128,2048]{1,0:T(8,128)S(1)}) custom-call(bf16[2048,512]{1,0:T(8,128)(2,1)S(1)} %bitcast.12, bf16[2048,2048]{1,0:T(8,128)(2,1)S(1)} %copy-done.1), custom_call_target="tpu_custom_call" | custom-call | flops 2147483648 | bytes 8388608 | tf_op jit(solution)/shard_map/pallas_call | solution.py:116
  28.8 0.6 fusion.8
  29.4 4.3 %collective-permute-done = f32[128,2048]{1,0:T(8,128)} collective-permute-done((f32[128,2048]{1,0:T(8,128)}, f32[128,2048]{1,0:T(8,128)}, u32[]{:S(2)}, u32[]{:S(2)}) %collective-permute-start) | collective-permute-done | bytes 1048608 | tf_op jit(solution)/shard_map/ppermute | solution.py:275
  33.7 1.1 %select_add_fusion.1 = f32[64,2048]{1,0:T(8,128)S(1)} fusion(f32[128,2048]{1,0:T(8,128)} %collective-permute-done, f32[128,2048]{1,0:T(8,128)S(1)} %get-tuple-element.27, pred[]{:T(512)S(6)} %or.3), kind=kLoop, calls=%fused_computation.5 | loop fusion | flops 262144 | bytes 1572865 | tf_op jit(solution)/shard_map/add | solution.py:284
  34.8 2.5 %collective-permute-start.6 = (f32[64,2048]{1,0:T(8,128)S(1)}, f32[64,2048]{1,0:T(8,128)S(1)}, u32[]{:S(2)}, u32[]{:S(2)}) collective-permute-start(f32[64,2048]{1,0:T(8,128)S(1)} %select_add_fusion.1), channel_id=1, source_target_pairs={{0,4},{4,12},{12,8},{8,0},{1,5},{5,13},{13,9},{9,1},{2,6},{6,14},{... | collective-permute-start | bytes 1572872 | tf_op jit(solution)/shard_map/ppermute | solution.py:284
  37.3 1.1 %select_add_fusion.2 = (f32[32,2048]{1,0:T(8,128)S(1)}, f32[32,2048]{1,0:T(8,128)S(1)}, f32[32,2048]{1,0:T(8,128)S(1)}) fusion(f32[128,2048]{1,0:T(8,128)} %collective-permute-done, f32[128,2048]{1,0:T(8,128)S(1)} %get-tuple-element.27, pred[]{:T(512)S(6)} %or.3, f32[32,2048]{1,0:T(8,128)S(1)} %copy-done.10), kind=kLoop, calls=%fused_computation.12 | loop fusion | flops 262144 | bytes 2097153 | tf_op jit(solution)/shard_map/add | solution.py:286
  38.5 0.0 copy-start.7
  38.5 0.0 copy-start.8
  38.5 0.0 copy-start.9
  38.5 1.5 %collective-permute-start.1 = (f32[64,2048]{1,0:T(8,128)S(1)}, f32[64,2048]{1,0:T(8,128)S(1)}, u32[]{:S(2)}, u32[]{:S(2)}) collective-permute-start(f32[64,2048]{1,0:T(8,128)S(1)} %pad_maximum_fusion), channel_id=1, source_target_pairs={{0,4},{4,12},{12,8},{8,0},{1,5},{5,13},{13,9},{9,1},{2,6},{6,14},{... | collective-permute-start | bytes 1572872 | tf_op jit(solution)/shard_map/ppermute | solution.py:287
  40.1 1.3 %select_add_fusion = f32[128,2048]{1,0:T(8,128)S(1)} fusion(f32[128,2048]{1,0:T(8,128)S(1)} %get-tuple-element.25, f32[128,2048]{1,0:T(8,128)} %collective-permute-done, pred[]{:T(512)S(6)} %or.3), kind=kLoop, calls=%fused_computation | loop fusion | flops 524288 | bytes 3145729 | tf_op jit(solution)/shard_map/add | solution.py:290
  41.4 2.3 %collective-permute-start.2 = (f32[32,2048]{1,0:T(8,128)S(1)}, f32[32,2048]{1,0:T(8,128)S(1)}, u32[]{:S(2)}, u32[]{:S(2)}) collective-permute-start(f32[32,2048]{1,0:T(8,128)S(1)} %get-tuple-element.37), channel_id=1, source_target_pairs={{0,4},{12,8},{1,5},{13,9},{2,6},{14,10},{3,7},{15,11},{16,20},{28,... | collective-permute-start | bytes 786440 | tf_op jit(solution)/shard_map/ppermute | solution.py:288
  43.7 6.9 %collective-permute-done.5 = f32[96,2048]{1,0:T(8,128)} collective-permute-done((f32[96,2048]{1,0:T(8,128)}, f32[96,2048]{1,0:T(8,128)}, u32[]{:S(2)}, u32[]{:S(2)}) %collective-permute-start.5) | collective-permute-done | bytes 786464 | tf_op jit(solution)/shard_map/ppermute | solution.py:277
  50.6 13.0 %collective-permute-done.6 = f32[64,2048]{1,0:T(8,128)S(1)} collective-permute-done((f32[64,2048]{1,0:T(8,128)S(1)}, f32[64,2048]{1,0:T(8,128)S(1)}, u32[]{:S(2)}, u32[]{:S(2)}) %collective-permute-start.6) | collective-permute-done | bytes 524320 | tf_op jit(solution)/shard_map/ppermute | solution.py:284
  63.6 2.1 %fusion.1.refs_0_ = f32[64,2048]{1,0:T(8,128)} fusion(f32[64,2048]{1,0:T(8,128)S(1)} %collective-permute-done.6, f32[96,2048]{1,0:T(8,128)} %collective-permute-done.5, f32[96,2048]{1,0:T(8,128)} %collective-permute-done.4, f32[128,2048]{1,0:T(8,128)S(1)} %select_add_fusion), kind=kLoop, calls=%fused_computation.3 | loop fusion | flops 393216 | bytes 2621440 | tf_op jit(solution)/shard_map/add | solution.py:291
  65.7 1.5 %collective-permute-start.9 = (f32[64,2048]{1,0:T(8,128)}, f32[64,2048]{1,0:T(8,128)}, u32[]{:S(2)}, u32[]{:S(2)}) collective-permute-start(f32[64,2048]{1,0:T(8,128)} %fusion.1.refs_0_), channel_id=1, source_target_pairs={{0,2},{2,0},{1,3},{3,1},{4,6},{6,4},{5,7},{7,5},{8,10},{10,8},{9,1... | collective-permute-start | bytes 1572872 | tf_op jit(solution)/shard_map/ppermute | solution.py:295
  67.2 7.5 %collective-permute-done.1 = f32[64,2048]{1,0:T(8,128)S(1)} collective-permute-done((f32[64,2048]{1,0:T(8,128)S(1)}, f32[64,2048]{1,0:T(8,128)S(1)}, u32[]{:S(2)}, u32[]{:S(2)}) %collective-permute-start.1) | collective-permute-done | bytes 524320 | tf_op jit(solution)/shard_map/ppermute | solution.py:287
  74.7 0.9 collective-permute-start.3
  75.6 1.8 %fusion.3.refs_0_ = f32[32,2048]{1,0:T(8,128)} fusion(f32[96,2048]{1,0:T(8,128)} %collective-permute-done.5, f32[96,2048]{1,0:T(8,128)} %collective-permute-done.4, f32[128,2048]{1,0:T(8,128)S(1)} %select_add_fusion, f32[64,2048]{1,0:T(8,128)S(1)} %collective-permute-done.1), kind=kLoop, calls=%fused_computation.8 | loop fusion | flops 196608 | bytes 1310720 | tf_op jit(solution)/shard_map/add | solution.py:293
  77.4 1.5 %collective-permute-start.8 = (f32[32,2048]{1,0:T(8,128)}, f32[32,2048]{1,0:T(8,128)}, u32[]{:S(2)}, u32[]{:S(2)}) collective-permute-start(f32[32,2048]{1,0:T(8,128)} %fusion.3.refs_0_), channel_id=1, source_target_pairs={{0,2},{2,0},{1,3},{3,1},{4,6},{6,4},{5,7},{7,5},{8,10},{10,8},{9,1... | collective-permute-start | bytes 786440 | tf_op jit(solution)/shard_map/ppermute | solution.py:299
  78.9 0.0 collective-permute-done.2
  78.9 0.8 fusion.4.refs_0_
  79.7 0.5 collective-permute-start.7
  80.4 2.7 %shard_map.69.refs_7_ = f32[4,2048]{1,0:T(4,128)S(1)} custom-call(f32[64,2048]{1,0:T(8,128)} %fusion.1.refs_0_, f32[64,2048]{1,0:T(8,128)} %collective-permute-done.9.refs_1_, f32[4,2048]{1,0:T(4,128)S(1)} %reshape.129.refs_2_, f32[32,128]{1,0:T(8,128)S(1)} %copy-done.9, bf16[256,256]{1,0:T(8,128)(2,1)S(1)} %copy-done.7, bf16[256,256]{1,0:T(8,128)(2,1)S(1)} %copy-done.8, ...), custom_call_target="tpu_custom_call" | custom-call | flops 402653184 | bytes 3145728 | tf_op jit(solution)/shard_map/pallas_call | solution.py:237
  83.1 3.8 %collective-permute-done.8.refs_1_ = f32[32,2048]{1,0:T(8,128)} collective-permute-done((f32[32,2048]{1,0:T(8,128)}, f32[32,2048]{1,0:T(8,128)}, u32[]{:S(2)}, u32[]{:S(2)}) %collective-permute-start.8) | collective-permute-done | bytes 262176 | tf_op jit(solution)/shard_map/ppermute | solution.py:299
  86.9 2.2 %shard_map.70.refs_7_ = f32[4,2048]{1,0:T(4,128)S(1)} custom-call(f32[32,2048]{1,0:T(8,128)} %fusion.3.refs_0_, f32[32,2048]{1,0:T(8,128)} %collective-permute-done.8.refs_1_, f32[4,2048]{1,0:T(4,128)S(1)} %reshape.129.refs_2_, f32[32,128]{1,0:T(8,128)S(1)} %copy-done.9, bf16[256,256]{1,0:T(8,128)(2,1)S(1)} %copy-done.7, bf16[256,256]{1,0:T(8,128)(2,1)S(1)} %copy-done.8, ...), custom_call_target="tpu_custom_call" | custom-call | flops 201326592 | bytes 1572864 | tf_op jit(solution)/shard_map/pallas_call | solution.py:237
  89.1 2.4 %collective-permute-done.7.refs_1_ = f32[32,2048]{1,0:T(8,128)} collective-permute-done((f32[32,2048]{1,0:T(8,128)}, f32[32,2048]{1,0:T(8,128)}, u32[]{:S(2)}, u32[]{:S(2)}) %collective-permute-start.7) | collective-permute-done | bytes 262176 | tf_op jit(solution)/shard_map/ppermute | solution.py:299
  91.6 2.2 %shard_map.71 = f32[4,2048]{1,0:T(4,128)S(1)} custom-call(f32[32,2048]{1,0:T(8,128)} %fusion.4.refs_0_, f32[32,2048]{1,0:T(8,128)} %collective-permute-done.7.refs_1_, f32[4,2048]{1,0:T(4,128)S(1)} %reshape.129.refs_2_, f32[32,128]{1,0:T(8,128)S(1)} %copy-done.9, bf16[256,256]{1,0:T(8,128)(2,1)S(1)} %copy-done.7, bf16[256,256]{1,0:T(8,128)(2,1)S(1)} %copy-done.8, ...), custom_call_target="tpu_custom_call" | custom-call | flops 201326592 | bytes 1572864 | tf_op jit(solution)/shard_map/pallas_call | solution.py:237
  93.8 0.1 collective-permute-start.10
  93.9 1.2 %collective-permute-done.10 = f32[4,2048]{1,0:T(4,128)S(1)} collective-permute-done((f32[4,2048]{1,0:T(4,128)S(1)}, f32[4,2048]{1,0:T(4,128)S(1)}, u32[]{:S(2)}, u32[]{:S(2)}) %collective-permute-start.10) | collective-permute-done | bytes 32800 | tf_op jit(solution)/shard_map/ppermute | solution.py:265
  95.1 1.2 %collective-permute-start.11 = (f32[4,2048]{1,0:T(4,128)S(1)}, f32[4,2048]{1,0:T(4,128)S(1)}, u32[]{:S(2)}, u32[]{:S(2)}) collective-permute-start(f32[4,2048]{1,0:T(4,128)S(1)} %add.140), channel_id=1, source_target_pairs={{0,4},{4,0},{8,12},{12,8},{1,5},{5,1},{9,13},{13,9},{2,6},{6,2},{1... | collective-permute-start | bytes 98312 | tf_op jit(solution)/shard_map/ppermute | solution.py:259
  96.3 0.7 collective-permute-start.12
  97.1 2.5 %collective-permute-start.13 = (f32[4,2048]{1,0:T(4,128)S(1)}, f32[4,2048]{1,0:T(4,128)S(1)}, u32[]{:S(2)}, u32[]{:S(2)}) collective-permute-start(f32[4,2048]{1,0:T(4,128)S(1)} %add.140), channel_id=1, source_target_pairs={{0,12},{4,8},{8,4},{12,0},{1,13},{5,9},{9,5},{13,1},{2,14},{6,10},... | collective-permute-start | bytes 98312 | tf_op jit(solution)/shard_map/ppermute | solution.py:259
  99.5 1.6 %collective-permute-done.12 = f32[4,2048]{1,0:T(4,128)S(1)} collective-permute-done((f32[4,2048]{1,0:T(4,128)S(1)}, f32[4,2048]{1,0:T(4,128)S(1)}, u32[]{:S(2)}, u32[]{:S(2)}) %collective-permute-start.12) | collective-permute-done | bytes 32800 | tf_op jit(solution)/shard_map/ppermute | solution.py:259
  101.1 1.6 %collective-permute-done.13 = f32[4,2048]{1,0:T(4,128)S(1)} collective-permute-done((f32[4,2048]{1,0:T(4,128)S(1)}, f32[4,2048]{1,0:T(4,128)S(1)}, u32[]{:S(2)}, u32[]{:S(2)}) %collective-permute-start.13) | collective-permute-done | bytes 32800 | tf_op jit(solution)/shard_map/ppermute | solution.py:259
  102.8 0.1 copy.8
  102.9 0.8 mul.70
  (28 shorter events, 0.2 us)
Async XLA Ops:
  0.0 17.1 %copy-start = (f32[2,2,1,128,2048]{4,3,2,1,0:T(8,128)S(1)}, f32[2,2,1,128,2048]{4,3,2,1,0:T(8,128)}, u32[]{:S(2)}) copy-start(f32[2,2,1,128,2048]{4,3,2,1,0:T(8,128)} %param.8) | copy-start | bytes 12582916
  6.7 27.0 %collective-permute-start = (f32[128,2048]{1,0:T(8,128)}, f32[128,2048]{1,0:T(8,128)}, u32[]{:S(2)}, u32[]{:S(2)}) collective-permute-start(f32[128,2048]{1,0:T(8,128)} %get-tuple-element.20), channel_id=1, source_target_pairs={{0,4},{4,0},{8,12},{12,8},{1,5},{5,1},{9,13},{13,9},{2,6},{6,2},{1... | collective-permute-start | bytes 3145736 | tf_op jit(solution)/shard_map/ppermute | solution.py:275
  9.8 33.9 %collective-permute-start.4 = (f32[96,2048]{1,0:T(8,128)}, f32[96,2048]{1,0:T(8,128)}, u32[]{:S(2)}, u32[]{:S(2)}) collective-permute-start(f32[96,2048]{1,0:T(8,128)} %get-tuple-element.29), channel_id=1, source_target_pairs={{4,8},{8,4},{5,9},{9,5},{6,10},{10,6},{7,11},{11,7},{20,24},{24,20... | collective-permute-start | bytes 2359304 | tf_op jit(solution)/shard_map/ppermute | solution.py:276
  11.4 39.2 %collective-permute-start.5 = (f32[96,2048]{1,0:T(8,128)}, f32[96,2048]{1,0:T(8,128)}, u32[]{:S(2)}, u32[]{:S(2)}) collective-permute-start(f32[96,2048]{1,0:T(8,128)} %get-tuple-element.29), channel_id=1, source_target_pairs={{0,8},{12,4},{1,9},{13,5},{2,10},{14,6},{3,11},{15,7},{16,24},{28,... | collective-permute-start | bytes 2359304 | tf_op jit(solution)/shard_map/ppermute | solution.py:277
  18.4 1.4 %copy-start.3 = (f32[4,64,2048]{2,1,0:T(8,128)}, f32[4,64,2048]{2,1,0:T(8,128)S(1)}, u32[]{:S(2)}) copy-start(f32[4,64,2048]{2,1,0:T(8,128)S(1)} %shard_map.66.refs_6_) | copy-start | bytes 6291460
  18.4 2.7 %copy-start.2 = (bf16[2048,1,512]{2,0,1:T(8,128)(2,1)S(1)}, bf16[2048,1,512]{2,0,1:T(8,128)(2,1)}, u32[]{:S(2)}) copy-start(bf16[2048,1,512]{2,0,1:T(8,128)(2,1)} %param.7) | copy-start | bytes 6291460
  19.1 1.0 copy-start.5
  21.1 3.4 %copy-start.1 = (bf16[2048,2048]{1,0:T(8,128)(2,1)S(1)}, bf16[2048,2048]{1,0:T(8,128)(2,1)}, u32[]{:S(2)}) copy-start(bf16[2048,2048]{1,0:T(8,128)(2,1)} %data_ref.2) | copy-start | bytes 25165828
  24.5 12.8 %copy-start.10 = (f32[32,2048]{1,0:T(8,128)S(1)}, f32[32,2048]{1,0:T(8,128)}, u32[]{:S(2)}) copy-start(f32[32,2048]{1,0:T(8,128)} %get-tuple-element.28) | copy-start | bytes 786436
  34.8 28.8 %collective-permute-start.6 = (f32[64,2048]{1,0:T(8,128)S(1)}, f32[64,2048]{1,0:T(8,128)S(1)}, u32[]{:S(2)}, u32[]{:S(2)}) collective-permute-start(f32[64,2048]{1,0:T(8,128)S(1)} %select_add_fusion.1), channel_id=1, source_target_pairs={{0,4},{4,12},{12,8},{8,0},{1,5},{5,13},{13,9},{9,1},{2,6},{6,14},{... | collective-permute-start | bytes 1572872 | tf_op jit(solution)/shard_map/ppermute | solution.py:284
  38.5 41.8 %copy-start.4 = (f32[4,64,2048]{2,1,0:T(8,128)S(1)}, f32[4,64,2048]{2,1,0:T(8,128)}, u32[]{:S(2)}) copy-start(f32[4,64,2048]{2,1,0:T(8,128)} %copy-done.3) | copy-start | bytes 6291460
  38.5 41.8 %copy-start.7 = (bf16[256,256]{1,0:T(8,128)(2,1)S(1)}, bf16[256,256]{1,0:T(8,128)(2,1)}, u32[]{:S(2)}) copy-start(bf16[256,256]{1,0:T(8,128)(2,1)} %constant.58.clone.refs_4_) | copy-start | bytes 393220
  38.5 41.8 %copy-start.8 = (bf16[256,256]{1,0:T(8,128)(2,1)S(1)}, bf16[256,256]{1,0:T(8,128)(2,1)}, u32[]{:S(2)}) copy-start(bf16[256,256]{1,0:T(8,128)(2,1)} %constant.59.clone.refs_5_) | copy-start | bytes 393220
  38.5 41.8 %copy-start.9 = (f32[32,128]{1,0:T(8,128)S(1)}, f32[32,128]{1,0:T(8,128)}, u32[]{:S(2)}) copy-start(f32[32,128]{1,0:T(8,128)} %constant.57.clone.refs_3_) | copy-start | bytes 49156
  38.5 36.2 %collective-permute-start.1 = (f32[64,2048]{1,0:T(8,128)S(1)}, f32[64,2048]{1,0:T(8,128)S(1)}, u32[]{:S(2)}, u32[]{:S(2)}) collective-permute-start(f32[64,2048]{1,0:T(8,128)S(1)} %pad_maximum_fusion), channel_id=1, source_target_pairs={{0,4},{4,12},{12,8},{8,0},{1,5},{5,13},{13,9},{9,1},{2,6},{6,14},{... | collective-permute-start | bytes 1572872 | tf_op jit(solution)/shard_map/ppermute | solution.py:287
  41.4 37.5 %collective-permute-start.2 = (f32[32,2048]{1,0:T(8,128)S(1)}, f32[32,2048]{1,0:T(8,128)S(1)}, u32[]{:S(2)}, u32[]{:S(2)}) collective-permute-start(f32[32,2048]{1,0:T(8,128)S(1)} %get-tuple-element.37), channel_id=1, source_target_pairs={{0,4},{12,8},{1,5},{13,9},{2,6},{14,10},{3,7},{15,11},{16,20},{28,... | collective-permute-start | bytes 786440 | tf_op jit(solution)/shard_map/ppermute | solution.py:288
  65.7 14.6 %collective-permute-start.9 = (f32[64,2048]{1,0:T(8,128)}, f32[64,2048]{1,0:T(8,128)}, u32[]{:S(2)}, u32[]{:S(2)}) collective-permute-start(f32[64,2048]{1,0:T(8,128)} %fusion.1.refs_0_), channel_id=1, source_target_pairs={{0,2},{2,0},{1,3},{3,1},{4,6},{6,4},{5,7},{7,5},{8,10},{10,8},{9,1... | collective-permute-start | bytes 1572872 | tf_op jit(solution)/shard_map/ppermute | solution.py:295
  74.7 4.2 %collective-permute-start.3 = (f32[32,2048]{1,0:T(8,128)S(1)}, f32[32,2048]{1,0:T(8,128)S(1)}, u32[]{:S(2)}, u32[]{:S(2)}) collective-permute-start(f32[32,2048]{1,0:T(8,128)S(1)} %slice_add_fusion.3), channel_id=1, source_target_pairs={{4,8},{8,4},{5,9},{9,5},{6,10},{10,6},{7,11},{11,7},{20,24},{24,20... | collective-permute-start | bytes 786440 | tf_op jit(solution)/shard_map/ppermute | solution.py:289
  77.4 9.5 %collective-permute-start.8 = (f32[32,2048]{1,0:T(8,128)}, f32[32,2048]{1,0:T(8,128)}, u32[]{:S(2)}, u32[]{:S(2)}) collective-permute-start(f32[32,2048]{1,0:T(8,128)} %fusion.3.refs_0_), channel_id=1, source_target_pairs={{0,2},{2,0},{1,3},{3,1},{4,6},{6,4},{5,7},{7,5},{8,10},{10,8},{9,1... | collective-permute-start | bytes 786440 | tf_op jit(solution)/shard_map/ppermute | solution.py:299
  79.7 11.9 %collective-permute-start.7 = (f32[32,2048]{1,0:T(8,128)}, f32[32,2048]{1,0:T(8,128)}, u32[]{:S(2)}, u32[]{:S(2)}) collective-permute-start(f32[32,2048]{1,0:T(8,128)} %fusion.4.refs_0_), channel_id=1, source_target_pairs={{0,2},{2,0},{1,3},{3,1},{4,6},{6,4},{5,7},{7,5},{8,10},{10,8},{9,1... | collective-permute-start | bytes 786440 | tf_op jit(solution)/shard_map/ppermute | solution.py:299
  80.3 6.6 %copy-start.6 = (f32[4,32,2048]{2,1,0:T(8,128)S(1)}, f32[4,32,2048]{2,1,0:T(8,128)}, u32[]{:S(2)}) copy-start(f32[4,32,2048]{2,1,0:T(8,128)} %copy-done.5) | copy-start | bytes 3145732
  93.8 1.3 %collective-permute-start.10 = (f32[4,2048]{1,0:T(4,128)S(1)}, f32[4,2048]{1,0:T(4,128)S(1)}, u32[]{:S(2)}, u32[]{:S(2)}) collective-permute-start(f32[4,2048]{1,0:T(4,128)S(1)} %shard_map.71), channel_id=1, source_target_pairs={{0,1},{1,0},{2,3},{3,2},{4,5},{5,4},{6,7},{7,6},{8,9},{9,8},{10,11... | collective-permute-start | bytes 98312 | tf_op jit(solution)/shard_map/ppermute | solution.py:265
  95.1 4.5 %collective-permute-start.11 = (f32[4,2048]{1,0:T(4,128)S(1)}, f32[4,2048]{1,0:T(4,128)S(1)}, u32[]{:S(2)}, u32[]{:S(2)}) collective-permute-start(f32[4,2048]{1,0:T(4,128)S(1)} %add.140), channel_id=1, source_target_pairs={{0,4},{4,0},{8,12},{12,8},{1,5},{5,1},{9,13},{13,9},{2,6},{6,2},{1... | collective-permute-start | bytes 98312 | tf_op jit(solution)/shard_map/ppermute | solution.py:259
  96.3 4.8 %collective-permute-start.12 = (f32[4,2048]{1,0:T(4,128)S(1)}, f32[4,2048]{1,0:T(4,128)S(1)}, u32[]{:S(2)}, u32[]{:S(2)}) collective-permute-start(f32[4,2048]{1,0:T(4,128)S(1)} %add.140), channel_id=1, source_target_pairs={{0,8},{4,12},{8,0},{12,4},{1,9},{5,13},{9,1},{13,5},{2,10},{6,14},... | collective-permute-start | bytes 98312 | tf_op jit(solution)/shard_map/ppermute | solution.py:259
  97.1 5.7 %collective-permute-start.13 = (f32[4,2048]{1,0:T(4,128)S(1)}, f32[4,2048]{1,0:T(4,128)S(1)}, u32[]{:S(2)}, u32[]{:S(2)}) collective-permute-start(f32[4,2048]{1,0:T(4,128)S(1)} %add.140), channel_id=1, source_target_pairs={{0,12},{4,8},{8,4},{12,0},{1,13},{5,9},{9,5},{13,1},{2,14},{6,10},... | collective-permute-start | bytes 98312 | tf_op jit(solution)/shard_map/ppermute | solution.py:259

commit v6 on v5

--- a/solution.py
+++ b/solution.py
@@ -293,8 +293,9 @@
     hint_b = base[2 * q : h] + (cross[2 * q :] + direct[2 * q :]) + waited[:q]
     far_sum, _ = lax.optimization_barrier((far_sum, hint_b))
     with_a = lambda t: transform_products([hint_a, lax.ppermute(hint_a, "row", SWAP)], tables, swapped[0], t)
+    total = with_a(total)
+    far_sum, total = lax.optimization_barrier((far_sum, total))
     hint_c = base[h:] + jnp.where(end, round_b[q:], 0.0) + (near_tail + far_sum)
-    total = with_a(total)
     for hint, part in ((hint_b, swapped[1]), (hint_c, swapped[2])):
         total = transform_products([hint, lax.ppermute(hint, "row", SWAP)], tables, part, total)
     return total

time: 104 us -> 102 us (0.981)
  waiting for transfers between devices: 42.3 us -> 45.7 us
  Pallas kernels: 20.8 us -> 17.5 us
  other arithmetic: 8.99 us -> 6.73 us
  starting transfers between devices: 25.6 us -> 26.9 us
    pallas_call x3, Pallas kernels: 7.21 us -> 3.88 us  [transform_products(): pl.pallas_call(functools.partial(transform_kernel, len(hints), radix, row...]
    ppermute x2, waiting for transfers between devices: 6.2 us -> 7.56 us  [line_total(): lax.ppermute(hint, 'row', SWAP)]
    ppermute x2, starting transfers between devices: 2.03 us -> 3.11 us  [line_total(): lax.ppermute(hint, 'row', SWAP)]
  transfers between devices with their start and end apart: 14 -> 14, of which waited for: 9 -> 10; matrix products, arithmetic and copies ran while one was open for 9% -> 7% of each run, Pallas kernels for 11% -> 9%
where the time goes in v6:
time: 102 us
  waiting for transfers between devices  45.7 us (45%)
  starting transfers between devices  26.9 us (26%)
  Pallas kernels  17.5 us (17%)
  other arithmetic  6.73 us (7%)
  local copies, waits for them, and re-layouts  5.03 us (5%)
    ppermute x1, waiting for transfers between devices, line_total(): lax.ppermute(later[:2 * q] + jnp.where(end, 0.0, near[:2 * q]), 'col', RO...  13 us
    pallas_call x2, Pallas kernels, line_hint(): pl.pallas_call(functools.partial(line_hint_kernel, roles, cuts, tile), in...  11 us
    ppermute x1, waiting for transfers between devices, line_total(): lax.ppermute(jnp.concatenate([piece, spare], axis=0), 'col', ROUND)  8.28 us
    ppermute x2, waiting for transfers between devices, line_total(): lax.ppermute(hint, 'row', SWAP)  7.56 us
    ppermute x1, waiting for transfers between devices, line_total(): direct = lax.ppermute(far_mid, 'col', END_TO_FAR_MIDDLE)  6.77 us
    ppermute x1, starting transfers between devices, line_total(): direct = lax.ppermute(far_mid, 'col', END_TO_FAR_MIDDLE)  5.77 us
    ppermute x1, waiting for transfers between devices, line_total(): near = lax.ppermute(first, 'col', NEIGHBOURS)  4.87 us
    ppermute x3, starting transfers between devices, sum_over(): lax.ppermute(x, axis, xor_pairs(size, step))  4.45 us
  transfers between devices with their start and end apart: 14, of which 10 were waited for; matrix products, arithmetic and copies ran while one was open for 7% of the time, Pallas kernels for 9%

profile of v6, /device:TPU:0, one launch (start us, length us, event | category | flops | bytes accessed | tf_op | source)
XLA Modules:
  0.0 102.1 jit_solution(8895273827114920748)
XLA Ops:
  0.0 6.7 %shard_map.64 = (f32[128,2048]{1,0:T(8,128)}, f32[96,2048]{1,0:T(8,128)}, f32[32,2048]{1,0:T(8,128)}) custom-call(bf16[2048,512]{1,0:T(8,128)(2,1)} %bitcast.11, bf16[2048,2048]{1,0:T(8,128)(2,1)} %data_ref.2), custom_call_target="tpu_custom_call" | custom-call | flops 2147483648 | bytes 8388608 | tf_op jit(solution)/shard_map/pallas_call | solution.py:116
  6.7 3.1 %collective-permute-start = (f32[128,2048]{1,0:T(8,128)}, f32[128,2048]{1,0:T(8,128)}, u32[]{:S(2)}, u32[]{:S(2)}) collective-permute-start(f32[128,2048]{1,0:T(8,128)} %get-tuple-element.22), channel_id=1, source_target_pairs={{0,4},{4,0},{8,12},{12,8},{1,5},{5,1},{9,13},{13,9},{2,6},{6,2},{1... | collective-permute-start | bytes 3145736 | tf_op jit(solution)/shard_map/ppermute | solution.py:275
  9.8 1.6 %collective-permute-start.4 = (f32[96,2048]{1,0:T(8,128)}, f32[96,2048]{1,0:T(8,128)}, u32[]{:S(2)}, u32[]{:S(2)}) collective-permute-start(f32[96,2048]{1,0:T(8,128)} %get-tuple-element.31), channel_id=1, source_target_pairs={{4,8},{8,4},{5,9},{9,5},{6,10},{10,6},{7,11},{11,7},{20,24},{24,20... | collective-permute-start | bytes 2359304 | tf_op jit(solution)/shard_map/ppermute | solution.py:276
  11.4 5.8 %collective-permute-start.5 = (f32[96,2048]{1,0:T(8,128)}, f32[96,2048]{1,0:T(8,128)}, u32[]{:S(2)}, u32[]{:S(2)}) collective-permute-start(f32[96,2048]{1,0:T(8,128)} %get-tuple-element.31), channel_id=1, source_target_pairs={{0,8},{12,4},{1,9},{13,5},{2,10},{14,6},{3,11},{15,7},{16,24},{28,... | collective-permute-start | bytes 2359304 | tf_op jit(solution)/shard_map/ppermute | solution.py:277
  17.2 1.3 %shard_map.66.refs_6_ = f32[4,64,2048]{2,1,0:T(8,128)S(1)} custom-call(f32[4,128,2048]{2,1,0:T(8,128)S(1)} %bitcast.8), custom_call_target="tpu_custom_call" | custom-call | bytes 4194304 | tf_op jit(solution)/shard_map/pallas_call | solution.py:158
  18.4 0.0 copy-start.2
  18.5 0.7 shard_map.67.refs_6_
  19.1 0.7 shard_map.68.refs_6_
  19.8 0.3 copy-done.5
  20.1 0.6 fusion.8
  20.8 0.3 copy-done.2
  21.2 3.4 %copy-done.1 = bf16[2048,2048]{1,0:T(8,128)(2,1)S(1)} copy-done((bf16[2048,2048]{1,0:T(8,128)(2,1)S(1)}, bf16[2048,2048]{1,0:T(8,128)(2,1)}, u32[]{:S(2)}) %copy-start.1) | copy-done | bytes 8388632
  24.6 4.3 %shard_map.65 = (f32[128,2048]{1,0:T(8,128)S(1)}, f32[128,2048]{1,0:T(8,128)S(1)}) custom-call(bf16[2048,512]{1,0:T(8,128)(2,1)S(1)} %bitcast.12, bf16[2048,2048]{1,0:T(8,128)(2,1)S(1)} %copy-done.1), custom_call_target="tpu_custom_call" | custom-call | flops 2147483648 | bytes 8388608 | tf_op jit(solution)/shard_map/pallas_call | solution.py:116
  28.8 4.9 %collective-permute-done = f32[128,2048]{1,0:T(8,128)} collective-permute-done((f32[128,2048]{1,0:T(8,128)}, f32[128,2048]{1,0:T(8,128)}, u32[]{:S(2)}, u32[]{:S(2)}) %collective-permute-start) | collective-permute-done | bytes 1048608 | tf_op jit(solution)/shard_map/ppermute | solution.py:275
  33.7 1.1 %select_add_fusion.1 = f32[64,2048]{1,0:T(8,128)S(1)} fusion(f32[128,2048]{1,0:T(8,128)} %collective-permute-done, f32[128,2048]{1,0:T(8,128)S(1)} %get-tuple-element.29, pred[]{:T(512)S(6)} %or.3), kind=kLoop, calls=%fused_computation.5 | loop fusion | flops 262144 | bytes 1572865 | tf_op jit(solution)/shard_map/add | solution.py:284
  34.8 2.5 %collective-permute-start.6 = (f32[64,2048]{1,0:T(8,128)S(1)}, f32[64,2048]{1,0:T(8,128)S(1)}, u32[]{:S(2)}, u32[]{:S(2)}) collective-permute-start(f32[64,2048]{1,0:T(8,128)S(1)} %select_add_fusion.1), channel_id=1, source_target_pairs={{0,4},{4,12},{12,8},{8,0},{1,5},{5,13},{13,9},{9,1},{2,6},{6,14},{... | collective-permute-start | bytes 1572872 | tf_op jit(solution)/shard_map/ppermute | solution.py:284
  37.3 1.1 %select_add_fusion.2 = (f32[32,2048]{1,0:T(8,128)S(1)}, f32[32,2048]{1,0:T(8,128)S(1)}, f32[32,2048]{1,0:T(8,128)S(1)}) fusion(f32[128,2048]{1,0:T(8,128)} %collective-permute-done, f32[128,2048]{1,0:T(8,128)S(1)} %get-tuple-element.29, pred[]{:T(512)S(6)} %or.3, f32[32,2048]{1,0:T(8,128)S(1)} %copy-done.10), kind=kLoop, calls=%fused_computation.12 | loop fusion | flops 262144 | bytes 2097153 | tf_op jit(solution)/shard_map/add | solution.py:286
  38.5 0.0 copy-start.7
  38.5 0.0 copy-start.8
  38.5 0.0 copy-start.9
  38.5 1.5 %collective-permute-start.1 = (f32[64,2048]{1,0:T(8,128)S(1)}, f32[64,2048]{1,0:T(8,128)S(1)}, u32[]{:S(2)}, u32[]{:S(2)}) collective-permute-start(f32[64,2048]{1,0:T(8,128)S(1)} %pad_maximum_fusion), channel_id=1, source_target_pairs={{0,4},{4,12},{12,8},{8,0},{1,5},{5,13},{13,9},{9,1},{2,6},{6,14},{... | collective-permute-start | bytes 1572872 | tf_op jit(solution)/shard_map/ppermute | solution.py:287
  40.1 1.3 %select_add_fusion = f32[128,2048]{1,0:T(8,128)S(1)} fusion(f32[128,2048]{1,0:T(8,128)S(1)} %get-tuple-element.27, f32[128,2048]{1,0:T(8,128)} %collective-permute-done, pred[]{:T(512)S(6)} %or.3), kind=kLoop, calls=%fused_computation | loop fusion | flops 524288 | bytes 3145729 | tf_op jit(solution)/shard_map/add | solution.py:290
  41.4 2.4 %collective-permute-start.2 = (f32[32,2048]{1,0:T(8,128)S(1)}, f32[32,2048]{1,0:T(8,128)S(1)}, u32[]{:S(2)}, u32[]{:S(2)}) collective-permute-start(f32[32,2048]{1,0:T(8,128)S(1)} %get-tuple-element.41), channel_id=1, source_target_pairs={{0,4},{12,8},{1,5},{13,9},{2,6},{14,10},{3,7},{15,11},{16,20},{28,... | collective-permute-start | bytes 786440 | tf_op jit(solution)/shard_map/ppermute | solution.py:288
  43.8 6.8 %collective-permute-done.5 = f32[96,2048]{1,0:T(8,128)} collective-permute-done((f32[96,2048]{1,0:T(8,128)}, f32[96,2048]{1,0:T(8,128)}, u32[]{:S(2)}, u32[]{:S(2)}) %collective-permute-start.5) | collective-permute-done | bytes 786464 | tf_op jit(solution)/shard_map/ppermute | solution.py:277
  50.6 13.0 %collective-permute-done.6 = f32[64,2048]{1,0:T(8,128)S(1)} collective-permute-done((f32[64,2048]{1,0:T(8,128)S(1)}, f32[64,2048]{1,0:T(8,128)S(1)}, u32[]{:S(2)}, u32[]{:S(2)}) %collective-permute-start.6) | collective-permute-done | bytes 524320 | tf_op jit(solution)/shard_map/ppermute | solution.py:284
  63.6 1.3 %fusion.1.refs_0_ = f32[64,2048]{1,0:T(8,128)S(1)} fusion(f32[64,2048]{1,0:T(8,128)S(1)} %collective-permute-done.6, f32[96,2048]{1,0:T(8,128)} %collective-permute-done.5, f32[96,2048]{1,0:T(8,128)} %collective-permute-done.4, f32[128,2048]{1,0:T(8,128)S(1)} %select_add_fusion), kind=kLoop, calls=%fused_computation.3 | loop fusion | flops 393216 | bytes 2621440 | tf_op jit(solution)/shard_map/add | solution.py:291
  64.9 1.6 %collective-permute-start.7 = (f32[64,2048]{1,0:T(8,128)S(1)}, f32[64,2048]{1,0:T(8,128)S(1)}, u32[]{:S(2)}, u32[]{:S(2)}) collective-permute-start(f32[64,2048]{1,0:T(8,128)S(1)} %fusion.1.refs_0_), channel_id=1, source_target_pairs={{0,2},{2,0},{1,3},{3,1},{4,6},{6,4},{5,7},{7,5},{8,10},{10,8},{9,1... | collective-permute-start | bytes 1572872 | tf_op jit(solution)/shard_map/ppermute | solution.py:295
  66.4 8.3 %collective-permute-done.1 = f32[64,2048]{1,0:T(8,128)S(1)} collective-permute-done((f32[64,2048]{1,0:T(8,128)S(1)}, f32[64,2048]{1,0:T(8,128)S(1)}, u32[]{:S(2)}, u32[]{:S(2)}) %collective-permute-start.1) | collective-permute-done | bytes 524320 | tf_op jit(solution)/shard_map/ppermute | solution.py:287
  74.7 0.9 collective-permute-start.3
  75.6 1.1 %fusion.3.refs_0_ = f32[32,2048]{1,0:T(8,128)S(1)} fusion(f32[96,2048]{1,0:T(8,128)} %collective-permute-done.5, f32[96,2048]{1,0:T(8,128)} %collective-permute-done.4, f32[128,2048]{1,0:T(8,128)S(1)} %select_add_fusion, f32[64,2048]{1,0:T(8,128)S(1)} %collective-permute-done.1), kind=kLoop, calls=%fused_computation.8 | loop fusion | flops 196608 | bytes 1310720 | tf_op jit(solution)/shard_map/add | solution.py:293
  76.7 1.6 %collective-permute-start.9 = (f32[32,2048]{1,0:T(8,128)S(1)}, f32[32,2048]{1,0:T(8,128)S(1)}, u32[]{:S(2)}, u32[]{:S(2)}) collective-permute-start(f32[32,2048]{1,0:T(8,128)S(1)} %fusion.3.refs_0_), channel_id=1, source_target_pairs={{0,2},{2,0},{1,3},{3,1},{4,6},{6,4},{5,7},{7,5},{8,10},{10,8},{9,1... | collective-permute-start | bytes 786440 | tf_op jit(solution)/shard_map/ppermute | solution.py:300
  78.3 0.4 collective-permute-done.7.refs_1_
  78.7 1.5 %shard_map.69.refs_7_ = f32[4,2048]{1,0:T(4,128)S(1)} custom-call(f32[64,2048]{1,0:T(8,128)S(1)} %fusion.1.refs_0_, f32[64,2048]{1,0:T(8,128)S(1)} %collective-permute-done.7.refs_1_, f32[4,2048]{1,0:T(4,128)S(1)} %reshape.129.refs_2_, f32[32,128]{1,0:T(8,128)S(1)} %copy-done.9, bf16[256,256]{1,0:T(8,128)(2,1)S(1)} %copy-done.7, ...), custom_call_target="tpu_custom_call" | custom-call | flops 402653184 | bytes 3145728 | tf_op jit(solution)/shard_map/pallas_call | solution.py:237
  80.2 0.1 fusion.4.refs_0_
  80.3 1.6 %collective-permute-start.8 = (f32[32,2048]{1,0:T(8,128)S(1)}, f32[32,2048]{1,0:T(8,128)S(1)}, u32[]{:S(2)}, u32[]{:S(2)}) collective-permute-start(f32[32,2048]{1,0:T(8,128)S(1)} %fusion.4.refs_0_), channel_id=1, source_target_pairs={{0,2},{2,0},{1,3},{3,1},{4,6},{6,4},{5,7},{7,5},{8,10},{10,8},{9,1... | collective-permute-start | bytes 786440 | tf_op jit(solution)/shard_map/ppermute | solution.py:300
  81.8 4.1 %collective-permute-done.9.refs_1_ = f32[32,2048]{1,0:T(8,128)S(1)} collective-permute-done((f32[32,2048]{1,0:T(8,128)S(1)}, f32[32,2048]{1,0:T(8,128)S(1)}, u32[]{:S(2)}, u32[]{:S(2)}) %collective-permute-start.9) | collective-permute-done | bytes 262176 | tf_op jit(solution)/shard_map/ppermute | solution.py:300
  85.9 1.2 %shard_map.70.refs_7_ = f32[4,2048]{1,0:T(4,128)S(1)} custom-call(f32[32,2048]{1,0:T(8,128)S(1)} %fusion.3.refs_0_, f32[32,2048]{1,0:T(8,128)S(1)} %collective-permute-done.9.refs_1_, f32[4,2048]{1,0:T(4,128)S(1)} %reshape.129.refs_2_, f32[32,128]{1,0:T(8,128)S(1)} %copy-done.9, bf16[256,256]{1,0:T(8,128)(2,1)S(1)} %copy-done.7, ...), custom_call_target="tpu_custom_call" | custom-call | flops 201326592 | bytes 1572864 | tf_op jit(solution)/shard_map/pallas_call | solution.py:237
  87.1 3.5 %collective-permute-done.8.refs_1_ = f32[32,2048]{1,0:T(8,128)S(1)} collective-permute-done((f32[32,2048]{1,0:T(8,128)S(1)}, f32[32,2048]{1,0:T(8,128)S(1)}, u32[]{:S(2)}, u32[]{:S(2)}) %collective-permute-start.8) | collective-permute-done | bytes 262176 | tf_op jit(solution)/shard_map/ppermute | solution.py:300
  90.6 1.2 %shard_map.71 = f32[4,2048]{1,0:T(4,128)S(1)} custom-call(f32[32,2048]{1,0:T(8,128)S(1)} %fusion.4.refs_0_, f32[32,2048]{1,0:T(8,128)S(1)} %collective-permute-done.8.refs_1_, f32[4,2048]{1,0:T(4,128)S(1)} %reshape.129.refs_2_, f32[32,128]{1,0:T(8,128)S(1)} %copy-done.9, bf16[256,256]{1,0:T(8,128)(2,1)S(1)} %copy-done.7, bf16[256,256]{1,0:T(8,128)(2,1)S(1)} %copy-done.8, ...), custom_call_target="tpu_custom_call" | custom-call | flops 201326592 | bytes 1572864 | tf_op jit(solution)/shard_map/pallas_call | solution.py:237
  91.8 0.1 collective-permute-start.10
  91.9 1.2 %collective-permute-done.10 = f32[4,2048]{1,0:T(4,128)S(1)} collective-permute-done((f32[4,2048]{1,0:T(4,128)S(1)}, f32[4,2048]{1,0:T(4,128)S(1)}, u32[]{:S(2)}, u32[]{:S(2)}) %collective-permute-start.10) | collective-permute-done | bytes 32800 | tf_op jit(solution)/shard_map/ppermute | solution.py:265
  93.1 1.8 %collective-permute-start.11 = (f32[4,2048]{1,0:T(4,128)S(1)}, f32[4,2048]{1,0:T(4,128)S(1)}, u32[]{:S(2)}, u32[]{:S(2)}) collective-permute-start(f32[4,2048]{1,0:T(4,128)S(1)} %add.140), channel_id=1, source_target_pairs={{0,4},{4,0},{8,12},{12,8},{1,5},{5,1},{9,13},{13,9},{2,6},{6,2},{1... | collective-permute-start | bytes 98312 | tf_op jit(solution)/shard_map/ppermute | solution.py:259
  94.9 0.6 collective-permute-start.12
  95.4 2.1 %collective-permute-start.13 = (f32[4,2048]{1,0:T(4,128)S(1)}, f32[4,2048]{1,0:T(4,128)S(1)}, u32[]{:S(2)}, u32[]{:S(2)}) collective-permute-start(f32[4,2048]{1,0:T(4,128)S(1)} %add.140), channel_id=1, source_target_pairs={{0,12},{4,8},{8,4},{12,0},{1,13},{5,9},{9,5},{13,1},{2,14},{6,10},... | collective-permute-start | bytes 98312 | tf_op jit(solution)/shard_map/ppermute | solution.py:259
  97.6 2.9 %collective-permute-done.12 = f32[4,2048]{1,0:T(4,128)S(1)} collective-permute-done((f32[4,2048]{1,0:T(4,128)S(1)}, f32[4,2048]{1,0:T(4,128)S(1)}, u32[]{:S(2)}, u32[]{:S(2)}) %collective-permute-start.12) | collective-permute-done | bytes 32800 | tf_op jit(solution)/shard_map/ppermute | solution.py:259
  100.4 0.7 collective-permute-done.13
  101.2 0.1 copy.8
  101.3 0.8 mul.70
  (28 shorter events, 0.2 us)
Async XLA Ops:
  0.0 17.1 %copy-start = (f32[2,2,1,128,2048]{4,3,2,1,0:T(8,128)S(1)}, f32[2,2,1,128,2048]{4,3,2,1,0:T(8,128)}, u32[]{:S(2)}) copy-start(f32[2,2,1,128,2048]{4,3,2,1,0:T(8,128)} %param.8) | copy-start | bytes 12582916
  6.7 27.0 %collective-permute-start = (f32[128,2048]{1,0:T(8,128)}, f32[128,2048]{1,0:T(8,128)}, u32[]{:S(2)}, u32[]{:S(2)}) collective-permute-start(f32[128,2048]{1,0:T(8,128)} %get-tuple-element.22), channel_id=1, source_target_pairs={{0,4},{4,0},{8,12},{12,8},{1,5},{5,1},{9,13},{13,9},{2,6},{6,2},{1... | collective-permute-start | bytes 3145736 | tf_op jit(solution)/shard_map/ppermute | solution.py:275
  9.8 34.0 %collective-permute-start.4 = (f32[96,2048]{1,0:T(8,128)}, f32[96,2048]{1,0:T(8,128)}, u32[]{:S(2)}, u32[]{:S(2)}) collective-permute-start(f32[96,2048]{1,0:T(8,128)} %get-tuple-element.31), channel_id=1, source_target_pairs={{4,8},{8,4},{5,9},{9,5},{6,10},{10,6},{7,11},{11,7},{20,24},{24,20... | collective-permute-start | bytes 2359304 | tf_op jit(solution)/shard_map/ppermute | solution.py:276
  11.4 39.2 %collective-permute-start.5 = (f32[96,2048]{1,0:T(8,128)}, f32[96,2048]{1,0:T(8,128)}, u32[]{:S(2)}, u32[]{:S(2)}) collective-permute-start(f32[96,2048]{1,0:T(8,128)} %get-tuple-element.31), channel_id=1, source_target_pairs={{0,8},{12,4},{1,9},{13,5},{2,10},{14,6},{3,11},{15,7},{16,24},{28,... | collective-permute-start | bytes 2359304 | tf_op jit(solution)/shard_map/ppermute | solution.py:277
  18.4 1.4 %copy-start.3 = (f32[4,64,2048]{2,1,0:T(8,128)}, f32[4,64,2048]{2,1,0:T(8,128)S(1)}, u32[]{:S(2)}) copy-start(f32[4,64,2048]{2,1,0:T(8,128)S(1)} %shard_map.66.refs_6_) | copy-start | bytes 6291460
  18.4 2.7 %copy-start.2 = (bf16[2048,1,512]{2,0,1:T(8,128)(2,1)S(1)}, bf16[2048,1,512]{2,0,1:T(8,128)(2,1)}, u32[]{:S(2)}) copy-start(bf16[2048,1,512]{2,0,1:T(8,128)(2,1)} %param.7) | copy-start | bytes 6291460
  19.1 1.0 copy-start.5
  21.2 3.4 %copy-start.1 = (bf16[2048,2048]{1,0:T(8,128)(2,1)S(1)}, bf16[2048,2048]{1,0:T(8,128)(2,1)}, u32[]{:S(2)}) copy-start(bf16[2048,2048]{1,0:T(8,128)(2,1)} %data_ref.2) | copy-start | bytes 25165828
  24.6 12.8 %copy-start.10 = (f32[32,2048]{1,0:T(8,128)S(1)}, f32[32,2048]{1,0:T(8,128)}, u32[]{:S(2)}) copy-start(f32[32,2048]{1,0:T(8,128)} %get-tuple-element.30) | copy-start | bytes 786436
  34.8 28.8 %collective-permute-start.6 = (f32[64,2048]{1,0:T(8,128)S(1)}, f32[64,2048]{1,0:T(8,128)S(1)}, u32[]{:S(2)}, u32[]{:S(2)}) collective-permute-start(f32[64,2048]{1,0:T(8,128)S(1)} %select_add_fusion.1), channel_id=1, source_target_pairs={{0,4},{4,12},{12,8},{8,0},{1,5},{5,13},{13,9},{9,1},{2,6},{6,14},{... | collective-permute-start | bytes 1572872 | tf_op jit(solution)/shard_map/ppermute | solution.py:284
  38.5 40.2 %copy-start.4 = (f32[4,64,2048]{2,1,0:T(8,128)S(1)}, f32[4,64,2048]{2,1,0:T(8,128)}, u32[]{:S(2)}) copy-start(f32[4,64,2048]{2,1,0:T(8,128)} %copy-done.3) | copy-start | bytes 6291460
  38.5 40.2 %copy-start.7 = (bf16[256,256]{1,0:T(8,128)(2,1)S(1)}, bf16[256,256]{1,0:T(8,128)(2,1)}, u32[]{:S(2)}) copy-start(bf16[256,256]{1,0:T(8,128)(2,1)} %constant.58.clone.refs_4_) | copy-start | bytes 393220
  38.5 40.2 %copy-start.8 = (bf16[256,256]{1,0:T(8,128)(2,1)S(1)}, bf16[256,256]{1,0:T(8,128)(2,1)}, u32[]{:S(2)}) copy-start(bf16[256,256]{1,0:T(8,128)(2,1)} %constant.59.clone.refs_5_) | copy-start | bytes 393220
  38.5 40.2 %copy-start.9 = (f32[32,128]{1,0:T(8,128)S(1)}, f32[32,128]{1,0:T(8,128)}, u32[]{:S(2)}) copy-start(f32[32,128]{1,0:T(8,128)} %constant.57.clone.refs_3_) | copy-start | bytes 49156
  38.5 36.2 %collective-permute-start.1 = (f32[64,2048]{1,0:T(8,128)S(1)}, f32[64,2048]{1,0:T(8,128)S(1)}, u32[]{:S(2)}, u32[]{:S(2)}) collective-permute-start(f32[64,2048]{1,0:T(8,128)S(1)} %pad_maximum_fusion), channel_id=1, source_target_pairs={{0,4},{4,12},{12,8},{8,0},{1,5},{5,13},{13,9},{9,1},{2,6},{6,14},{... | collective-permute-start | bytes 1572872 | tf_op jit(solution)/shard_map/ppermute | solution.py:287
  41.4 44.5 %copy-start.6 = (f32[4,32,2048]{2,1,0:T(8,128)S(1)}, f32[4,32,2048]{2,1,0:T(8,128)}, u32[]{:S(2)}) copy-start(f32[4,32,2048]{2,1,0:T(8,128)} %copy-done.5) | copy-start | bytes 3145732
  41.4 38.8 %collective-permute-start.2 = (f32[32,2048]{1,0:T(8,128)S(1)}, f32[32,2048]{1,0:T(8,128)S(1)}, u32[]{:S(2)}, u32[]{:S(2)}) collective-permute-start(f32[32,2048]{1,0:T(8,128)S(1)} %get-tuple-element.41), channel_id=1, source_target_pairs={{0,4},{12,8},{1,5},{13,9},{2,6},{14,10},{3,7},{15,11},{16,20},{28,... | collective-permute-start | bytes 786440 | tf_op jit(solution)/shard_map/ppermute | solution.py:288
  64.9 13.8 %collective-permute-start.7 = (f32[64,2048]{1,0:T(8,128)S(1)}, f32[64,2048]{1,0:T(8,128)S(1)}, u32[]{:S(2)}, u32[]{:S(2)}) collective-permute-start(f32[64,2048]{1,0:T(8,128)S(1)} %fusion.1.refs_0_), channel_id=1, source_target_pairs={{0,2},{2,0},{1,3},{3,1},{4,6},{6,4},{5,7},{7,5},{8,10},{10,8},{9,1... | collective-permute-start | bytes 1572872 | tf_op jit(solution)/shard_map/ppermute | solution.py:295
  74.7 3.5 %collective-permute-start.3 = (f32[32,2048]{1,0:T(8,128)S(1)}, f32[32,2048]{1,0:T(8,128)S(1)}, u32[]{:S(2)}, u32[]{:S(2)}) collective-permute-start(f32[32,2048]{1,0:T(8,128)S(1)} %slice_add_fusion.3), channel_id=1, source_target_pairs={{4,8},{8,4},{5,9},{9,5},{6,10},{10,6},{7,11},{11,7},{20,24},{24,20... | collective-permute-start | bytes 786440 | tf_op jit(solution)/shard_map/ppermute | solution.py:289
  76.7 9.2 %collective-permute-start.9 = (f32[32,2048]{1,0:T(8,128)S(1)}, f32[32,2048]{1,0:T(8,128)S(1)}, u32[]{:S(2)}, u32[]{:S(2)}) collective-permute-start(f32[32,2048]{1,0:T(8,128)S(1)} %fusion.3.refs_0_), channel_id=1, source_target_pairs={{0,2},{2,0},{1,3},{3,1},{4,6},{6,4},{5,7},{7,5},{8,10},{10,8},{9,1... | collective-permute-start | bytes 786440 | tf_op jit(solution)/shard_map/ppermute | solution.py:300
  80.3 10.3 %collective-permute-start.8 = (f32[32,2048]{1,0:T(8,128)S(1)}, f32[32,2048]{1,0:T(8,128)S(1)}, u32[]{:S(2)}, u32[]{:S(2)}) collective-permute-start(f32[32,2048]{1,0:T(8,128)S(1)} %fusion.4.refs_0_), channel_id=1, source_target_pairs={{0,2},{2,0},{1,3},{3,1},{4,6},{6,4},{5,7},{7,5},{8,10},{10,8},{9,1... | collective-permute-start | bytes 786440 | tf_op jit(solution)/shard_map/ppermute | solution.py:300
  91.8 1.3 %collective-permute-start.10 = (f32[4,2048]{1,0:T(4,128)S(1)}, f32[4,2048]{1,0:T(4,128)S(1)}, u32[]{:S(2)}, u32[]{:S(2)}) collective-permute-start(f32[4,2048]{1,0:T(4,128)S(1)} %shard_map.71), channel_id=1, source_target_pairs={{0,1},{1,0},{2,3},{3,2},{4,5},{5,4},{6,7},{7,6},{8,9},{9,8},{10,11... | collective-permute-start | bytes 98312 | tf_op jit(solution)/shard_map/ppermute | solution.py:265
  93.1 4.5 %collective-permute-start.11 = (f32[4,2048]{1,0:T(4,128)S(1)}, f32[4,2048]{1,0:T(4,128)S(1)}, u32[]{:S(2)}, u32[]{:S(2)}) collective-permute-start(f32[4,2048]{1,0:T(4,128)S(1)} %add.140), channel_id=1, source_target_pairs={{0,4},{4,0},{8,12},{12,8},{1,5},{5,1},{9,13},{13,9},{2,6},{6,2},{1... | collective-permute-start | bytes 98312 | tf_op jit(solution)/shard_map/ppermute | solution.py:259
  94.9 5.6 %collective-permute-start.12 = (f32[4,2048]{1,0:T(4,128)S(1)}, f32[4,2048]{1,0:T(4,128)S(1)}, u32[]{:S(2)}, u32[]{:S(2)}) collective-permute-start(f32[4,2048]{1,0:T(4,128)S(1)} %add.140), channel_id=1, source_target_pairs={{0,8},{4,12},{8,0},{12,4},{1,9},{5,13},{9,1},{13,5},{2,10},{6,14},... | collective-permute-start | bytes 98312 | tf_op jit(solution)/shard_map/ppermute | solution.py:259
  95.4 5.7 %collective-permute-start.13 = (f32[4,2048]{1,0:T(4,128)S(1)}, f32[4,2048]{1,0:T(4,128)S(1)}, u32[]{:S(2)}, u32[]{:S(2)}) collective-permute-start(f32[4,2048]{1,0:T(4,128)S(1)} %add.140), channel_id=1, source_target_pairs={{0,12},{4,8},{8,4},{12,0},{1,13},{5,9},{9,5},{13,1},{2,14},{6,10},... | collective-permute-start | bytes 98312 | tf_op jit(solution)/shard_map/ppermute | solution.py:259

commit v7 on v6

--- a/solution.py
+++ b/solution.py
@@ -79,15 +79,20 @@
     lwe_v, data_v, turned, made, lwe_sem, data_sem, out_sem = rest[len(pieces) :]
     rows = data_ref.shape[0]
     own = made.shape[0] // len(roles)
-    lwe_copy = pltpu.make_async_copy(lwe_ref, lwe_v, lwe_sem)
-    lwe_copy.start()
+    share = lwe_ref.shape[0] // 4
+    lwe_copies = []
+    for i in range(4):
+        at = slice(i * share, (i + 1) * share)
+        lwe_copies.append(pltpu.make_async_copy(lwe_ref.at[at, :], lwe_v.at[at, :], lwe_sem.at[i]))
+        lwe_copies[-1].start()
     tiles = []
     for i in range(rows // tile):
         at = slice(i * tile, (i + 1) * tile)
         tiles.append(pltpu.make_async_copy(data_ref.at[at, :], data_v.at[at, :], data_sem.at[i]))
     for c in tiles[:1]:
         c.start()
-    lwe_copy.wait()
+    for c in lwe_copies:
+        c.wait()
     for c in tiles[1:]:
         c.start()
     for b, role in enumerate(roles):
@@ -123,7 +128,7 @@
             pltpu.VMEM((rows, depth), jnp.bfloat16),
             pltpu.VMEM((len(roles) * own, depth), jnp.bfloat16),
             pltpu.VMEM((len(roles) * own, rows), jnp.float32),
-            pltpu.SemaphoreType.DMA,
+            pltpu.SemaphoreType.DMA((4,)),
             pltpu.SemaphoreType.DMA((rows // tile,)),
             pltpu.SemaphoreType.DMA((rows // tile * sum(len(c) for c in cuts),)),
         ],

time: 102 us -> 102 us (level)
  no operation moved by 1% of the time
where the time goes in v7:
time: 102 us
  waiting for transfers between devices  45.6 us (45%)
  starting transfers between devices  26.9 us (26%)
  Pallas kernels  17.5 us (17%)
  other arithmetic  6.73 us (7%)
  local copies, waits for them, and re-layouts  5.03 us (5%)
    ppermute x1, waiting for transfers between devices, line_total(): lax.ppermute(later[:2 * q] + jnp.where(end, 0.0, near[:2 * q]), 'col', RO...  13 us
    pallas_call x2, Pallas kernels, line_hint(): pl.pallas_call(functools.partial(line_hint_kernel, roles, cuts, tile), in...  11 us
    ppermute x1, waiting for transfers between devices, line_total(): lax.ppermute(jnp.concatenate([piece, spare], axis=0), 'col', ROUND)  8.28 us
    ppermute x2, waiting for transfers between devices, line_total(): lax.ppermute(hint, 'row', SWAP)  7.56 us
    ppermute x1, waiting for transfers between devices, line_total(): direct = lax.ppermute(far_mid, 'col', END_TO_FAR_MIDDLE)  6.77 us
    ppermute x1, starting transfers between devices, line_total(): direct = lax.ppermute(far_mid, 'col', END_TO_FAR_MIDDLE)  5.77 us
    ppermute x1, waiting for transfers between devices, line_total(): near = lax.ppermute(first, 'col', NEIGHBOURS)  4.84 us
    ppermute x3, starting transfers between devices, sum_over(): lax.ppermute(x, axis, xor_pairs(size, step))  4.45 us
  transfers between devices with their start and end apart: 14, of which 10 were waited for; matrix products, arithmetic and copies ran while one was open for 7% of the time, Pallas kernels for 9%

profile of v7, /device:TPU:0, one launch (start us, length us, event | category | flops | bytes accessed | tf_op | source)
XLA Modules:
  0.0 102.0 jit_solution(12089468520172308676)
XLA Ops:
  0.0 6.7 %shard_map.64 = (f32[128,2048]{1,0:T(8,128)}, f32[96,2048]{1,0:T(8,128)}, f32[32,2048]{1,0:T(8,128)}) custom-call(bf16[2048,512]{1,0:T(8,128)(2,1)} %bitcast.11, bf16[2048,2048]{1,0:T(8,128)(2,1)} %data_ref.2), custom_call_target="tpu_custom_call" | custom-call | flops 2147483648 | bytes 8388608 | tf_op jit(solution)/shard_map/pallas_call | solution.py:121
  6.7 3.1 %collective-permute-start = (f32[128,2048]{1,0:T(8,128)}, f32[128,2048]{1,0:T(8,128)}, u32[]{:S(2)}, u32[]{:S(2)}) collective-permute-start(f32[128,2048]{1,0:T(8,128)} %get-tuple-element.22), channel_id=1, source_target_pairs={{0,4},{4,0},{8,12},{12,8},{1,5},{5,1},{9,13},{13,9},{2,6},{6,2},{1... | collective-permute-start | bytes 3145736 | tf_op jit(solution)/shard_map/ppermute | solution.py:280
  9.8 1.6 %collective-permute-start.4 = (f32[96,2048]{1,0:T(8,128)}, f32[96,2048]{1,0:T(8,128)}, u32[]{:S(2)}, u32[]{:S(2)}) collective-permute-start(f32[96,2048]{1,0:T(8,128)} %get-tuple-element.31), channel_id=1, source_target_pairs={{4,8},{8,4},{5,9},{9,5},{6,10},{10,6},{7,11},{11,7},{20,24},{24,20... | collective-permute-start | bytes 2359304 | tf_op jit(solution)/shard_map/ppermute | solution.py:281
  11.3 5.8 %collective-permute-start.5 = (f32[96,2048]{1,0:T(8,128)}, f32[96,2048]{1,0:T(8,128)}, u32[]{:S(2)}, u32[]{:S(2)}) collective-permute-start(f32[96,2048]{1,0:T(8,128)} %get-tuple-element.31), channel_id=1, source_target_pairs={{0,8},{12,4},{1,9},{13,5},{2,10},{14,6},{3,11},{15,7},{16,24},{28,... | collective-permute-start | bytes 2359304 | tf_op jit(solution)/shard_map/ppermute | solution.py:282
  17.1 1.3 %shard_map.66.refs_6_ = f32[4,64,2048]{2,1,0:T(8,128)S(1)} custom-call(f32[4,128,2048]{2,1,0:T(8,128)S(1)} %bitcast.8), custom_call_target="tpu_custom_call" | custom-call | bytes 4194304 | tf_op jit(solution)/shard_map/pallas_call | solution.py:163
  18.4 0.0 copy-start.2
  18.4 0.7 shard_map.67.refs_6_
  19.1 0.7 shard_map.68.refs_6_
  19.7 0.3 copy-done.5
  20.1 0.6 fusion.8
  20.8 0.3 copy-done.2
  21.1 3.4 %copy-done.1 = bf16[2048,2048]{1,0:T(8,128)(2,1)S(1)} copy-done((bf16[2048,2048]{1,0:T(8,128)(2,1)S(1)}, bf16[2048,2048]{1,0:T(8,128)(2,1)}, u32[]{:S(2)}) %copy-start.1) | copy-done | bytes 8388632
  24.5 4.3 %shard_map.65 = (f32[128,2048]{1,0:T(8,128)S(1)}, f32[128,2048]{1,0:T(8,128)S(1)}) custom-call(bf16[2048,512]{1,0:T(8,128)(2,1)S(1)} %bitcast.12, bf16[2048,2048]{1,0:T(8,128)(2,1)S(1)} %copy-done.1), custom_call_target="tpu_custom_call" | custom-call | flops 2147483648 | bytes 8388608 | tf_op jit(solution)/shard_map/pallas_call | solution.py:121
  28.8 4.8 %collective-permute-done = f32[128,2048]{1,0:T(8,128)} collective-permute-done((f32[128,2048]{1,0:T(8,128)}, f32[128,2048]{1,0:T(8,128)}, u32[]{:S(2)}, u32[]{:S(2)}) %collective-permute-start) | collective-permute-done | bytes 1048608 | tf_op jit(solution)/shard_map/ppermute | solution.py:280
  33.6 1.1 %select_add_fusion.1 = f32[64,2048]{1,0:T(8,128)S(1)} fusion(f32[128,2048]{1,0:T(8,128)} %collective-permute-done, f32[128,2048]{1,0:T(8,128)S(1)} %get-tuple-element.29, pred[]{:T(512)S(6)} %or.3), kind=kLoop, calls=%fused_computation.5 | loop fusion | flops 262144 | bytes 1572865 | tf_op jit(solution)/shard_map/add | solution.py:289
  34.7 2.5 %collective-permute-start.6 = (f32[64,2048]{1,0:T(8,128)S(1)}, f32[64,2048]{1,0:T(8,128)S(1)}, u32[]{:S(2)}, u32[]{:S(2)}) collective-permute-start(f32[64,2048]{1,0:T(8,128)S(1)} %select_add_fusion.1), channel_id=1, source_target_pairs={{0,4},{4,12},{12,8},{8,0},{1,5},{5,13},{13,9},{9,1},{2,6},{6,14},{... | collective-permute-start | bytes 1572872 | tf_op jit(solution)/shard_map/ppermute | solution.py:289
  37.3 1.1 %select_add_fusion.2 = (f32[32,2048]{1,0:T(8,128)S(1)}, f32[32,2048]{1,0:T(8,128)S(1)}, f32[32,2048]{1,0:T(8,128)S(1)}) fusion(f32[128,2048]{1,0:T(8,128)} %collective-permute-done, f32[128,2048]{1,0:T(8,128)S(1)} %get-tuple-element.29, pred[]{:T(512)S(6)} %or.3, f32[32,2048]{1,0:T(8,128)S(1)} %copy-done.10), kind=kLoop, calls=%fused_computation.12 | loop fusion | flops 262144 | bytes 2097153 | tf_op jit(solution)/shard_map/add | solution.py:291
  38.4 0.0 copy-start.7
  38.5 0.0 copy-start.8
  38.5 0.0 copy-start.9
  38.5 1.5 %collective-permute-start.1 = (f32[64,2048]{1,0:T(8,128)S(1)}, f32[64,2048]{1,0:T(8,128)S(1)}, u32[]{:S(2)}, u32[]{:S(2)}) collective-permute-start(f32[64,2048]{1,0:T(8,128)S(1)} %pad_maximum_fusion), channel_id=1, source_target_pairs={{0,4},{4,12},{12,8},{8,0},{1,5},{5,13},{13,9},{9,1},{2,6},{6,14},{... | collective-permute-start | bytes 1572872 | tf_op jit(solution)/shard_map/ppermute | solution.py:292
  40.0 1.3 %select_add_fusion = f32[128,2048]{1,0:T(8,128)S(1)} fusion(f32[128,2048]{1,0:T(8,128)S(1)} %get-tuple-element.27, f32[128,2048]{1,0:T(8,128)} %collective-permute-done, pred[]{:T(512)S(6)} %or.3), kind=kLoop, calls=%fused_computation | loop fusion | flops 524288 | bytes 3145729 | tf_op jit(solution)/shard_map/add | solution.py:295
  41.4 2.4 %collective-permute-start.2 = (f32[32,2048]{1,0:T(8,128)S(1)}, f32[32,2048]{1,0:T(8,128)S(1)}, u32[]{:S(2)}, u32[]{:S(2)}) collective-permute-start(f32[32,2048]{1,0:T(8,128)S(1)} %get-tuple-element.41), channel_id=1, source_target_pairs={{0,4},{12,8},{1,5},{13,9},{2,6},{14,10},{3,7},{15,11},{16,20},{28,... | collective-permute-start | bytes 786440 | tf_op jit(solution)/shard_map/ppermute | solution.py:293
  43.8 6.8 %collective-permute-done.5 = f32[96,2048]{1,0:T(8,128)} collective-permute-done((f32[96,2048]{1,0:T(8,128)}, f32[96,2048]{1,0:T(8,128)}, u32[]{:S(2)}, u32[]{:S(2)}) %collective-permute-start.5) | collective-permute-done | bytes 786464 | tf_op jit(solution)/shard_map/ppermute | solution.py:282
  50.5 13.0 %collective-permute-done.6 = f32[64,2048]{1,0:T(8,128)S(1)} collective-permute-done((f32[64,2048]{1,0:T(8,128)S(1)}, f32[64,2048]{1,0:T(8,128)S(1)}, u32[]{:S(2)}, u32[]{:S(2)}) %collective-permute-start.6) | collective-permute-done | bytes 524320 | tf_op jit(solution)/shard_map/ppermute | solution.py:289
  63.5 1.3 %fusion.1.refs_0_ = f32[64,2048]{1,0:T(8,128)S(1)} fusion(f32[64,2048]{1,0:T(8,128)S(1)} %collective-permute-done.6, f32[96,2048]{1,0:T(8,128)} %collective-permute-done.5, f32[96,2048]{1,0:T(8,128)} %collective-permute-done.4, f32[128,2048]{1,0:T(8,128)S(1)} %select_add_fusion), kind=kLoop, calls=%fused_computation.3 | loop fusion | flops 393216 | bytes 2621440 | tf_op jit(solution)/shard_map/add | solution.py:296
  64.8 1.6 %collective-permute-start.7 = (f32[64,2048]{1,0:T(8,128)S(1)}, f32[64,2048]{1,0:T(8,128)S(1)}, u32[]{:S(2)}, u32[]{:S(2)}) collective-permute-start(f32[64,2048]{1,0:T(8,128)S(1)} %fusion.1.refs_0_), channel_id=1, source_target_pairs={{0,2},{2,0},{1,3},{3,1},{4,6},{6,4},{5,7},{7,5},{8,10},{10,8},{9,1... | collective-permute-start | bytes 1572872 | tf_op jit(solution)/shard_map/ppermute | solution.py:300
  66.4 8.3 %collective-permute-done.1 = f32[64,2048]{1,0:T(8,128)S(1)} collective-permute-done((f32[64,2048]{1,0:T(8,128)S(1)}, f32[64,2048]{1,0:T(8,128)S(1)}, u32[]{:S(2)}, u32[]{:S(2)}) %collective-permute-start.1) | collective-permute-done | bytes 524320 | tf_op jit(solution)/shard_map/ppermute | solution.py:292
  74.7 0.9 collective-permute-start.3
  75.5 1.1 %fusion.3.refs_0_ = f32[32,2048]{1,0:T(8,128)S(1)} fusion(f32[96,2048]{1,0:T(8,128)} %collective-permute-done.5, f32[96,2048]{1,0:T(8,128)} %collective-permute-done.4, f32[128,2048]{1,0:T(8,128)S(1)} %select_add_fusion, f32[64,2048]{1,0:T(8,128)S(1)} %collective-permute-done.1), kind=kLoop, calls=%fused_computation.8 | loop fusion | flops 196608 | bytes 1310720 | tf_op jit(solution)/shard_map/add | solution.py:298
  76.6 1.6 %collective-permute-start.9 = (f32[32,2048]{1,0:T(8,128)S(1)}, f32[32,2048]{1,0:T(8,128)S(1)}, u32[]{:S(2)}, u32[]{:S(2)}) collective-permute-start(f32[32,2048]{1,0:T(8,128)S(1)} %fusion.3.refs_0_), channel_id=1, source_target_pairs={{0,2},{2,0},{1,3},{3,1},{4,6},{6,4},{5,7},{7,5},{8,10},{10,8},{9,1... | collective-permute-start | bytes 786440 | tf_op jit(solution)/shard_map/ppermute | solution.py:305
  78.2 0.4 collective-permute-done.7.refs_1_
  78.7 1.5 %shard_map.69.refs_7_ = f32[4,2048]{1,0:T(4,128)S(1)} custom-call(f32[64,2048]{1,0:T(8,128)S(1)} %fusion.1.refs_0_, f32[64,2048]{1,0:T(8,128)S(1)} %collective-permute-done.7.refs_1_, f32[4,2048]{1,0:T(4,128)S(1)} %reshape.129.refs_2_, f32[32,128]{1,0:T(8,128)S(1)} %copy-done.9, bf16[256,256]{1,0:T(8,128)(2,1)S(1)} %copy-done.7, ...), custom_call_target="tpu_custom_call" | custom-call | flops 402653184 | bytes 3145728 | tf_op jit(solution)/shard_map/pallas_call | solution.py:242
  80.1 0.1 fusion.4.refs_0_
  80.2 1.6 %collective-permute-start.8 = (f32[32,2048]{1,0:T(8,128)S(1)}, f32[32,2048]{1,0:T(8,128)S(1)}, u32[]{:S(2)}, u32[]{:S(2)}) collective-permute-start(f32[32,2048]{1,0:T(8,128)S(1)} %fusion.4.refs_0_), channel_id=1, source_target_pairs={{0,2},{2,0},{1,3},{3,1},{4,6},{6,4},{5,7},{7,5},{8,10},{10,8},{9,1... | collective-permute-start | bytes 786440 | tf_op jit(solution)/shard_map/ppermute | solution.py:305
  81.8 4.1 %collective-permute-done.9.refs_1_ = f32[32,2048]{1,0:T(8,128)S(1)} collective-permute-done((f32[32,2048]{1,0:T(8,128)S(1)}, f32[32,2048]{1,0:T(8,128)S(1)}, u32[]{:S(2)}, u32[]{:S(2)}) %collective-permute-start.9) | collective-permute-done | bytes 262176 | tf_op jit(solution)/shard_map/ppermute | solution.py:305
  85.9 1.2 %shard_map.70.refs_7_ = f32[4,2048]{1,0:T(4,128)S(1)} custom-call(f32[32,2048]{1,0:T(8,128)S(1)} %fusion.3.refs_0_, f32[32,2048]{1,0:T(8,128)S(1)} %collective-permute-done.9.refs_1_, f32[4,2048]{1,0:T(4,128)S(1)} %reshape.129.refs_2_, f32[32,128]{1,0:T(8,128)S(1)} %copy-done.9, bf16[256,256]{1,0:T(8,128)(2,1)S(1)} %copy-done.7, ...), custom_call_target="tpu_custom_call" | custom-call | flops 201326592 | bytes 1572864 | tf_op jit(solution)/shard_map/pallas_call | solution.py:242
  87.1 3.5 %collective-permute-done.8.refs_1_ = f32[32,2048]{1,0:T(8,128)S(1)} collective-permute-done((f32[32,2048]{1,0:T(8,128)S(1)}, f32[32,2048]{1,0:T(8,128)S(1)}, u32[]{:S(2)}, u32[]{:S(2)}) %collective-permute-start.8) | collective-permute-done | bytes 262176 | tf_op jit(solution)/shard_map/ppermute | solution.py:305
  90.5 1.2 %shard_map.71 = f32[4,2048]{1,0:T(4,128)S(1)} custom-call(f32[32,2048]{1,0:T(8,128)S(1)} %fusion.4.refs_0_, f32[32,2048]{1,0:T(8,128)S(1)} %collective-permute-done.8.refs_1_, f32[4,2048]{1,0:T(4,128)S(1)} %reshape.129.refs_2_, f32[32,128]{1,0:T(8,128)S(1)} %copy-done.9, bf16[256,256]{1,0:T(8,128)(2,1)S(1)} %copy-done.7, bf16[256,256]{1,0:T(8,128)(2,1)S(1)} %copy-done.8, ...), custom_call_target="tpu_custom_call" | custom-call | flops 201326592 | bytes 1572864 | tf_op jit(solution)/shard_map/pallas_call | solution.py:242
  91.8 0.1 collective-permute-start.10
  91.8 1.2 %collective-permute-done.10 = f32[4,2048]{1,0:T(4,128)S(1)} collective-permute-done((f32[4,2048]{1,0:T(4,128)S(1)}, f32[4,2048]{1,0:T(4,128)S(1)}, u32[]{:S(2)}, u32[]{:S(2)}) %collective-permute-start.10) | collective-permute-done | bytes 32800 | tf_op jit(solution)/shard_map/ppermute | solution.py:270
  93.0 1.8 %collective-permute-start.11 = (f32[4,2048]{1,0:T(4,128)S(1)}, f32[4,2048]{1,0:T(4,128)S(1)}, u32[]{:S(2)}, u32[]{:S(2)}) collective-permute-start(f32[4,2048]{1,0:T(4,128)S(1)} %add.140), channel_id=1, source_target_pairs={{0,4},{4,0},{8,12},{12,8},{1,5},{5,1},{9,13},{13,9},{2,6},{6,2},{1... | collective-permute-start | bytes 98312 | tf_op jit(solution)/shard_map/ppermute | solution.py:264
  94.8 0.6 collective-permute-start.12
  95.4 2.1 %collective-permute-start.13 = (f32[4,2048]{1,0:T(4,128)S(1)}, f32[4,2048]{1,0:T(4,128)S(1)}, u32[]{:S(2)}, u32[]{:S(2)}) collective-permute-start(f32[4,2048]{1,0:T(4,128)S(1)} %add.140), channel_id=1, source_target_pairs={{0,12},{4,8},{8,4},{12,0},{1,13},{5,9},{9,5},{13,1},{2,14},{6,10},... | collective-permute-start | bytes 98312 | tf_op jit(solution)/shard_map/ppermute | solution.py:264
  97.5 2.9 %collective-permute-done.12 = f32[4,2048]{1,0:T(4,128)S(1)} collective-permute-done((f32[4,2048]{1,0:T(4,128)S(1)}, f32[4,2048]{1,0:T(4,128)S(1)}, u32[]{:S(2)}, u32[]{:S(2)}) %collective-permute-start.12) | collective-permute-done | bytes 32800 | tf_op jit(solution)/shard_map/ppermute | solution.py:264
  100.4 0.7 collective-permute-done.13
  101.1 0.1 copy.8
  101.2 0.8 mul.70
  (28 shorter events, 0.2 us)
Async XLA Ops:
  0.0 17.1 %copy-start = (f32[2,2,1,128,2048]{4,3,2,1,0:T(8,128)S(1)}, f32[2,2,1,128,2048]{4,3,2,1,0:T(8,128)}, u32[]{:S(2)}) copy-start(f32[2,2,1,128,2048]{4,3,2,1,0:T(8,128)} %param.8) | copy-start | bytes 12582916
  6.7 27.0 %collective-permute-start = (f32[128,2048]{1,0:T(8,128)}, f32[128,2048]{1,0:T(8,128)}, u32[]{:S(2)}, u32[]{:S(2)}) collective-permute-start(f32[128,2048]{1,0:T(8,128)} %get-tuple-element.22), channel_id=1, source_target_pairs={{0,4},{4,0},{8,12},{12,8},{1,5},{5,1},{9,13},{13,9},{2,6},{6,2},{1... | collective-permute-start | bytes 3145736 | tf_op jit(solution)/shard_map/ppermute | solution.py:280
  9.8 34.0 %collective-permute-start.4 = (f32[96,2048]{1,0:T(8,128)}, f32[96,2048]{1,0:T(8,128)}, u32[]{:S(2)}, u32[]{:S(2)}) collective-permute-start(f32[96,2048]{1,0:T(8,128)} %get-tuple-element.31), channel_id=1, source_target_pairs={{4,8},{8,4},{5,9},{9,5},{6,10},{10,6},{7,11},{11,7},{20,24},{24,20... | collective-permute-start | bytes 2359304 | tf_op jit(solution)/shard_map/ppermute | solution.py:281
  11.3 39.2 %collective-permute-start.5 = (f32[96,2048]{1,0:T(8,128)}, f32[96,2048]{1,0:T(8,128)}, u32[]{:S(2)}, u32[]{:S(2)}) collective-permute-start(f32[96,2048]{1,0:T(8,128)} %get-tuple-element.31), channel_id=1, source_target_pairs={{0,8},{12,4},{1,9},{13,5},{2,10},{14,6},{3,11},{15,7},{16,24},{28,... | collective-permute-start | bytes 2359304 | tf_op jit(solution)/shard_map/ppermute | solution.py:282
  18.4 1.4 %copy-start.3 = (f32[4,64,2048]{2,1,0:T(8,128)}, f32[4,64,2048]{2,1,0:T(8,128)S(1)}, u32[]{:S(2)}) copy-start(f32[4,64,2048]{2,1,0:T(8,128)S(1)} %shard_map.66.refs_6_) | copy-start | bytes 6291460
  18.4 2.7 %copy-start.2 = (bf16[2048,1,512]{2,0,1:T(8,128)(2,1)S(1)}, bf16[2048,1,512]{2,0,1:T(8,128)(2,1)}, u32[]{:S(2)}) copy-start(bf16[2048,1,512]{2,0,1:T(8,128)(2,1)} %param.7) | copy-start | bytes 6291460
  19.1 1.0 copy-start.5
  21.1 3.4 %copy-start.1 = (bf16[2048,2048]{1,0:T(8,128)(2,1)S(1)}, bf16[2048,2048]{1,0:T(8,128)(2,1)}, u32[]{:S(2)}) copy-start(bf16[2048,2048]{1,0:T(8,128)(2,1)} %data_ref.2) | copy-start | bytes 25165828
  24.5 12.8 %copy-start.10 = (f32[32,2048]{1,0:T(8,128)S(1)}, f32[32,2048]{1,0:T(8,128)}, u32[]{:S(2)}) copy-start(f32[32,2048]{1,0:T(8,128)} %get-tuple-element.30) | copy-start | bytes 786436
  34.7 28.8 %collective-permute-start.6 = (f32[64,2048]{1,0:T(8,128)S(1)}, f32[64,2048]{1,0:T(8,128)S(1)}, u32[]{:S(2)}, u32[]{:S(2)}) collective-permute-start(f32[64,2048]{1,0:T(8,128)S(1)} %select_add_fusion.1), channel_id=1, source_target_pairs={{0,4},{4,12},{12,8},{8,0},{1,5},{5,13},{13,9},{9,1},{2,6},{6,14},{... | collective-permute-start | bytes 1572872 | tf_op jit(solution)/shard_map/ppermute | solution.py:289
  38.4 40.2 %copy-start.4 = (f32[4,64,2048]{2,1,0:T(8,128)S(1)}, f32[4,64,2048]{2,1,0:T(8,128)}, u32[]{:S(2)}) copy-start(f32[4,64,2048]{2,1,0:T(8,128)} %copy-done.3) | copy-start | bytes 6291460
  38.4 40.2 %copy-start.7 = (bf16[256,256]{1,0:T(8,128)(2,1)S(1)}, bf16[256,256]{1,0:T(8,128)(2,1)}, u32[]{:S(2)}) copy-start(bf16[256,256]{1,0:T(8,128)(2,1)} %constant.58.clone.refs_4_) | copy-start | bytes 393220
  38.5 40.2 %copy-start.8 = (bf16[256,256]{1,0:T(8,128)(2,1)S(1)}, bf16[256,256]{1,0:T(8,128)(2,1)}, u32[]{:S(2)}) copy-start(bf16[256,256]{1,0:T(8,128)(2,1)} %constant.59.clone.refs_5_) | copy-start | bytes 393220
  38.5 40.2 %copy-start.9 = (f32[32,128]{1,0:T(8,128)S(1)}, f32[32,128]{1,0:T(8,128)}, u32[]{:S(2)}) copy-start(f32[32,128]{1,0:T(8,128)} %constant.57.clone.refs_3_) | copy-start | bytes 49156
  38.5 36.2 %collective-permute-start.1 = (f32[64,2048]{1,0:T(8,128)S(1)}, f32[64,2048]{1,0:T(8,128)S(1)}, u32[]{:S(2)}, u32[]{:S(2)}) collective-permute-start(f32[64,2048]{1,0:T(8,128)S(1)} %pad_maximum_fusion), channel_id=1, source_target_pairs={{0,4},{4,12},{12,8},{8,0},{1,5},{5,13},{13,9},{9,1},{2,6},{6,14},{... | collective-permute-start | bytes 1572872 | tf_op jit(solution)/shard_map/ppermute | solution.py:292
  41.4 44.5 %copy-start.6 = (f32[4,32,2048]{2,1,0:T(8,128)S(1)}, f32[4,32,2048]{2,1,0:T(8,128)}, u32[]{:S(2)}) copy-start(f32[4,32,2048]{2,1,0:T(8,128)} %copy-done.5) | copy-start | bytes 3145732
  41.4 38.8 %collective-permute-start.2 = (f32[32,2048]{1,0:T(8,128)S(1)}, f32[32,2048]{1,0:T(8,128)S(1)}, u32[]{:S(2)}, u32[]{:S(2)}) collective-permute-start(f32[32,2048]{1,0:T(8,128)S(1)} %get-tuple-element.41), channel_id=1, source_target_pairs={{0,4},{12,8},{1,5},{13,9},{2,6},{14,10},{3,7},{15,11},{16,20},{28,... | collective-permute-start | bytes 786440 | tf_op jit(solution)/shard_map/ppermute | solution.py:293
  64.8 13.8 %collective-permute-start.7 = (f32[64,2048]{1,0:T(8,128)S(1)}, f32[64,2048]{1,0:T(8,128)S(1)}, u32[]{:S(2)}, u32[]{:S(2)}) collective-permute-start(f32[64,2048]{1,0:T(8,128)S(1)} %fusion.1.refs_0_), channel_id=1, source_target_pairs={{0,2},{2,0},{1,3},{3,1},{4,6},{6,4},{5,7},{7,5},{8,10},{10,8},{9,1... | collective-permute-start | bytes 1572872 | tf_op jit(solution)/shard_map/ppermute | solution.py:300
  74.7 3.5 %collective-permute-start.3 = (f32[32,2048]{1,0:T(8,128)S(1)}, f32[32,2048]{1,0:T(8,128)S(1)}, u32[]{:S(2)}, u32[]{:S(2)}) collective-permute-start(f32[32,2048]{1,0:T(8,128)S(1)} %slice_add_fusion.3), channel_id=1, source_target_pairs={{4,8},{8,4},{5,9},{9,5},{6,10},{10,6},{7,11},{11,7},{20,24},{24,20... | collective-permute-start | bytes 786440 | tf_op jit(solution)/shard_map/ppermute | solution.py:294
  76.6 9.2 %collective-permute-start.9 = (f32[32,2048]{1,0:T(8,128)S(1)}, f32[32,2048]{1,0:T(8,128)S(1)}, u32[]{:S(2)}, u32[]{:S(2)}) collective-permute-start(f32[32,2048]{1,0:T(8,128)S(1)} %fusion.3.refs_0_), channel_id=1, source_target_pairs={{0,2},{2,0},{1,3},{3,1},{4,6},{6,4},{5,7},{7,5},{8,10},{10,8},{9,1... | collective-permute-start | bytes 786440 | tf_op jit(solution)/shard_map/ppermute | solution.py:305
  80.2 10.3 %collective-permute-start.8 = (f32[32,2048]{1,0:T(8,128)S(1)}, f32[32,2048]{1,0:T(8,128)S(1)}, u32[]{:S(2)}, u32[]{:S(2)}) collective-permute-start(f32[32,2048]{1,0:T(8,128)S(1)} %fusion.4.refs_0_), channel_id=1, source_target_pairs={{0,2},{2,0},{1,3},{3,1},{4,6},{6,4},{5,7},{7,5},{8,10},{10,8},{9,1... | collective-permute-start | bytes 786440 | tf_op jit(solution)/shard_map/ppermute | solution.py:305
  91.8 1.3 %collective-permute-start.10 = (f32[4,2048]{1,0:T(4,128)S(1)}, f32[4,2048]{1,0:T(4,128)S(1)}, u32[]{:S(2)}, u32[]{:S(2)}) collective-permute-start(f32[4,2048]{1,0:T(4,128)S(1)} %shard_map.71), channel_id=1, source_target_pairs={{0,1},{1,0},{2,3},{3,2},{4,5},{5,4},{6,7},{7,6},{8,9},{9,8},{10,11... | collective-permute-start | bytes 98312 | tf_op jit(solution)/shard_map/ppermute | solution.py:270
  93.0 4.5 %collective-permute-start.11 = (f32[4,2048]{1,0:T(4,128)S(1)}, f32[4,2048]{1,0:T(4,128)S(1)}, u32[]{:S(2)}, u32[]{:S(2)}) collective-permute-start(f32[4,2048]{1,0:T(4,128)S(1)} %add.140), channel_id=1, source_target_pairs={{0,4},{4,0},{8,12},{12,8},{1,5},{5,1},{9,13},{13,9},{2,6},{6,2},{1... | collective-permute-start | bytes 98312 | tf_op jit(solution)/shard_map/ppermute | solution.py:264
  94.8 5.5 %collective-permute-start.12 = (f32[4,2048]{1,0:T(4,128)S(1)}, f32[4,2048]{1,0:T(4,128)S(1)}, u32[]{:S(2)}, u32[]{:S(2)}) collective-permute-start(f32[4,2048]{1,0:T(4,128)S(1)} %add.140), channel_id=1, source_target_pairs={{0,8},{4,12},{8,0},{12,4},{1,9},{5,13},{9,1},{13,5},{2,10},{6,14},... | collective-permute-start | bytes 98312 | tf_op jit(solution)/shard_map/ppermute | solution.py:264
  95.4 5.7 %collective-permute-start.13 = (f32[4,2048]{1,0:T(4,128)S(1)}, f32[4,2048]{1,0:T(4,128)S(1)}, u32[]{:S(2)}, u32[]{:S(2)}) collective-permute-start(f32[4,2048]{1,0:T(4,128)S(1)} %add.140), channel_id=1, source_target_pairs={{0,12},{4,8},{8,4},{12,0},{1,13},{5,9},{9,5},{13,1},{2,14},{6,10},... | collective-permute-start | bytes 98312 | tf_op jit(solution)/shard_map/ppermute | solution.py:264
